TPU v7x, 32 devices: a whole 2x2x4 slice. The times are simulated.
32 devices in a mesh: slab: 2 (over x), phase: 16 (over z, y, core).
Axes of the slice: x: 2, y: 2, z: 4, core: 2. Of those that a mesh axis runs over, the one named last changes fastest.
Arguments:
- estimate: float32 [32, 256, 512], P(('slab', 'phase')), parts along dimension 0, may hold values from -6 to 6
- kdata: float32 [32, 32, 256, 512], P('slab', 'phase'), parts along dimension 0, may hold values from -4 to 4
- maps: float32 [64, 256, 512], P(('slab', 'phase')), parts along dimension 0, may hold values from -1 to 1
- mask: int32 [32, 256], P('slab'), parts along dimension 0, may hold values 0 or 1
- w_first: bfloat16 [16, 2, 3, 3, 3], replicated, may hold values from -0.875 to 0.875
- w_middle: bfloat16 [16, 16, 3, 3, 3], replicated, may hold values from -0.3125 to 0.3125
- w_last: bfloat16 [2, 16, 3, 3, 3], replicated, may hold values from -0.3125 to 0.3125
Outputs:
- updated: float32 [32, 256, 512], P(('slab', 'phase')), parts along dimension 0
There are 2 independent parts, one for each index of `slab`. A program takes and returns all parts, laid end to end along the dimension named above; an argument that names none is the same for every part. Nothing has to cross between parts.
All inputs are finite; a program needn't handle non-finite values.
Results may differ from a plain program's by a relative error of at most 0.0019.
Values may be sent and summed in bfloat16 or wider, within the bound.
No kernel may reach another device: no remote copies, remote signals or barrier semaphores. Data moves between devices by JAX's collectives and lax.ppermute only.
A program may use at most 448 MiB of HBM per device.

v0:
```python
import functools
import math

import jax
import jax.numpy as jnp
import numpy as np
from jax import lax
from jax.experimental import pallas as pl
from jax.experimental.pallas import tpu as pltpu
from jax.sharding import PartitionSpec as P

STEP_SIZE = 0.5
WEIGHT_RED = 0.5
BF = jnp.bfloat16
F32 = jnp.float32
LANE_BLOCKS = 4
VMEM_LIMIT = 56 * 1024 * 1024


def trig(rows, cols, length):
    angle = (rows[:, None] * cols[None, :] % length) * (2.0 * math.pi / length)
    scale = 1.0 / math.sqrt(length)
    return np.cos(angle) * scale, np.sin(angle) * scale


def as_bf16(table):
    return jnp.asarray(table.astype(np.float32)).astype(BF)


def left_tables(length):
    half = np.arange(length // 2)
    tables = []
    for parity in (0, 1):
        c, s = trig(half, 2 * half + parity, length)
        tables.append(np.block([[c, -s], [s, c]]))
    return as_bf16(np.stack(tables))


def right_inverse(length):
    full = np.arange(length)
    c, s = trig(full, full, length)
    return as_bf16(np.block([[c, s], [-s, c]]))


def projector_tables(length):
    half = np.arange(length // 2)
    first, second = [], []
    for parity in (0, 1):
        c, s = trig(half, 2 * half + parity, length)
        first.append(np.block([[c, -s], [s, c]]))
        second.append(np.block([[c.T, s.T], [-s.T, c.T]]))
    return as_bf16(np.stack(first)), as_bf16(np.stack(second))


def dot(a, b):
    return jnp.dot(a, b, preferred_element_type=F32)


def data_kernel(ids, *refs):
    kd = refs[:LANE_BLOCKS]
    maps, mask_wide, mask_par, left, right, first, second, out, proj = refs[LANE_BLOCKS:]
    coils, rows, wide = maps.shape
    width, half = wide // 2, rows // 2
    for e in range(2):
        lhs = first[e] * mask_par[0, e : e + 1].astype(BF)
        proj[0, e] = dot(lhs, second[e]).astype(BF)
    keep = mask_wide[0].astype(BF)
    total = None
    for c in range(coils):
        parts = []
        for e in range(2):
            lines = [part[0, c, pl.ds(e, half, stride=2), :].astype(BF) for part in kd]
            real, imag = lines[: LANE_BLOCKS // 2], lines[LANE_BLOCKS // 2 :]
            stacked = jnp.concatenate([jnp.concatenate(real, 1), jnp.concatenate(imag, 1)], 0)
            parts.append(dot(left[e], stacked))
        upper, lower = parts[0] + parts[1], parts[0] - parts[1]
        real = jnp.concatenate([upper[:half], lower[:half]], 0).astype(BF)
        imag = jnp.concatenate([upper[half:], lower[half:]], 0).astype(BF)
        back = dot(jnp.concatenate([real, imag], 1) * keep, right[...])
        br, bi = back[:, :width], back[:, width:]
        sr, si = maps[c, :, :width], maps[c, :, width:]
        term = (sr * br + si * bi, sr * bi - si * br)
        total = term if total is None else (total[0] + term[0], total[1] + term[1])
    out[0, :, :width] = total[0]
    out[0, :, width:] = total[1]


def data_term(ids, kdata, maps, mask_wide, mask_par, tables):
    left, right, first, second = tables
    phases, coils, rows, wide = kdata.shape
    count = ids.shape[0]
    whole = lambda a: pl.BlockSpec(a.shape, lambda i, ids: (0,) * a.ndim)
    lanes = wide // LANE_BLOCKS
    block = lambda q: pl.BlockSpec((1, coils, rows, lanes), lambda i, ids: (ids[i], 0, 0, q))
    return pl.pallas_call(
        data_kernel,
        grid_spec=pltpu.PrefetchScalarGridSpec(
            num_scalar_prefetch=1,
            grid=(count,),
            in_specs=[
                *[block(q) for q in range(LANE_BLOCKS)],
                whole(maps),
                pl.BlockSpec((1, 1, wide), lambda i, ids: (ids[i], 0, 0)),
                pl.BlockSpec((1, 2, wide // 2), lambda i, ids: (ids[i], 0, 0)),
                whole(left),
                whole(right),
                whole(first),
                whole(second),
            ],
            out_specs=[
                pl.BlockSpec((1, rows, wide), lambda i, ids: (i, 0, 0)),
                pl.BlockSpec((1, 2, wide // 2, wide // 2), lambda i, ids: (i, 0, 0, 0)),
            ],
        ),
        out_shape=[
            jax.ShapeDtypeStruct((count, rows, wide), F32),
            jax.ShapeDtypeStruct((count, 2, wide // 2, wide // 2), BF),
        ],
        compiler_params=pltpu.CompilerParams(vmem_limit_bytes=VMEM_LIMIT),
        cost_estimate=pl.CostEstimate(
            flops=count * coils * 12 * rows * (wide // 2) ** 2,
            bytes_accessed=count * coils * rows * wide * 4,
            transcendentals=0,
        ),
        name="data_term",
    )(ids, *[kdata] * LANE_BLOCKS, maps, mask_wide, mask_par, left, right, first, second)


def image_kernel(ids, place, xz, xy, xc, maps, data, proj, noise, away, mine, held):
    step = pl.program_id(0)
    coils, rows, wide = maps.shape
    width, quarter = wide // 2, wide // 4
    strip = noise.shape[1]

    @pl.when(step < 2)
    def _():
        held[...] = xc[jnp.minimum(step, 1)]

    @pl.when(step == 2)
    def _():
        held[...] = xz[0]

    @pl.when(step == 3)
    def _():
        held[...] = xy[0]

    xr = held[:, :width].astype(F32)
    xi = held[:, width:].astype(F32)
    real, imag = -data[0, :, :width], -data[0, :, width:]
    for c in range(coils):
        sr, si = maps[c, :, :width], maps[c, :, width:]
        cr, ci = sr * xr - si * xi, sr * xi + si * xr
        plus = jnp.concatenate(
            [cr[:, :quarter] + cr[:, quarter:], ci[:, :quarter] + ci[:, quarter:]], 1
        )
        minus = jnp.concatenate(
            [cr[:, :quarter] - cr[:, quarter:], ci[:, :quarter] - ci[:, quarter:]], 1
        )
        even = dot(plus.astype(BF), proj[0, 0])
        odd = dot(minus.astype(BF), proj[0, 1])
        low, high = even + odd, even - odd
        br = jnp.concatenate([low[:, :quarter], high[:, :quarter]], 1)
        bi = jnp.concatenate([low[:, quarter:], high[:, quarter:]], 1)
        real = real + sr * br + si * bi
        imag = imag + sr * bi - si * br
    held[:, :width] = real.astype(BF)
    held[:, width:] = imag.astype(BF)
    at = pl.ds(pl.multiple_of(place[0], strip), strip)
    held[at, :] = (held[at, :].astype(F32) + WEIGHT_RED * noise[0]).astype(BF)

    @pl.when(step < 2)
    def _():
        away[0] = held[...]

    @pl.when(step >= 2)
    def _():
        mine[0] = held[...]


def image_term(ids, place, xz, xy, xc, maps, data, proj, noise):
    coils, rows, wide = maps.shape
    strip = noise.shape[1]
    whole = lambda a: pl.BlockSpec(a.shape, lambda i, ids, place: (0,) * a.ndim)
    return pl.pallas_call(
        image_kernel,
        grid_spec=pltpu.PrefetchScalarGridSpec(
            num_scalar_prefetch=2,
            grid=(4,),
            in_specs=[
                whole(xz),
                whole(xy),
                whole(xc),
                whole(maps),
                pl.BlockSpec((1, rows, wide), lambda i, ids, place: (i, 0, 0)),
                pl.BlockSpec((1, 2, wide // 2, wide // 2), lambda i, ids, place: (i, 0, 0, 0)),
                pl.BlockSpec((1, strip, wide), lambda i, ids, place: (ids[i], 0, 0)),
            ],
            out_specs=[
                pl.BlockSpec((1, rows, wide), lambda i, ids, place: (jnp.minimum(i, 1), 0, 0)),
                pl.BlockSpec((1, rows, wide), lambda i, ids, place: (jnp.maximum(i - 2, 0), 0, 0)),
            ],
            scratch_shapes=[pltpu.VMEM((rows, wide), BF)],
        ),
        out_shape=[jax.ShapeDtypeStruct((2, rows, wide), BF)] * 2,
        compiler_params=pltpu.CompilerParams(vmem_limit_bytes=VMEM_LIMIT),
        cost_estimate=pl.CostEstimate(
            flops=4 * coils * 4 * rows * (wide // 2) ** 2,
            bytes_accessed=4 * rows * wide * 8,
            transcendentals=0,
        ),
        name="image_term",
    )(ids, place, xz, xy, xc, maps, data, proj, noise)


def shifted(value, step):
    if step == 1:
        return value
    width = value.shape[1]
    lane = lax.broadcasted_iota(jnp.int32, value.shape, 1)
    if step == 0:
        return jnp.where(lane == 0, 0.0, pltpu.roll(value, 1, 1))
    return jnp.where(lane == width - 1, 0.0, pltpu.roll(value, width - 1, 1))


def conv_kernel(ch, strips, a1, a2, a3, valid1, valid2, out, x1, h1, noise):
    phases, tall, wide = strips.shape
    width = wide // 2
    strip = tall - 8
    n2 = (strip + 2) // 2

    def load(p, carry):
        image = strips[p].astype(F32)
        both = jnp.concatenate([image[:, :width], image[:, width:]], 0)
        for f in range(3):
            x1[p + 1, f * 2 * tall : (f + 1) * 2 * tall] = shifted(both, f).astype(BF)
        return carry

    lax.fori_loop(0, phases, load, 0)
    x1[0] = x1[phases]
    x1[phases + 1] = x1[1]

    def first(p, carry):
        stacked = x1[pl.ds(p, 3)].reshape(18 * tall, width)
        value = jnp.maximum(dot(a1[...], stacked), 0.0) * valid1[...]
        for f in range(3):
            h1[p + 1, f] = shifted(value, f).astype(BF)
        return carry

    lax.fori_loop(0, phases, first, 0)
    h1[0] = h1[phases]
    h1[phases + 1] = h1[1]
    noise[...] = jnp.zeros_like(noise)

    def second(p, carry):
        blocks = []
        for b in range(2):
            lo = b * n2 * ch
            stacked = h1[pl.ds(p, 3), :, lo : lo + (n2 + 2) * ch, :]
            stacked = stacked.reshape(9 * (n2 + 2) * ch, width)
            blocks.append(dot(a2[...], stacked))
        value = jnp.maximum(jnp.concatenate(blocks, 0), 0.0) * valid2[...]
        spread = dot(a3[...], value.astype(BF))
        for d in range(3):
            part = None
            for f in range(3):
                lo = (d * 3 + f) * 2 * strip
                piece = shifted(spread[lo : lo + 2 * strip], f)
                part = piece if part is None else part + piece
            noise[p + 2 - d] += part
        return carry

    lax.fori_loop(0, phases, second, 0)
    noise[phases] += noise[0]
    noise[1] += noise[phases + 1]

    def store(p, carry):
        both = noise[p + 1]
        out[p, :, :width] = both[:strip]
        out[p, :, width:] = both[strip:]
        return carry

    lax.fori_loop(0, phases, store, 0)


def band(weight, outs, ins, offset):
    moved = jnp.transpose(weight, (0, 2, 4, 1, 3))
    zero = ((0, 0),) * 4
    rows = [
        jnp.pad(moved, zero + ((r + offset, ins - 3 - r - offset),)) for r in range(outs)
    ]
    return jnp.stack(rows)


def denoise(strips, w_first, w_middle, w_last, place, image_rows):
    phases, tall, wide = strips.shape
    strip, width, ch = tall - 8, wide // 2, w_first.shape[0]
    n2 = (strip + 2) // 2
    a1 = band(w_first, strip + 4, tall, 1).reshape((strip + 4) * ch, 18 * tall)
    a2 = jnp.swapaxes(band(w_middle, n2, n2 + 2, 0), 4, 5).reshape(n2 * ch, 9 * (n2 + 2) * ch)
    a3 = jnp.transpose(band(w_last, strip, strip + 2, 0), (2, 3, 1, 0, 5, 4))
    a3 = a3.reshape(18 * strip, (strip + 2) * ch)
    row1 = place - 2 + jnp.arange((strip + 4) * ch) // ch
    row2 = place - 1 + jnp.arange((strip + 2) * ch) // ch
    valid1 = ((row1 >= 0) & (row1 < image_rows)).astype(F32)[:, None]
    valid2 = ((row2 >= 0) & (row2 < image_rows)).astype(F32)[:, None]
    return pl.pallas_call(
        functools.partial(conv_kernel, ch),
        out_shape=jax.ShapeDtypeStruct((phases, strip, wide), F32),
        scratch_shapes=[
            pltpu.VMEM((phases + 2, 6 * tall, width), BF),
            pltpu.VMEM((phases + 2, 3, (strip + 4) * ch, width), BF),
            pltpu.VMEM((phases + 2, 2 * strip, width), F32),
        ],
        compiler_params=pltpu.CompilerParams(vmem_limit_bytes=VMEM_LIMIT),
        cost_estimate=pl.CostEstimate(
            flops=phases * 2 * width * (a1.size + 2 * a2.size + a3.size),
            bytes_accessed=phases * tall * wide * 6,
            transcendentals=0,
        ),
        name="denoise",
    )(strips, a1, a2, a3, valid1, valid2)


def shards(estimate, kdata, maps, mask, w_first, w_middle, w_last):
    count = lax.axis_size("phase")
    me = lax.axis_index("phase")
    planes = count // 4
    rows, wide = estimate.shape[1:]
    strip = rows // count
    image = estimate.astype(BF)
    tables = (left_tables(rows), right_inverse(wide // 2)) + projector_tables(wide // 2)
    mask_float = mask.astype(F32)
    mask_wide = jnp.concatenate([mask_float, mask_float], -1)[:, None]
    pairs = jnp.stack([mask_float[:, 0::2], mask_float[:, 1::2]], 1)
    mask_par = jnp.concatenate([pairs, pairs], -1)
    place = (me * strip).astype(jnp.int32)

    def send(value, shift=0, flip=0):
        pairs = [(i, ((i ^ flip) + 4 * shift) % count) for i in range(count)]
        return lax.ppermute(value, "phase", pairs)

    padded = jnp.pad(image[0], ((4, 4), (0, 0)))
    strips = jnp.stack([padded[strip * j : strip * j + strip + 8] for j in range(count)])
    strips = lax.all_to_all(strips, "phase", 0, 0, tiled=True)

    order = [k for k in (2, 1, planes - 1) if 0 < k < planes]
    order = list(dict.fromkeys(order + list(range(1, planes)) + [0]))
    images = {}
    for k in order:
        xz = image if k == 0 else send(image, shift=planes - k)
        xy = send(xz, flip=2)
        xc = send(jnp.concatenate([xz, xy]), flip=1)
        images[k] = (xz, xy, xc)

    noise = denoise(strips, w_first, w_middle, w_last, place, rows)
    flips = jnp.array([1, 3, 0, 2], jnp.int32)
    terms = {}
    for k in order:
        ids = ((me ^ flips) + 4 * k) % count
        terms[k] = (ids,) + tuple(data_term(ids, kdata, maps, mask_wide, mask_par, tables))

    total = None
    for k in order:
        ids, data, proj = terms[k]
        away, mine = image_term(ids, place[None], *images[k], maps, data, proj, noise)
        got = send(away, flip=1)
        pair = mine.astype(F32) + got.astype(F32)
        other = send(pair[1].astype(BF), flip=2)
        plane = pair[0] + other.astype(F32)
        if k:
            plane = send(plane.astype(BF), shift=k).astype(F32)
        total = plane if total is None else total + plane
    return estimate - STEP_SIZE * total[None]


def solution(mesh):
    return jax.shard_map(
        shards,
        mesh=mesh,
        in_specs=(
            P(("slab", "phase"), None, None),
            P("slab", "phase", None, None),
            P(("slab", "phase"), None, None),
            P("slab", None),
            P(),
            P(),
            P(),
        ),
        out_specs=P(("slab", "phase"), None, None),
        check_vma=False,
    )
```

profile of v0, /device:TPU:0, one launch (start us, length us, event | category | flops | bytes accessed | tf_op | source)
XLA Modules:
  0.0 195.7 jit_solution(9523119131294871738)
XLA Ops:
  0.0 1.1 convert_element_type.200.xz
  1.1 4.1 %collective-permute-start = (bf16[1,256,512]{2,1,0:T(8,128)(2,1)S(1)}, bf16[1,256,512]{2,1,0:T(8,128)(2,1)}, u32[]{:S(2)}, u32[]{:S(2)}) collective-permute-start(bf16[1,256,512]{2,1,0:T(8,128)(2,1)S(1)} %convert_element_type.200.xz), channel_id=1, source_target_pairs={{0,8},{1,9},{2,10},{3,11},{4,12},{5,13},{6,14},{7,15},{8,0},{9,1},... | collective-permute-start | bytes 786440 | tf_op jit(solution)/shard_map/ppermute | solution.py:340
  5.2 1.3 collective-permute-start.6
  6.6 0.7 collective-permute-start.12
  7.2 1.5 collective-permute-start.18
  8.8 1.1 convert_bitcast_fusion
  10.4 0.6 constant_dynamic-update-slice_fusion.14
  11.1 0.6 constant_dynamic-update-slice_fusion.13
  15.4 0.6 constant_dynamic-update-slice_fusion.6
  17.8 0.6 constant_dynamic-update-slice_fusion.2
  19.7 4.7 %all-to-all-start = ((bf16[16,24,512]{2,1,0:T(8,128)(2,1)}), bf16[16,24,512]{2,1,0:T(8,128)(2,1)}, u32[]{:S(2)}, u32[]{:S(2)}) async-start(bf16[16,24,512]{2,1,0:T(8,128)(2,1)} %constant_dynamic-update-slice_fusion), calls=%async_computation | async-start | bytes 786432 | tf_op jit(solution)/shard_map/all_to_all | solution.py:344
  26.6 1.4 copy-done.5
  28.7 0.8 bitcast_dynamic-update-slice_fusion.8
  29.5 0.8 bitcast_dynamic-update-slice_fusion.7
  30.3 0.8 bitcast_dynamic-update-slice_fusion.6
  31.1 0.8 bitcast_dynamic-update-slice_fusion.5
  31.9 0.8 bitcast_dynamic-update-slice_fusion.4
  32.8 0.9 bitcast_dynamic-update-slice_fusion.3
  33.6 0.8 bitcast_dynamic-update-slice_fusion.2
  34.4 0.8 bitcast_dynamic-update-slice_fusion.1
  35.3 0.8 bitcast_dynamic-update-slice_fusion
  36.1 0.7 fusion.21.valid1
  36.8 0.7 fusion.29.valid2
  37.5 0.6 copy.31.refs_5_
  38.7 0.6 maximum_maximum_fusion.refs_6_
  39.4 7.7 %data_term.7 = (f32[4,256,512]{2,1,0:T(8,128)}, bf16[4,2,256,256]{3,2,1,0:T(8,128)(2,1)}) custom-call(s32[4]{0:T(128)} %get-tuple-element.39.ids, f32[16,2,256,512]{3,2,1,0:T(8,128)} %refs_3_.7, f32[16,2,256,512]{3,2,1,0:T(8,128)} %refs_3_.7, f32[16,2,256,512]{3,2,1,0:T(8,128)} %refs_3_.7, f32[16,2,256,512]{3,2,1,0:T(8,128)} %refs_3_.7, ...), custom_call_target="tpu_custom_call" | custom-call | flops 1610612736 | bytes 4194304 | tf_op jit(solution)/shard_map/data_term/pallas_call | solution.py:95
  47.2 2.0 collective-permute-start.1
  49.5 6.0 %copy.32 = bf16[20,16,3,3,2,24]{5,4,3,2,1,0:T(2,128)(2,1)S(1)} copy(bf16[20,16,3,3,2,24]{1,4,3,5,2,0:T(2,128)(2,1)} %copy-done.5) | data formatting | bytes 552960 | tf_op jit(solution)/shard_map/stack | solution.py:291
  55.6 1.6 reshape.140.a1
  57.1 1.5 copy.34
  58.7 0.7 reshape.142
  59.4 0.8 copy.37.a3
  60.2 5.6 %copy.33 = bf16[9,16,3,3,11,16]{5,4,3,2,1,0:T(8,128)(2,1)} copy(bf16[9,16,3,3,11,16]{5,1,3,4,2,0:T(8,128)(2,1)} %bitcast.39) | data formatting | bytes 912384 | tf_op jit(solution)/shard_map/transpose | solution.py:299
  65.8 6.2 %reshape.141.a2 = bf16[144,1584]{1,0:T(8,128)(2,1)} reshape(bf16[9,16,3,3,11,16]{5,4,3,2,1,0:T(8,128)(2,1)} %copy.33) | data formatting | bytes 912384 | tf_op jit(solution)/shard_map/reshape | solution.py:299
  72.0 1.9 collective-permute-start.13
  73.9 1.8 pad_maximum_fusion.3
  75.7 1.9 pad_maximum_fusion
  78.1 1.9 pad_maximum_fusion.1
  80.0 0.9 pad_maximum_fusion.2
  81.4 21.0 %denoise.1.noise = f32[16,16,512]{2,1,0:T(8,128)} custom-call(bf16[16,24,512]{2,1,0:T(8,128)(2,1)} %all-to-all-done.strips, bf16[320,432]{1,0:T(8,128)(2,1)} %reshape.140.a1, bf16[144,1584]{1,0:T(8,128)(2,1)} %reshape.141.a2, bf16[288,288]{1,0:T(8,128)(2,1)} %copy.37.a3, f32[320,1]{1,0:T(8,128)} %fusion.21.valid1, f32[288,1]{1,0:T(8,128)} %fusion.29.valid2), custom_call_target="tpu_custom_call" | custom-call | flops 5549064192 | bytes 1179648 | tf_op jit(solution)/shard_map/denoise/pallas_call | solution.py:306
  102.4 0.8 copy-done.11
  103.2 6.2 %image_term.7 = (bf16[2,256,512]{2,1,0:T(8,128)(2,1)}, bf16[2,256,512]{2,1,0:T(8,128)(2,1)}) custom-call(s32[4]{0:T(128)} %get-tuple-element.39.ids, s32[1]{0:T(128)} %bitcast.place, bf16[1,256,512]{2,1,0:T(8,128)(2,1)} %copy-done.2, bf16[1,256,512]{2,1,0:T(8,128)(2,1)} %collective-permute-done.18.xy, bf16[2,256,512]{2,1,0:T(8,128)(2,1)} %copy-done.11, ...), custom_call_target="tpu_custom_call" | custom-call | flops 536870912 | bytes 4194304 | tf_op jit(solution)/shard_map/image_term/pallas_call | solution.py:184
  109.4 7.7 %data_term.4 = (f32[4,256,512]{2,1,0:T(8,128)}, bf16[4,2,256,256]{3,2,1,0:T(8,128)(2,1)}) custom-call(s32[4]{0:T(128)} %get-tuple-element.37.ids, f32[16,2,256,512]{3,2,1,0:T(8,128)} %refs_3_.7, f32[16,2,256,512]{3,2,1,0:T(8,128)} %refs_3_.7, f32[16,2,256,512]{3,2,1,0:T(8,128)} %refs_3_.7, f32[16,2,256,512]{3,2,1,0:T(8,128)} %refs_3_.7, ...), custom_call_target="tpu_custom_call" | custom-call | flops 1610612736 | bytes 4194304 | tf_op jit(solution)/shard_map/data_term/pallas_call | solution.py:95
  117.1 7.9 %data_term.5 = (f32[4,256,512]{2,1,0:T(8,128)}, bf16[4,2,256,256]{3,2,1,0:T(8,128)(2,1)}) custom-call(s32[4]{0:T(128)} %get-tuple-element.40.ids, f32[16,2,256,512]{3,2,1,0:T(8,128)} %refs_3_.7, f32[16,2,256,512]{3,2,1,0:T(8,128)} %refs_3_.7, f32[16,2,256,512]{3,2,1,0:T(8,128)} %refs_3_.7, f32[16,2,256,512]{3,2,1,0:T(8,128)} %refs_3_.7, ...), custom_call_target="tpu_custom_call" | custom-call | flops 1610612736 | bytes 4194304 | tf_op jit(solution)/shard_map/data_term/pallas_call | solution.py:95
  125.0 7.7 %data_term.6 = (f32[4,256,512]{2,1,0:T(8,128)}, bf16[4,2,256,256]{3,2,1,0:T(8,128)(2,1)}) custom-call(s32[4]{0:T(128)} %get-tuple-element.38.ids, f32[16,2,256,512]{3,2,1,0:T(8,128)} %refs_3_.7, f32[16,2,256,512]{3,2,1,0:T(8,128)} %refs_3_.7, f32[16,2,256,512]{3,2,1,0:T(8,128)} %refs_3_.7, f32[16,2,256,512]{3,2,1,0:T(8,128)} %refs_3_.7, ...), custom_call_target="tpu_custom_call" | custom-call | flops 1610612736 | bytes 4194304 | tf_op jit(solution)/shard_map/data_term/pallas_call | solution.py:95
  132.7 0.8 copy-done.10
  133.5 6.3 %image_term.4 = (bf16[2,256,512]{2,1,0:T(8,128)(2,1)}, bf16[2,256,512]{2,1,0:T(8,128)(2,1)}) custom-call(s32[4]{0:T(128)} %get-tuple-element.37.ids, s32[1]{0:T(128)} %bitcast.place, bf16[1,256,512]{2,1,0:T(8,128)(2,1)} %collective-permute-done.xz, bf16[1,256,512]{2,1,0:T(8,128)(2,1)} %collective-permute-done.1.xy, bf16[2,256,512]{2,1,0:T(8,128)(2,1)} %copy-done.10, ...), custom_call_target="tpu_custom_call" | custom-call | flops 536870912 | bytes 4194304 | tf_op jit(solution)/shard_map/image_term/pallas_call | solution.py:184
  140.3 0.8 copy-done.9
  141.1 6.3 %image_term.5 = (bf16[2,256,512]{2,1,0:T(8,128)(2,1)}, bf16[2,256,512]{2,1,0:T(8,128)(2,1)}) custom-call(s32[4]{0:T(128)} %get-tuple-element.40.ids, s32[1]{0:T(128)} %bitcast.place, bf16[1,256,512]{2,1,0:T(8,128)(2,1)} %collective-permute-done.6.xz, bf16[1,256,512]{2,1,0:T(8,128)(2,1)} %collective-permute-done.7.xy, bf16[2,256,512]{2,1,0:T(8,128)(2,1)} %copy-done.9, ...), custom_call_target="tpu_custom_call" | custom-call | flops 536870912 | bytes 4194304 | tf_op jit(solution)/shard_map/image_term/pallas_call | solution.py:184
  147.4 0.8 copy-done.8
  148.2 6.4 %image_term.6 = (bf16[2,256,512]{2,1,0:T(8,128)(2,1)}, bf16[2,256,512]{2,1,0:T(8,128)(2,1)}) custom-call(s32[4]{0:T(128)} %get-tuple-element.38.ids, s32[1]{0:T(128)} %bitcast.place, bf16[1,256,512]{2,1,0:T(8,128)(2,1)} %copy-done.6, bf16[1,256,512]{2,1,0:T(8,128)(2,1)} %copy-done.7, bf16[2,256,512]{2,1,0:T(8,128)(2,1)} %copy-done.8, f32[2,256,512]{2,1,0:T(8,128)} %maps.7, ...), custom_call_target="tpu_custom_call" | custom-call | flops 536870912 | bytes 4194304 | tf_op jit(solution)/shard_map/image_term/pallas_call | solution.py:184
  155.3 1.3 collective-permute-start.21
  156.8 0.9 collective-permute-start.4
  157.9 1.3 collective-permute-start.10
  159.4 0.9 collective-permute-start.16
  160.3 9.9 %collective-permute-done.4 = bf16[256,512]{1,0:T(8,128)(2,1)S(1)} collective-permute-done((bf16[256,512]{1,0:T(8,128)(2,1)S(1)}, bf16[256,512]{1,0:T(8,128)(2,1)S(1)}, u32[]{:S(2)}, u32[]{:S(2)}) %collective-permute-start.4) | collective-permute-done | bytes 262176 | tf_op jit(solution)/shard_map/ppermute | solution.py:340
  170.3 2.4 %collective-permute-start.5 = (bf16[256,512]{1,0:T(8,128)(2,1)S(1)}, bf16[256,512]{1,0:T(8,128)(2,1)S(1)}, u32[]{:S(2)}, u32[]{:S(2)}) collective-permute-start(bf16[256,512]{1,0:T(8,128)(2,1)S(1)} %fusion.10), channel_id=1, source_target_pairs={{0,8},{1,9},{2,10},{3,11},{4,12},{5,13},{6,14},{7,15},{8,0},{9,1},... | collective-permute-start | bytes 786440 | tf_op jit(solution)/shard_map/ppermute | solution.py:340
  172.6 3.2 %collective-permute-done.10 = bf16[256,512]{1,0:T(8,128)(2,1)S(1)} collective-permute-done((bf16[256,512]{1,0:T(8,128)(2,1)S(1)}, bf16[256,512]{1,0:T(8,128)(2,1)S(1)}, u32[]{:S(2)}, u32[]{:S(2)}) %collective-permute-start.10) | collective-permute-done | bytes 262176 | tf_op jit(solution)/shard_map/ppermute | solution.py:340
  175.9 1.5 collective-permute-start.11
  177.3 3.2 %collective-permute-done.16 = bf16[256,512]{1,0:T(8,128)(2,1)S(1)} collective-permute-done((bf16[256,512]{1,0:T(8,128)(2,1)S(1)}, bf16[256,512]{1,0:T(8,128)(2,1)S(1)}, u32[]{:S(2)}, u32[]{:S(2)}) %collective-permute-start.16) | collective-permute-done | bytes 262176 | tf_op jit(solution)/shard_map/ppermute | solution.py:340
  180.6 3.5 %collective-permute-start.17 = (bf16[256,512]{1,0:T(8,128)(2,1)S(1)}, bf16[256,512]{1,0:T(8,128)(2,1)S(1)}, u32[]{:S(2)}, u32[]{:S(2)}) collective-permute-start(bf16[256,512]{1,0:T(8,128)(2,1)S(1)} %fusion.6), channel_id=1, source_target_pairs={{0,12},{1,13},{2,14},{3,15},{4,0},{5,1},{6,2},{7,3},{8,4},{9,5},{1... | collective-permute-start | bytes 786440 | tf_op jit(solution)/shard_map/ppermute | solution.py:340
  184.1 6.4 %collective-permute-done.5 = bf16[256,512]{1,0:T(8,128)(2,1)S(1)} collective-permute-done((bf16[256,512]{1,0:T(8,128)(2,1)S(1)}, bf16[256,512]{1,0:T(8,128)(2,1)S(1)}, u32[]{:S(2)}, u32[]{:S(2)}) %collective-permute-start.5) | collective-permute-done | bytes 262176 | tf_op jit(solution)/shard_map/ppermute | solution.py:340
  190.5 4.3 %collective-permute-done.17 = bf16[256,512]{1,0:T(8,128)(2,1)S(1)} collective-permute-done((bf16[256,512]{1,0:T(8,128)(2,1)S(1)}, bf16[256,512]{1,0:T(8,128)(2,1)S(1)}, u32[]{:S(2)}, u32[]{:S(2)}) %collective-permute-start.17) | collective-permute-done | bytes 262176 | tf_op jit(solution)/shard_map/ppermute | solution.py:340
  194.7 1.0 fusion.4
  (122 shorter events, 14.4 us)
Async XLA Ops:
  0.0 24.4 %copy-start.16 = (s32[16,256]{1,0:T(8,128)S(1)}, s32[16,256]{1,0:T(8,128)}, u32[]{:S(2)}) copy-start(s32[16,256]{1,0:T(8,128)} %param.15) | copy-start | bytes 49156
  0.0 25.1 %copy-start.1 = (bf16[16,2,3,3,3]{0,1,4,3,2:T(2,128)(2,1)S(1)}, bf16[16,2,3,3,3]{0,1,4,3,2:T(2,128)(2,1)}, u32[]{:S(2)}) copy-start(bf16[16,2,3,3,3]{0,1,4,3,2:T(2,128)(2,1)} %param.16) | copy-start | bytes 5188
  1.1 72.8 %copy-start.2 = (bf16[1,256,512]{2,1,0:T(8,128)(2,1)}, bf16[1,256,512]{2,1,0:T(8,128)(2,1)S(1)}, u32[]{:S(2)}) copy-start(bf16[1,256,512]{2,1,0:T(8,128)(2,1)S(1)} %convert_element_type.200.xz) | copy-start | bytes 786436
  1.1 46.1 %collective-permute-start = (bf16[1,256,512]{2,1,0:T(8,128)(2,1)S(1)}, bf16[1,256,512]{2,1,0:T(8,128)(2,1)}, u32[]{:S(2)}, u32[]{:S(2)}) collective-permute-start(bf16[1,256,512]{2,1,0:T(8,128)(2,1)S(1)} %convert_element_type.200.xz), channel_id=1, source_target_pairs={{0,8},{1,9},{2,10},{3,11},{4,12},{5,13},{6,14},{7,15},{8,0},{9,1},... | collective-permute-start | bytes 786440 | tf_op jit(solution)/shard_map/ppermute | solution.py:340
  5.2 44.0 %collective-permute-start.6 = (bf16[1,256,512]{2,1,0:T(8,128)(2,1)S(1)}, bf16[1,256,512]{2,1,0:T(8,128)(2,1)}, u32[]{:S(2)}, u32[]{:S(2)}) collective-permute-start(bf16[1,256,512]{2,1,0:T(8,128)(2,1)S(1)} %convert_element_type.200.xz), channel_id=1, source_target_pairs={{0,12},{1,13},{2,14},{3,15},{4,0},{5,1},{6,2},{7,3},{8,4},{9,5},{1... | collective-permute-start | bytes 786440 | tf_op jit(solution)/shard_map/ppermute | solution.py:340
  6.6 65.4 %collective-permute-start.12 = (bf16[1,256,512]{2,1,0:T(8,128)(2,1)S(1)}, bf16[1,256,512]{2,1,0:T(8,128)(2,1)S(1)}, u32[]{:S(2)}, u32[]{:S(2)}) collective-permute-start(bf16[1,256,512]{2,1,0:T(8,128)(2,1)S(1)} %convert_element_type.200.xz), channel_id=1, source_target_pairs={{0,4},{1,5},{2,6},{3,7},{4,8},{5,9},{6,10},{7,11},{8,12},{9,13},{1... | collective-permute-start | bytes 786440 | tf_op jit(solution)/shard_map/ppermute | solution.py:340
  7.2 66.6 %collective-permute-start.18 = (bf16[1,256,512]{2,1,0:T(8,128)(2,1)S(1)}, bf16[1,256,512]{2,1,0:T(8,128)(2,1)}, u32[]{:S(2)}, u32[]{:S(2)}) collective-permute-start(bf16[1,256,512]{2,1,0:T(8,128)(2,1)S(1)} %convert_element_type.200.xz), channel_id=1, source_target_pairs={{0,2},{1,3},{2,0},{3,1},{4,6},{5,7},{6,4},{7,5},{8,10},{9,11},{10,... | collective-permute-start | bytes 786440 | tf_op jit(solution)/shard_map/ppermute | solution.py:340
  10.4 17.6 %copy-start.4 = (bf16[2,16,3,3,3]{1,0,4,3,2:T(2,128)(2,1)S(1)}, bf16[2,16,3,3,3]{1,0,4,3,2:T(2,128)(2,1)}, u32[]{:S(2)}) copy-start(bf16[2,16,3,3,3]{1,0,4,3,2:T(2,128)(2,1)} %param.18) | copy-start | bytes 5188
  19.6 9.0 %copy-start = (bf16[16,16,3,3,3]{1,0,4,3,2:T(8,128)(2,1)S(1)}, bf16[16,16,3,3,3]{1,0,4,3,2:T(8,128)(2,1)}, u32[]{:S(2)}) copy-start(bf16[16,16,3,3,3]{1,0,4,3,2:T(8,128)(2,1)} %param.17) | copy-start | bytes 41476
  19.7 61.7 %all-to-all-start = ((bf16[16,24,512]{2,1,0:T(8,128)(2,1)}), bf16[16,24,512]{2,1,0:T(8,128)(2,1)}, u32[]{:S(2)}, u32[]{:S(2)}) async-start(bf16[16,24,512]{2,1,0:T(8,128)(2,1)} %constant_dynamic-update-slice_fusion), calls=%async_computation | async-start | bytes 786432 | tf_op jit(solution)/shard_map/all_to_all | solution.py:344
  26.6 1.4 copy-start.5
  29.5 8.6 %copy-start.17 = (s32[4]{0:T(128)S(1)}, s32[4]{0:T(128)}, u32[]{:S(2)}) copy-start(s32[4]{0:T(128)} %constant.91.clone) | copy-start | bytes 52
  47.2 28.4 %collective-permute-start.1 = (bf16[1,256,512]{2,1,0:T(8,128)(2,1)}, bf16[1,256,512]{2,1,0:T(8,128)(2,1)}, u32[]{:S(2)}, u32[]{:S(2)}) collective-permute-start(bf16[1,256,512]{2,1,0:T(8,128)(2,1)} %collective-permute-done.xz), channel_id=1, source_target_pairs={{0,2},{1,3},{2,0},{3,1},{4,6},{5,7},{6,4},{7,5},{8,10},{9,11},{10,... | collective-permute-start | bytes 786440 | tf_op jit(solution)/shard_map/ppermute | solution.py:340
  49.3 28.8 %collective-permute-start.7 = (bf16[1,256,512]{2,1,0:T(8,128)(2,1)}, bf16[1,256,512]{2,1,0:T(8,128)(2,1)}, u32[]{:S(2)}, u32[]{:S(2)}) collective-permute-start(bf16[1,256,512]{2,1,0:T(8,128)(2,1)} %collective-permute-done.6.xz), channel_id=1, source_target_pairs={{0,2},{1,3},{2,0},{3,1},{4,6},{5,7},{6,4},{7,5},{8,10},{9,11},{10,... | collective-permute-start | bytes 786440 | tf_op jit(solution)/shard_map/ppermute | solution.py:340
  72.0 30.4 %copy-start.6 = (bf16[1,256,512]{2,1,0:T(8,128)(2,1)}, bf16[1,256,512]{2,1,0:T(8,128)(2,1)S(1)}, u32[]{:S(2)}) copy-start(bf16[1,256,512]{2,1,0:T(8,128)(2,1)S(1)} %collective-permute-done.12.xz) | copy-start | bytes 786436
  72.0 8.0 %collective-permute-start.13 = (bf16[1,256,512]{2,1,0:T(8,128)(2,1)S(1)}, bf16[1,256,512]{2,1,0:T(8,128)(2,1)S(1)}, u32[]{:S(2)}, u32[]{:S(2)}) collective-permute-start(bf16[1,256,512]{2,1,0:T(8,128)(2,1)S(1)} %collective-permute-done.12.xz), channel_id=1, source_target_pairs={{0,2},{1,3},{2,0},{3,1},{4,6},{5,7},{6,4},{7,5},{8,10},{9,11},{10,... | collective-permute-start | bytes 786440 | tf_op jit(solution)/shard_map/ppermute | solution.py:340
  75.7 26.7 %collective-permute-start.19 = (bf16[2,256,512]{2,1,0:T(8,128)(2,1)}, bf16[2,256,512]{2,1,0:T(8,128)(2,1)S(1)}, u32[]{:S(2)}, u32[]{:S(2)}) collective-permute-start(bf16[2,256,512]{2,1,0:T(8,128)(2,1)} %pad_maximum_fusion.3), channel_id=1, source_target_pairs={{0,1},{1,0},{2,3},{3,2},{4,5},{5,4},{6,7},{7,6},{8,9},{9,8},{10,11... | collective-permute-start | bytes 1572872 | tf_op jit(solution)/shard_map/ppermute | solution.py:340
  77.6 55.2 %collective-permute-start.2 = (bf16[2,256,512]{2,1,0:T(8,128)(2,1)}, bf16[2,256,512]{2,1,0:T(8,128)(2,1)S(1)}, u32[]{:S(2)}, u32[]{:S(2)}) collective-permute-start(bf16[2,256,512]{2,1,0:T(8,128)(2,1)} %pad_maximum_fusion), channel_id=1, source_target_pairs={{0,1},{1,0},{2,3},{3,2},{4,5},{5,4},{6,7},{7,6},{8,9},{9,8},{10,11... | collective-permute-start | bytes 1572872 | tf_op jit(solution)/shard_map/ppermute | solution.py:340
  79.9 60.3 %collective-permute-start.8 = (bf16[2,256,512]{2,1,0:T(8,128)(2,1)}, bf16[2,256,512]{2,1,0:T(8,128)(2,1)S(1)}, u32[]{:S(2)}, u32[]{:S(2)}) collective-permute-start(bf16[2,256,512]{2,1,0:T(8,128)(2,1)} %pad_maximum_fusion.1), channel_id=1, source_target_pairs={{0,1},{1,0},{2,3},{3,2},{4,5},{5,4},{6,7},{7,6},{8,9},{9,8},{10,11... | collective-permute-start | bytes 1572872 | tf_op jit(solution)/shard_map/ppermute | solution.py:340
  80.0 22.4 %copy-start.7 = (bf16[1,256,512]{2,1,0:T(8,128)(2,1)}, bf16[1,256,512]{2,1,0:T(8,128)(2,1)S(1)}, u32[]{:S(2)}) copy-start(bf16[1,256,512]{2,1,0:T(8,128)(2,1)S(1)} %collective-permute-done.13.xy) | copy-start | bytes 786436
  80.9 66.5 %collective-permute-start.14 = (bf16[2,256,512]{2,1,0:T(8,128)(2,1)}, bf16[2,256,512]{2,1,0:T(8,128)(2,1)S(1)}, u32[]{:S(2)}, u32[]{:S(2)}) collective-permute-start(bf16[2,256,512]{2,1,0:T(8,128)(2,1)} %pad_maximum_fusion.2), channel_id=1, source_target_pairs={{0,1},{1,0},{2,3},{3,2},{4,5},{5,4},{6,7},{7,6},{8,9},{9,8},{10,11... | collective-permute-start | bytes 1572872 | tf_op jit(solution)/shard_map/ppermute | solution.py:340
  102.4 0.8 copy-start.11
  109.4 45.7 %collective-permute-start.20 = (bf16[2,256,512]{2,1,0:T(8,128)(2,1)}, bf16[2,256,512]{2,1,0:T(8,128)(2,1)S(1)}, u32[]{:S(2)}, u32[]{:S(2)}) collective-permute-start(bf16[2,256,512]{2,1,0:T(8,128)(2,1)} %get-tuple-element.36), channel_id=1, source_target_pairs={{0,1},{1,0},{2,3},{3,2},{4,5},{5,4},{6,7},{7,6},{8,9},{9,8},{10,11... | collective-permute-start | bytes 1572872 | tf_op jit(solution)/shard_map/ppermute | solution.py:340
  132.7 0.8 copy-start.10
  139.8 16.8 %collective-permute-start.3 = (bf16[2,256,512]{2,1,0:T(8,128)(2,1)}, bf16[2,256,512]{2,1,0:T(8,128)(2,1)S(1)}, u32[]{:S(2)}, u32[]{:S(2)}) collective-permute-start(bf16[2,256,512]{2,1,0:T(8,128)(2,1)} %get-tuple-element.24), channel_id=1, source_target_pairs={{0,1},{1,0},{2,3},{3,2},{4,5},{5,4},{6,7},{7,6},{8,9},{9,8},{10,11... | collective-permute-start | bytes 1572872 | tf_op jit(solution)/shard_map/ppermute | solution.py:340
  140.3 0.8 copy-start.9
  147.3 10.4 %collective-permute-start.9 = (bf16[2,256,512]{2,1,0:T(8,128)(2,1)}, bf16[2,256,512]{2,1,0:T(8,128)(2,1)S(1)}, u32[]{:S(2)}, u32[]{:S(2)}) collective-permute-start(bf16[2,256,512]{2,1,0:T(8,128)(2,1)} %get-tuple-element.28), channel_id=1, source_target_pairs={{0,1},{1,0},{2,3},{3,2},{4,5},{5,4},{6,7},{7,6},{8,9},{9,8},{10,11... | collective-permute-start | bytes 1572872 | tf_op jit(solution)/shard_map/ppermute | solution.py:340
  147.4 0.8 copy-start.8
  148.2 6.9 %copy-start.12 = (bf16[2,256,512]{2,1,0:T(8,128)(2,1)S(1)}, bf16[2,256,512]{2,1,0:T(8,128)(2,1)}, u32[]{:S(2)}) copy-start(bf16[2,256,512]{2,1,0:T(8,128)(2,1)} %get-tuple-element.35) | copy-start | bytes 1572868
  154.6 2.0 %copy-start.13 = (bf16[2,256,512]{2,1,0:T(8,128)(2,1)S(1)}, bf16[2,256,512]{2,1,0:T(8,128)(2,1)}, u32[]{:S(2)}) copy-start(bf16[2,256,512]{2,1,0:T(8,128)(2,1)} %get-tuple-element.23) | copy-start | bytes 1572868
  154.6 4.6 %collective-permute-start.15 = (bf16[2,256,512]{2,1,0:T(8,128)(2,1)}, bf16[2,256,512]{2,1,0:T(8,128)(2,1)S(1)}, u32[]{:S(2)}, u32[]{:S(2)}) collective-permute-start(bf16[2,256,512]{2,1,0:T(8,128)(2,1)} %get-tuple-element.32), channel_id=1, source_target_pairs={{0,1},{1,0},{2,3},{3,2},{4,5},{5,4},{6,7},{7,6},{8,9},{9,8},{10,11... | collective-permute-start | bytes 1572872 | tf_op jit(solution)/shard_map/ppermute | solution.py:340
  155.1 2.6 %copy-start.14 = (bf16[2,256,512]{2,1,0:T(8,128)(2,1)S(1)}, bf16[2,256,512]{2,1,0:T(8,128)(2,1)}, u32[]{:S(2)}) copy-start(bf16[2,256,512]{2,1,0:T(8,128)(2,1)} %get-tuple-element.27) | copy-start | bytes 1572868
  155.3 28.8 %collective-permute-start.21 = (bf16[256,512]{1,0:T(8,128)(2,1)S(1)}, bf16[256,512]{1,0:T(8,128)(2,1)S(1)}, u32[]{:S(2)}, u32[]{:S(2)}) collective-permute-start(bf16[256,512]{1,0:T(8,128)(2,1)S(1)} %fusion.14), channel_id=1, source_target_pairs={{0,2},{1,3},{2,0},{3,1},{4,6},{5,7},{6,4},{7,5},{8,10},{9,11},{10,... | collective-permute-start | bytes 786440 | tf_op jit(solution)/shard_map/ppermute | solution.py:340
  156.6 2.6 %copy-start.15 = (bf16[2,256,512]{2,1,0:T(8,128)(2,1)S(1)}, bf16[2,256,512]{2,1,0:T(8,128)(2,1)}, u32[]{:S(2)}) copy-start(bf16[2,256,512]{2,1,0:T(8,128)(2,1)} %get-tuple-element.31) | copy-start | bytes 1572868
  156.8 13.3 %collective-permute-start.4 = (bf16[256,512]{1,0:T(8,128)(2,1)S(1)}, bf16[256,512]{1,0:T(8,128)(2,1)S(1)}, u32[]{:S(2)}, u32[]{:S(2)}) collective-permute-start(bf16[256,512]{1,0:T(8,128)(2,1)S(1)} %fusion.11), channel_id=1, source_target_pairs={{0,2},{1,3},{2,0},{3,1},{4,6},{5,7},{6,4},{7,5},{8,10},{9,11},{10,... | collective-permute-start | bytes 786440 | tf_op jit(solution)/shard_map/ppermute | solution.py:340
  157.9 17.9 %collective-permute-start.10 = (bf16[256,512]{1,0:T(8,128)(2,1)S(1)}, bf16[256,512]{1,0:T(8,128)(2,1)S(1)}, u32[]{:S(2)}, u32[]{:S(2)}) collective-permute-start(bf16[256,512]{1,0:T(8,128)(2,1)S(1)} %fusion.12), channel_id=1, source_target_pairs={{0,2},{1,3},{2,0},{3,1},{4,6},{5,7},{6,4},{7,5},{8,10},{9,11},{10,... | collective-permute-start | bytes 786440 | tf_op jit(solution)/shard_map/ppermute | solution.py:340
  159.4 35.4 %copy-start.3 = (f32[1,256,512]{2,1,0:T(8,128)S(1)}, f32[1,256,512]{2,1,0:T(8,128)}, u32[]{:S(2)}) copy-start(f32[1,256,512]{2,1,0:T(8,128)} %param.12) | copy-start | bytes 1572868
  159.4 21.1 %collective-permute-start.16 = (bf16[256,512]{1,0:T(8,128)(2,1)S(1)}, bf16[256,512]{1,0:T(8,128)(2,1)S(1)}, u32[]{:S(2)}, u32[]{:S(2)}) collective-permute-start(bf16[256,512]{1,0:T(8,128)(2,1)S(1)} %fusion.13), channel_id=1, source_target_pairs={{0,2},{1,3},{2,0},{3,1},{4,6},{5,7},{6,4},{7,5},{8,10},{9,11},{10,... | collective-permute-start | bytes 786440 | tf_op jit(solution)/shard_map/ppermute | solution.py:340
  170.3 20.2 %collective-permute-start.5 = (bf16[256,512]{1,0:T(8,128)(2,1)S(1)}, bf16[256,512]{1,0:T(8,128)(2,1)S(1)}, u32[]{:S(2)}, u32[]{:S(2)}) collective-permute-start(bf16[256,512]{1,0:T(8,128)(2,1)S(1)} %fusion.10), channel_id=1, source_target_pairs={{0,8},{1,9},{2,10},{3,11},{4,12},{5,13},{6,14},{7,15},{8,0},{9,1},... | collective-permute-start | bytes 786440 | tf_op jit(solution)/shard_map/ppermute | solution.py:340
  175.9 14.6 %collective-permute-start.11 = (bf16[256,512]{1,0:T(8,128)(2,1)S(1)}, bf16[256,512]{1,0:T(8,128)(2,1)S(1)}, u32[]{:S(2)}, u32[]{:S(2)}) collective-permute-start(bf16[256,512]{1,0:T(8,128)(2,1)S(1)} %fusion.8), channel_id=1, source_target_pairs={{0,4},{1,5},{2,6},{3,7},{4,8},{5,9},{6,10},{7,11},{8,12},{9,13},{1... | collective-permute-start | bytes 786440 | tf_op jit(solution)/shard_map/ppermute | solution.py:340
  180.6 14.2 %collective-permute-start.17 = (bf16[256,512]{1,0:T(8,128)(2,1)S(1)}, bf16[256,512]{1,0:T(8,128)(2,1)S(1)}, u32[]{:S(2)}, u32[]{:S(2)}) collective-permute-start(bf16[256,512]{1,0:T(8,128)(2,1)S(1)} %fusion.6), channel_id=1, source_target_pairs={{0,12},{1,13},{2,14},{3,15},{4,0},{5,1},{6,2},{7,3},{8,4},{9,5},{1... | collective-permute-start | bytes 786440 | tf_op jit(solution)/shard_map/ppermute | solution.py:340
where the time goes:
time: 197 us; the launch traced here: 196 us
  Pallas kernels  77.2 us (39%)
  local copies, waits for them, and re-layouts  48.1 us (24%)
  starting transfers between devices  30.1 us (15%)
  waiting for transfers between devices  27 us (14%)
  other arithmetic  13.1 us (7%)
    pallas_call x4, Pallas kernels, data_term(): pl.pallas_call(data_kernel, grid_spec=pltpu.PrefetchScalarGridSpec(num_sc...  31 us
    ppermute x22, waiting for transfers between devices, send(): return lax.ppermute(value, 'phase', pairs)  27 us
    ppermute x22, starting transfers between devices, send(): return lax.ppermute(value, 'phase', pairs)  25.4 us
    pallas_call x4, Pallas kernels, image_term(): pl.pallas_call(image_kernel, grid_spec=pltpu.PrefetchScalarGridSpec(num_s...  25.2 us
    unnamed x93, local copies, waits for them, and re-layouts  22.7 us
    pallas_call x1, Pallas kernels, denoise(): pl.pallas_call(functools.partial(conv_kernel, ch), out_shape=jax.ShapeDty...  21 us
    another operation x4, local copies, waits for them, and re-layouts, band(): return jnp.stack(rows)  6.99 us
    concatenate x4, other arithmetic, shards(): xc = send(jnp.concatenate([xz, xy]), flip=1)  6.46 us
  transfers between devices with their start and end apart: 23, of which 5 were waited for; matrix products, arithmetic and copies ran while one was open for 28% of the time, Pallas kernels for 39%

commit v1 on v0

v1 whole, which is shorter than its diff:
```python
import functools
import math

import jax
import jax.numpy as jnp
import numpy as np
from jax import lax
from jax.experimental import pallas as pl
from jax.experimental.pallas import tpu as pltpu
from jax.sharding import PartitionSpec as P

STEP_SIZE = 0.5
WEIGHT_RED = 0.5
BF = jnp.bfloat16
F32 = jnp.float32
LANE_BLOCKS = 4
VMEM_LIMIT = 56 * 1024 * 1024


def trig(rows, cols, length):
    angle = (rows[:, None] * cols[None, :] % length) * (2.0 * math.pi / length)
    scale = 1.0 / math.sqrt(length)
    return np.cos(angle) * scale, np.sin(angle) * scale


def as_bf16(table):
    return jnp.asarray(table.astype(np.float32)).astype(BF)


def left_tables(length):
    half = np.arange(length // 2)
    tables = []
    for parity in (0, 1):
        c, s = trig(half, 2 * half + parity, length)
        tables.append(np.block([[c, -s], [s, c]]))
    return as_bf16(np.stack(tables))


def right_inverse(length):
    full = np.arange(length)
    c, s = trig(full, full, length)
    return as_bf16(np.block([[c, s], [-s, c]]))


def projector_tables(length):
    half = np.arange(length // 2)
    first, second = [], []
    for parity in (0, 1):
        c, s = trig(half, 2 * half + parity, length)
        first.append(np.block([[c, -s], [s, c]]))
        second.append(np.block([[c.T, s.T], [-s.T, c.T]]))
    return as_bf16(np.stack(first)), as_bf16(np.stack(second))


def cost(micros):
    return pl.CostEstimate(flops=int(micros * 1.0e9), bytes_accessed=0, transcendentals=0)


def dot(a, b):
    return jnp.dot(a, b, preferred_element_type=F32)


def data_kernel(group, ids, *refs):
    count = group * LANE_BLOCKS
    maps, left, right, first, second = refs[count : count + 5]
    masks = refs[count + 5 : count + 5 + group]
    out, proj = refs[count + 5 + group :]
    coils, rows, wide = maps.shape
    width, half = wide // 2, rows // 2
    for g in range(group):
        kd = refs[g * LANE_BLOCKS : (g + 1) * LANE_BLOCKS]
        mask = masks[g][0].astype(BF)
        keep = mask[:, :wide]
        masked = []
        for c in range(coils):
            parts = []
            for e in range(2):
                lines = [part[0, c, pl.ds(e, half, stride=2), :].astype(BF) for part in kd]
                real, imag = lines[: LANE_BLOCKS // 2], lines[LANE_BLOCKS // 2 :]
                stacked = jnp.concatenate([jnp.concatenate(real, 1), jnp.concatenate(imag, 1)], 0)
                parts.append(dot(left[e], stacked))
            upper, lower = parts[0] + parts[1], parts[0] - parts[1]
            real = jnp.concatenate([upper[:half], lower[:half]], 0).astype(BF)
            imag = jnp.concatenate([upper[half:], lower[half:]], 0).astype(BF)
            masked.append(jnp.concatenate([real, imag], 1) * keep)
        back = dot(jnp.concatenate(masked, 0), right[...])
        for e in range(2):
            lhs = first[e] * mask[:, wide + e * width : wide + (e + 1) * width]
            proj[g, e] = dot(lhs, second[e]).astype(BF)
        real, imag = None, None
        for c in range(coils):
            br, bi = back[c * rows : (c + 1) * rows, :width], back[c * rows : (c + 1) * rows, width:]
            sr, si = maps[c, :, :width], maps[c, :, width:]
            tr, ti = sr * br + si * bi, sr * bi - si * br
            real, imag = (tr, ti) if real is None else (real + tr, imag + ti)
        out[g, :, :width] = real.astype(BF)
        out[g, :, width:] = imag.astype(BF)


def data_term(ids, kdata, maps, masks, tables, group=2):
    phases, coils, rows, wide = kdata.shape
    count = ids.shape[0]
    lanes = wide // LANE_BLOCKS
    whole = lambda a: pl.BlockSpec(a.shape, lambda i, ids: (0,) * a.ndim)
    lines = lambda g, q: pl.BlockSpec(
        (1, coils, rows, lanes), lambda i, ids: (ids[group * i + g], 0, 0, q)
    )
    row = lambda g: pl.BlockSpec(
        (1,) + masks.shape[1:], lambda i, ids: (ids[group * i + g], 0, 0)
    )
    return pl.pallas_call(
        functools.partial(data_kernel, group),
        grid_spec=pltpu.PrefetchScalarGridSpec(
            num_scalar_prefetch=1,
            grid=(count // group,),
            in_specs=[lines(g, q) for g in range(group) for q in range(LANE_BLOCKS)]
            + [whole(a) for a in (maps,) + tables]
            + [row(g) for g in range(group)],
            out_specs=[
                pl.BlockSpec((group, rows, wide), lambda i, ids: (i, 0, 0)),
                pl.BlockSpec((group, 2, wide // 2, wide // 2), lambda i, ids: (i, 0, 0, 0)),
            ],
        ),
        out_shape=[
            jax.ShapeDtypeStruct((count, rows, wide), BF),
            jax.ShapeDtypeStruct((count, 2, wide // 2, wide // 2), BF),
        ],
        compiler_params=pltpu.CompilerParams(vmem_limit_bytes=VMEM_LIMIT),
        cost_estimate=cost(1.1 * count),
        name="data_term",
    )(ids, *[kdata] * (group * LANE_BLOCKS), maps, *tables, *[masks] * group)


def image_kernel(ids, place, far, near, maps, data, proj, noise_a, noise_b, away, mine, held):
    step = pl.program_id(0)
    coils, rows, wide = maps.shape
    width, quarter = wide // 2, wide // 4
    strip = noise_a.shape[1]

    @pl.when(step == 0)
    def _():
        held[...] = far[...]

    @pl.when(step == 1)
    def _():
        held[...] = near[...]

    at = pl.ds(pl.multiple_of(place[0], strip), strip)
    for g, noise in enumerate((noise_a, noise_b)):
        xr = held[g, :, :width].astype(F32)
        xi = held[g, :, width:].astype(F32)
        plus, minus = [], []
        for c in range(coils):
            sr, si = maps[c, :, :width], maps[c, :, width:]
            cr, ci = sr * xr - si * xi, sr * xi + si * xr
            cr0, cr1, ci0, ci1 = cr[:, :quarter], cr[:, quarter:], ci[:, :quarter], ci[:, quarter:]
            plus.append(jnp.concatenate([cr0 + cr1, ci0 + ci1], 1).astype(BF))
            minus.append(jnp.concatenate([cr0 - cr1, ci0 - ci1], 1).astype(BF))
        even = dot(jnp.concatenate(plus, 0), proj[g, 0])
        odd = dot(jnp.concatenate(minus, 0), proj[g, 1])
        real = -data[g, :, :width].astype(F32)
        imag = -data[g, :, width:].astype(F32)
        for c in range(coils):
            sr, si = maps[c, :, :width], maps[c, :, width:]
            p, q = even[c * rows : (c + 1) * rows], odd[c * rows : (c + 1) * rows]
            low, high = p + q, p - q
            br = jnp.concatenate([low[:, :quarter], high[:, :quarter]], 1)
            bi = jnp.concatenate([low[:, quarter:], high[:, quarter:]], 1)
            real = real + sr * br + si * bi
            imag = imag + sr * bi - si * br
        held[g, :, :width] = real.astype(BF)
        held[g, :, width:] = imag.astype(BF)
        held[g, at, :] = (held[g, at, :].astype(F32) + WEIGHT_RED * noise[0]).astype(BF)

    @pl.when(step == 0)
    def _():
        away[...] = held[...]

    @pl.when(step == 1)
    def _():
        mine[...] = held[...]


def image_term(ids, place, far, near, maps, data, proj, noise, chunk):
    coils, rows, wide = maps.shape
    strip, width = noise.shape[1], wide // 2
    whole = lambda a: pl.BlockSpec(a.shape, lambda i, ids, place: (0,) * a.ndim)
    extra = lambda g: pl.BlockSpec((1, strip, wide), lambda i, ids, place: (ids[2 * i + g], 0, 0))
    return pl.pallas_call(
        image_kernel,
        grid_spec=pltpu.PrefetchScalarGridSpec(
            num_scalar_prefetch=2,
            grid=(2,),
            in_specs=[
                whole(far),
                whole(near),
                whole(maps),
                pl.BlockSpec((2, rows, wide), lambda i, ids, place: (2 * chunk + i, 0, 0)),
                pl.BlockSpec((2, 2, width, width), lambda i, ids, place: (2 * chunk + i, 0, 0, 0)),
                extra(0),
                extra(1),
            ],
            out_specs=[whole(far)] * 2,
            scratch_shapes=[pltpu.VMEM((2, rows, wide), BF)],
        ),
        out_shape=[jax.ShapeDtypeStruct((2, rows, wide), BF)] * 2,
        compiler_params=pltpu.CompilerParams(vmem_limit_bytes=VMEM_LIMIT),
        cost_estimate=cost(5.0),
        name="image_term",
    )(ids, place, far, near, maps, data, proj, noise, noise)


def shifted(value, step):
    if step == 1:
        return value
    width = value.shape[1]
    lane = lax.broadcasted_iota(jnp.int32, value.shape, 1)
    if step == 0:
        return jnp.where(lane == 0, 0.0, pltpu.roll(value, 1, 1))
    return jnp.where(lane == width - 1, 0.0, pltpu.roll(value, width - 1, 1))


def conv_kernel(ch, place, strips, w1, w2, w3, pick1, pick2, spread3, out, x1, h1, noise, a1, a2, a3):
    phases, tall, wide = strips.shape
    width = wide // 2
    strip = tall - 8
    n1, n2, n3 = strip + 4, (strip + 2) // 2, strip + 2
    image_rows = strip * phases
    top = jnp.where(place[0] == 0, 0.0, 1.0)
    bottom = jnp.where(place[0] + strip == image_rows, 0.0, 1.0)

    base = dot(w1[...], pick1[...])
    for j in range(n1):
        line = base if j == 0 else pltpu.roll(base, j, 1)
        a1[j * ch : (j + 1) * ch] = line[:, : a1.shape[1]].astype(BF)
    base = dot(w2[...], pick2[...])
    for j in range(n2):
        line = base if j == 0 else pltpu.roll(base, j * ch, 1)
        a2[j * ch : (j + 1) * ch] = line[:, : a2.shape[1]].astype(BF)
    base = dot(w3[...], spread3[...])
    row = lax.broadcasted_iota(jnp.int32, (strip, base.shape[1]), 0)
    lane = lax.broadcasted_iota(jnp.int32, (strip, base.shape[1]), 1)
    for k in range(18):
        line = None
        for e in range(3):
            inside = (lane >= (row + e) * ch) & (lane < (row + e + 1) * ch)
            part = jnp.where(inside, base[3 * k + e : 3 * k + e + 1], 0.0)
            line = part if line is None else line + part
        a3[k * strip : (k + 1) * strip] = line[:, : a3.shape[1]].astype(BF)

    def inside_rows(value, rows):
        edge = rows * ch
        middle = value[edge : value.shape[0] - edge]
        return jnp.concatenate([value[:edge] * top, middle, value[value.shape[0] - edge :] * bottom], 0)

    def load(p, carry):
        image = strips[p].astype(F32)
        both = jnp.concatenate([image[:, :width], image[:, width:]], 0)
        for f in range(3):
            x1[p + 1, f * 2 * tall : (f + 1) * 2 * tall] = shifted(both, f).astype(BF)
        return carry

    lax.fori_loop(0, phases, load, 0, unroll=4)
    x1[0] = x1[phases]
    x1[phases + 1] = x1[1]

    def first(p, carry):
        stacked = x1[pl.ds(p, 3)].reshape(18 * tall, width)
        value = inside_rows(jnp.maximum(dot(a1[...], stacked), 0.0), 2)
        for f in range(3):
            h1[p + 1, f] = shifted(value, f).astype(BF)
        return carry

    lax.fori_loop(0, phases, first, 0, unroll=16)
    h1[0] = h1[phases]
    h1[phases + 1] = h1[1]
    noise[...] = jnp.zeros_like(noise)

    def second(p, carry):
        blocks = []
        for b in range(2):
            lo = b * n2 * ch
            stacked = h1[pl.ds(p, 3), :, lo : lo + (n2 + 2) * ch, :]
            stacked = stacked.reshape(9 * (n2 + 2) * ch, width)
            blocks.append(dot(a2[...], stacked))
        value = inside_rows(jnp.maximum(jnp.concatenate(blocks, 0), 0.0), 1)
        spread = dot(a3[...], value.astype(BF))
        for d in range(3):
            part = None
            for f in range(3):
                lo = (d * 3 + f) * 2 * strip
                piece = shifted(spread[lo : lo + 2 * strip], f)
                part = piece if part is None else part + piece
            noise[p + 2 - d] += part
        return carry

    lax.fori_loop(0, phases, second, 0, unroll=16)
    noise[phases] += noise[0]
    noise[1] += noise[phases + 1]

    def store(p, carry):
        both = noise[p + 1]
        out[p, :, :width] = both[:strip]
        out[p, :, width:] = both[strip:]
        return carry

    lax.fori_loop(0, phases, store, 0, unroll=4)


def pick_tables(cin, tall, n2, ch, n3):
    pad = lambda n: -(-n // 128) * 128
    pick1 = np.zeros((cin * 27, pad(9 * cin * tall)), np.float32)
    pick2 = np.zeros((ch * 27, pad(9 * (n2 + 2) * ch)), np.float32)
    for d in range(3):
        for e in range(3):
            for f in range(3):
                tap = (d * 3 + e) * 3 + f
                for c in range(cin):
                    pick1[c * 27 + tap, ((d * 3 + f) * cin + c) * tall + 1 + e] = 1.0
                for c in range(ch):
                    pick2[c * 27 + tap, ((d * 3 + f) * (n2 + 2) + e) * ch + c] = 1.0
    spread3 = np.zeros((ch, pad(n3 * ch)), np.float32)
    for c in range(ch):
        spread3[c, c : n3 * ch : ch] = 1.0
    return as_bf16(pick1), as_bf16(pick2), as_bf16(spread3)


def denoise(strips, w_first, w_middle, w_last, place):
    phases, tall, wide = strips.shape
    strip, width, (ch, cin) = tall - 8, wide // 2, w_first.shape[:2]
    n1, n2, n3 = strip + 4, (strip + 2) // 2, strip + 2
    picks = pick_tables(cin, tall, n2, ch, n3)
    weights = (
        w_first.reshape(ch, cin * 27),
        w_middle.reshape(ch, ch * 27),
        jnp.transpose(w_last, (2, 4, 0, 3, 1)).reshape(54, ch),
    )
    vmem = pl.BlockSpec(memory_space=pltpu.VMEM)
    return pl.pallas_call(
        functools.partial(conv_kernel, ch),
        in_specs=[pl.BlockSpec(memory_space=pltpu.SMEM)] + [vmem] * 7,
        out_specs=vmem,
        out_shape=jax.ShapeDtypeStruct((phases, strip, wide), F32),
        scratch_shapes=[
            pltpu.VMEM((phases + 2, 6 * tall, width), BF),
            pltpu.VMEM((phases + 2, 3, n1 * ch, width), BF),
            pltpu.VMEM((phases + 2, 2 * strip, width), F32),
            pltpu.VMEM((n1 * ch, 9 * cin * tall), BF),
            pltpu.VMEM((n2 * ch, 9 * (n2 + 2) * ch), BF),
            pltpu.VMEM((18 * strip, n3 * ch), BF),
        ],
        compiler_params=pltpu.CompilerParams(vmem_limit_bytes=VMEM_LIMIT),
        cost_estimate=cost(13.0),
        name="denoise",
    )(place, strips, *weights, *picks)


def prepare_kernel(estimate, mask, pick, image, strips, masks, padded):
    rows, wide = estimate.shape[1:]
    phases, tall = strips.shape[:2]
    strip = tall - 8
    value = estimate[0]
    image[0] = value.astype(BF)
    edge = jnp.zeros((4, wide), F32)
    padded[0:4] = edge
    padded[rows + 4 : rows + 8] = edge
    padded[4 : rows + 4] = value
    for j in range(phases):
        strips[j] = padded[j * strip : j * strip + tall].astype(BF)
    spread = dot(mask[...].astype(F32).astype(BF), pick[...])
    for p in range(phases):
        masks[p] = spread[p : p + 1]


def prepare(estimate, mask):
    rows, wide = estimate.shape[1:]
    phases, width = mask.shape
    tall = rows // phases + 8
    pick = np.zeros((width, 4 * width), np.float32)
    half = width // 2
    for k in range(width):
        pick[k, [k, width + k]] = 1.0
        at = 2 * width + (k % 2) * width + k // 2
        pick[k, [at, at + half]] = 1.0
    return pl.pallas_call(
        prepare_kernel,
        out_shape=[
            jax.ShapeDtypeStruct((1, rows, wide), BF),
            jax.ShapeDtypeStruct((phases, tall, wide), BF),
            jax.ShapeDtypeStruct((phases, 1, 4 * width), F32),
        ],
        scratch_shapes=[pltpu.VMEM((rows + 8, wide), F32)],
        cost_estimate=cost(2.0),
        name="prepare",
    )(estimate, mask, as_bf16(pick))


def shards(estimate, kdata, maps, mask, w_first, w_middle, w_last):
    count = lax.axis_size("phase")
    me = lax.axis_index("phase")
    planes = count // 4
    rows, wide = estimate.shape[1:]
    strip = rows // count
    tables = (left_tables(rows), right_inverse(wide // 2)) + projector_tables(wide // 2)
    place = (me * strip).astype(jnp.int32)[None]

    def send(value, shift=0, flip=0):
        pairs = [(i, ((i ^ flip) + 4 * shift) % count) for i in range(count)]
        return lax.ppermute(value, "phase", pairs)

    image, strips, masks = prepare(estimate, mask)
    strips = lax.all_to_all(strips, "phase", 0, 0, tiled=True)

    order = [k for k in (2, 1, planes - 1) if 0 < k < planes]
    order = list(dict.fromkeys(order + list(range(1, planes)) + [0]))
    images = {}
    for k in order:
        xz = image if k == 0 else send(image, shift=planes - k)
        near = jnp.concatenate([xz, send(xz, flip=2)])
        images[k] = (send(near, flip=1), near)

    flips = jnp.array([1, 3, 0, 2], jnp.int32)
    ids = {k: ((me ^ flips) + 4 * k) % count for k in order}
    terms = {}
    for pair in [order[i : i + 2] for i in range(0, planes, 2)]:
        both = jnp.concatenate([ids[k] for k in pair])
        data, proj = data_term(both, kdata, maps, masks, tables)
        for n, k in enumerate(pair):
            terms[k] = (data, proj, n)

    noise = denoise(strips, w_first, w_middle, w_last, place)

    total = None
    for k in order:
        data, proj, n = terms[k]
        away, mine = image_term(ids[k], place, *images[k], maps, data, proj, noise, n)
        got = send(away, flip=1)
        pair = mine.astype(F32) + got.astype(F32)
        other = send(pair[1].astype(BF), flip=2)
        plane = pair[0] + other.astype(F32)
        if k:
            plane = send(plane.astype(BF), shift=k).astype(F32)
        total = plane if total is None else total + plane
    return estimate - STEP_SIZE * total[None]


def solution(mesh):
    return jax.shard_map(
        shards,
        mesh=mesh,
        in_specs=(
            P(("slab", "phase"), None, None),
            P("slab", "phase", None, None),
            P(("slab", "phase"), None, None),
            P("slab", None),
            P(),
            P(),
            P(),
        ),
        out_specs=P(("slab", "phase"), None, None),
        check_vma=False,
    )
```

time: 197 us -> 138 us (0.70)
  local copies, waits for them, and re-layouts: 48.1 us -> 4.24 us
  Pallas kernels: 77.2 us -> 57.4 us
  waiting for transfers between devices: 27 us -> 42.2 us
  other arithmetic: 13.1 us -> 3.07 us
    unnamed x93 -> x46, local copies, waits for them, and re-layouts: 22.7 us -> 1.94 us
    pallas_call x5 -> x4, Pallas kernels: 51.9 us -> 34.5 us  [the longest x2 19.5 us: data_term(): pl.pallas_call(functools.partial(data_kernel, group), grid_spec=pltpu.Pre...]
    ppermute x22, waiting for transfers between devices: 27 us -> 42.2 us  [send(): return lax.ppermute(value, 'phase', pairs)]
    another operation x5 -> x0, local copies, waits for them, and re-layouts: 7.6 us -> none  [the longest x4 6.99 us: band(): return jnp.stack(rows)]
    transpose x2 -> x1, local copies, waits for them, and re-layouts: 7.17 us -> 0.01 us  [denoise(): jnp.transpose(w_last, (2, 4, 0, 3, 1)).reshape(54, ch)]
    reshape x4 -> x5, local copies, waits for them, and re-layouts: 9.22 us -> 2.08 us  [the longest x2 0.77 us: denoise(): w_middle.reshape(ch, ch * 27)]
    concatenate x5 -> x2, other arithmetic: 7.09 us -> 1.26 us  [shards(): both = jnp.concatenate([ids[k] for k in pair])]
    convert_element_type x4 -> x0, other arithmetic: 2.48 us -> none  [the longest x1 1.09 us: shards(): image = estimate.astype(BF)]
  transfers between devices with their start and end apart: 23 -> 23, of which waited for: 5 -> 8; matrix products, arithmetic and copies ran while one was open for 28% -> 3% of each run, Pallas kernels for 39% -> 40%
where the time goes in v1:
time: 138 us
  Pallas kernels  57.4 us (42%)
  waiting for transfers between devices  42.2 us (31%)
  starting transfers between devices  30.3 us (22%)
  local copies, waits for them, and re-layouts  4.24 us (3%)
  other arithmetic  3.07 us (2%)
    ppermute x22, waiting for transfers between devices, send(): return lax.ppermute(value, 'phase', pairs)  42.2 us
    ppermute x22, starting transfers between devices, send(): return lax.ppermute(value, 'phase', pairs)  25.8 us
    pallas_call x4, Pallas kernels, image_term(): pl.pallas_call(image_kernel, grid_spec=pltpu.PrefetchScalarGridSpec(num_s...  22.9 us
    pallas_call x2, Pallas kernels, data_term(): pl.pallas_call(functools.partial(data_kernel, group), grid_spec=pltpu.Pre...  19.5 us
    pallas_call x1, Pallas kernels, denoise(): pl.pallas_call(functools.partial(conv_kernel, ch), in_specs=[pl.BlockSpec...  12.7 us
    all_to_all x1, starting transfers between devices, shards(): strips = lax.all_to_all(strips, 'phase', 0, 0, tiled=True)  4.53 us
  transfers between devices with their start and end apart: 23, of which 8 were waited for; matrix products, arithmetic and copies ran while one was open for 3% of the time, Pallas kernels for 40%

profile of v1, /device:TPU:0, one launch (start us, length us, event | category | flops | bytes accessed | tf_op | source)
XLA Modules:
  0.0 137.7 jit_solution(7203854266913087778)
XLA Ops:
  0.0 2.3 %prepare.1 = (bf16[1,256,512]{2,1,0:T(8,128)(2,1)}, bf16[16,24,512]{2,1,0:T(8,128)(2,1)}, f32[16,1,1024]{2,1,0:T(1,128)}) custom-call(f32[1,256,512]{2,1,0:T(8,128)} %estimate.1, s32[16,256]{1,0:T(8,128)} %mask.1, bf16[256,1024]{1,0:T(8,128)(2,1)} %constant.69.pick), custom_call_target="tpu_custom_call" | custom-call | flops 2000000000 | tf_op jit(solution)/shard_map/prepare/pallas_call | solution.py:385
  2.3 4.0 %collective-permute-start = (bf16[1,256,512]{2,1,0:T(8,128)(2,1)}, bf16[1,256,512]{2,1,0:T(8,128)(2,1)S(1)}, u32[]{:S(2)}, u32[]{:S(2)}) collective-permute-start(bf16[1,256,512]{2,1,0:T(8,128)(2,1)} %get-tuple-element.20), channel_id=1, source_target_pairs={{0,8},{1,9},{2,10},{3,11},{4,12},{5,13},{6,14},{7,15},{8,0},{9,1},... | collective-permute-start | bytes 786440 | tf_op jit(solution)/shard_map/ppermute | solution.py:409
  6.3 1.3 collective-permute-start.6
  7.7 0.7 collective-permute-start.12
  8.4 1.5 %collective-permute-start.18 = (bf16[1,256,512]{2,1,0:T(8,128)(2,1)}, bf16[1,256,512]{2,1,0:T(8,128)(2,1)S(1)}, u32[]{:S(2)}, u32[]{:S(2)}) collective-permute-start(bf16[1,256,512]{2,1,0:T(8,128)(2,1)} %get-tuple-element.20), channel_id=1, source_target_pairs={{0,2},{1,3},{2,0},{3,1},{4,6},{5,7},{6,4},{7,5},{8,10},{9,11},{10,... | collective-permute-start | bytes 786440 | tf_op jit(solution)/shard_map/ppermute | solution.py:409
  9.9 4.5 %all-to-all-start = ((bf16[16,24,512]{2,1,0:T(8,128)(2,1)}), bf16[16,24,512]{2,1,0:T(8,128)(2,1)S(1)}, u32[]{:S(2)}, u32[]{:S(2)}) async-start(bf16[16,24,512]{2,1,0:T(8,128)(2,1)} %get-tuple-element.24), calls=%async_computation | async-start | bytes 786432 | tf_op jit(solution)/shard_map/all_to_all | solution.py:412
  14.5 0.6 pad_add_fusion.ids
  15.1 0.7 pad_add_fusion.1.ids
  15.7 9.7 %data_term.2 = (bf16[8,256,512]{2,1,0:T(8,128)(2,1)}, bf16[8,2,256,256]{3,2,1,0:T(8,128)(2,1)}) custom-call(s32[8]{0:T(128)} %pad_add_fusion.ids, f32[16,2,256,512]{3,2,1,0:T(8,128)} %refs_7_.3, f32[16,2,256,512]{3,2,1,0:T(8,128)} %refs_7_.3, f32[16,2,256,512]{3,2,1,0:T(8,128)} %refs_7_.3, f32[16,2,256,512]{3,2,1,0:T(8,128)} %refs_7_.3, ...), custom_call_target="tpu_custom_call" | custom-call | flops 8800000000 | tf_op jit(solution)/shard_map/data_term/pallas_call | solution.py:111
  25.5 0.0 copy-start.11
  25.5 0.0 copy-start.12
  25.6 0.0 copy-start.13
  25.6 9.8 %data_term.3 = (bf16[8,256,512]{2,1,0:T(8,128)(2,1)}, bf16[8,2,256,256]{3,2,1,0:T(8,128)(2,1)}) custom-call(s32[8]{0:T(128)} %pad_add_fusion.1.ids, f32[16,2,256,512]{3,2,1,0:T(8,128)} %refs_7_.3, f32[16,2,256,512]{3,2,1,0:T(8,128)} %refs_7_.3, f32[16,2,256,512]{3,2,1,0:T(8,128)} %refs_7_.3, f32[16,2,256,512]{3,2,1,0:T(8,128)} %refs_7_.3, ...), custom_call_target="tpu_custom_call" | custom-call | flops 8800000000 | tf_op jit(solution)/shard_map/data_term/pallas_call | solution.py:111
  35.4 0.1 copy.21
  35.6 0.1 reshape.15
  35.7 0.7 copy.24.w2
  36.4 0.7 copy.23.w1
  37.1 0.6 reshape.16.w3
  37.7 0.0 collective-permute-done.18
  37.7 0.0 copy-start.10
  37.7 0.5 collective-permute-start.19
  38.2 0.0 collective-permute-done
  38.2 1.7 %collective-permute-start.1 = (bf16[1,256,512]{2,1,0:T(8,128)(2,1)S(1)}, bf16[1,256,512]{2,1,0:T(8,128)(2,1)S(1)}, u32[]{:S(2)}, u32[]{:S(2)}) collective-permute-start(bf16[1,256,512]{2,1,0:T(8,128)(2,1)S(1)} %collective-permute-done), channel_id=1, source_target_pairs={{0,2},{1,3},{2,0},{3,1},{4,6},{5,7},{6,4},{7,5},{8,10},{9,11},{10,... | collective-permute-start | bytes 786440 | tf_op jit(solution)/shard_map/ppermute | solution.py:409
  39.9 0.0 collective-permute-done.6
  39.9 0.4 collective-permute-start.7
  40.4 1.7 %collective-permute-start.13 = (bf16[1,256,512]{2,1,0:T(8,128)(2,1)S(1)}, bf16[1,256,512]{2,1,0:T(8,128)(2,1)S(1)}, u32[]{:S(2)}, u32[]{:S(2)}) collective-permute-start(bf16[1,256,512]{2,1,0:T(8,128)(2,1)S(1)} %collective-permute-done.12), channel_id=1, source_target_pairs={{0,2},{1,3},{2,0},{3,1},{4,6},{5,7},{6,4},{7,5},{8,10},{9,11},{10,... | collective-permute-start | bytes 786440 | tf_op jit(solution)/shard_map/ppermute | solution.py:409
  42.1 5.2 %collective-permute-done.1 = bf16[1,256,512]{2,1,0:T(8,128)(2,1)S(1)} collective-permute-done((bf16[1,256,512]{2,1,0:T(8,128)(2,1)S(1)}, bf16[1,256,512]{2,1,0:T(8,128)(2,1)S(1)}, u32[]{:S(2)}, u32[]{:S(2)}) %collective-permute-start.1) | collective-permute-done | bytes 262176 | tf_op jit(solution)/shard_map/ppermute | solution.py:409
  47.4 0.1 collective-permute-start.2
  47.5 5.5 %collective-permute-done.7 = bf16[1,256,512]{2,1,0:T(8,128)(2,1)S(1)} collective-permute-done((bf16[1,256,512]{2,1,0:T(8,128)(2,1)S(1)}, bf16[1,256,512]{2,1,0:T(8,128)(2,1)S(1)}, u32[]{:S(2)}, u32[]{:S(2)}) %collective-permute-start.7) | collective-permute-done | bytes 262176 | tf_op jit(solution)/shard_map/ppermute | solution.py:409
  53.0 0.1 collective-permute-start.8
  53.1 4.9 %collective-permute-done.13 = bf16[1,256,512]{2,1,0:T(8,128)(2,1)S(1)} collective-permute-done((bf16[1,256,512]{2,1,0:T(8,128)(2,1)S(1)}, bf16[1,256,512]{2,1,0:T(8,128)(2,1)S(1)}, u32[]{:S(2)}, u32[]{:S(2)}) %collective-permute-start.13) | collective-permute-done | bytes 262176 | tf_op jit(solution)/shard_map/ppermute | solution.py:409
  58.0 0.1 collective-permute-start.14
  58.1 0.8 copy-done.5
  58.9 12.7 %denoise.1.noise_a.noise_b = f32[16,16,512]{2,1,0:T(8,128)} custom-call(s32[1]{0:T(128)} %bitcast.place, bf16[16,24,512]{2,1,0:T(8,128)(2,1)} %copy-done.5, bf16[16,54]{1,0:T(8,128)(2,1)} %copy.23.w1, bf16[16,432]{1,0:T(8,128)(2,1)} %copy.24.w2, bf16[54,16]{1,0:T(8,128)(2,1)} %reshape.16.w3, bf16[54,512]{1,0:T(8,128)(2,1)} %constant.73.pick1, ...), custom_call_target="tpu_custom_call" | custom-call | flops 12999999488 | tf_op jit(solution)/shard_map/denoise/pallas_call | solution.py:339
  71.6 5.6 %image_term.7 = (bf16[2,256,512]{2,1,0:T(8,128)(2,1)}, bf16[2,256,512]{2,1,0:T(8,128)(2,1)}) custom-call(s32[4]{0:T(128)} %copy-done.17, s32[1]{0:T(128)} %bitcast.place, bf16[2,256,512]{2,1,0:T(8,128)(2,1)} %collective-permute-done.19.far, bf16[2,256,512]{2,1,0:T(8,128)(2,1)} %copy-done.10, f32[2,256,512]{2,1,0:T(8,128)} %maps.7, ...), custom_call_target="tpu_custom_call" | custom-call | flops 5000000000 | tf_op jit(solution)/shard_map/image_term/pallas_call | solution.py:189
  77.2 0.4 collective-permute-start.20
  77.6 5.7 %image_term.4 = (bf16[2,256,512]{2,1,0:T(8,128)(2,1)}, bf16[2,256,512]{2,1,0:T(8,128)(2,1)}) custom-call(s32[4]{0:T(128)} %copy-done.16, s32[1]{0:T(128)} %bitcast.place, bf16[2,256,512]{2,1,0:T(8,128)(2,1)} %collective-permute-done.2.far, bf16[2,256,512]{2,1,0:T(8,128)(2,1)} %copy-done.9, f32[2,256,512]{2,1,0:T(8,128)} %maps.7, ...), custom_call_target="tpu_custom_call" | custom-call | flops 5000000000 | tf_op jit(solution)/shard_map/image_term/pallas_call | solution.py:189
  83.4 0.1 collective-permute-start.3
  83.5 5.7 %image_term.5 = (bf16[2,256,512]{2,1,0:T(8,128)(2,1)}, bf16[2,256,512]{2,1,0:T(8,128)(2,1)}) custom-call(s32[4]{0:T(128)} %copy-done.15, s32[1]{0:T(128)} %bitcast.place, bf16[2,256,512]{2,1,0:T(8,128)(2,1)} %collective-permute-done.8.far, bf16[2,256,512]{2,1,0:T(8,128)(2,1)} %copy-done.8, f32[2,256,512]{2,1,0:T(8,128)} %maps.7, ...), custom_call_target="tpu_custom_call" | custom-call | flops 5000000000 | tf_op jit(solution)/shard_map/image_term/pallas_call | solution.py:189
  89.1 0.4 collective-permute-start.9
  89.6 0.8 copy-done.19
  90.3 5.9 %image_term.6 = (bf16[2,256,512]{2,1,0:T(8,128)(2,1)}, bf16[2,256,512]{2,1,0:T(8,128)(2,1)}) custom-call(s32[4]{0:T(128)} %copy-done.14, s32[1]{0:T(128)} %bitcast.place, bf16[2,256,512]{2,1,0:T(8,128)(2,1)} %copy-done.19, bf16[2,256,512]{2,1,0:T(8,128)(2,1)} %copy-done.7, f32[2,256,512]{2,1,0:T(8,128)} %maps.7, ...), custom_call_target="tpu_custom_call" | custom-call | flops 5000000000 | tf_op jit(solution)/shard_map/image_term/pallas_call | solution.py:189
  96.2 0.1 collective-permute-start.15
  96.3 0.2 convert_add_fusion
  96.6 1.8 %collective-permute-start.21 = (bf16[256,512]{1,0:T(8,128)(2,1)S(1)}, bf16[256,512]{1,0:T(8,128)(2,1)S(1)}, u32[]{:S(2)}, u32[]{:S(2)}) collective-permute-start(bf16[256,512]{1,0:T(8,128)(2,1)S(1)} %fusion.14), channel_id=1, source_target_pairs={{0,2},{1,3},{2,0},{3,1},{4,6},{5,7},{6,4},{7,5},{8,10},{9,11},{10,... | collective-permute-start | bytes 786440 | tf_op jit(solution)/shard_map/ppermute | solution.py:409
  98.4 0.1 convert_add_fusion.3
  98.6 0.7 collective-permute-start.4
  99.3 0.1 convert_add_fusion.2
  99.5 1.5 %collective-permute-start.10 = (bf16[256,512]{1,0:T(8,128)(2,1)S(1)}, bf16[256,512]{1,0:T(8,128)(2,1)S(1)}, u32[]{:S(2)}, u32[]{:S(2)}) collective-permute-start(bf16[256,512]{1,0:T(8,128)(2,1)S(1)} %fusion.12), channel_id=1, source_target_pairs={{0,2},{1,3},{2,0},{3,1},{4,6},{5,7},{6,4},{7,5},{8,10},{9,11},{10,... | collective-permute-start | bytes 786440 | tf_op jit(solution)/shard_map/ppermute | solution.py:409
  101.0 0.1 convert_add_fusion.1
  101.1 0.0 copy-start
  101.2 0.7 collective-permute-start.16
  101.8 9.6 %collective-permute-done.4 = bf16[256,512]{1,0:T(8,128)(2,1)S(1)} collective-permute-done((bf16[256,512]{1,0:T(8,128)(2,1)S(1)}, bf16[256,512]{1,0:T(8,128)(2,1)S(1)}, u32[]{:S(2)}, u32[]{:S(2)}) %collective-permute-start.4) | collective-permute-done | bytes 262176 | tf_op jit(solution)/shard_map/ppermute | solution.py:409
  111.4 0.1 fusion.10
  111.5 2.6 %collective-permute-start.5 = (bf16[256,512]{1,0:T(8,128)(2,1)S(1)}, bf16[256,512]{1,0:T(8,128)(2,1)S(1)}, u32[]{:S(2)}, u32[]{:S(2)}) collective-permute-start(bf16[256,512]{1,0:T(8,128)(2,1)S(1)} %fusion.10), channel_id=1, source_target_pairs={{0,8},{1,9},{2,10},{3,11},{4,12},{5,13},{6,14},{7,15},{8,0},{9,1},... | collective-permute-start | bytes 786440 | tf_op jit(solution)/shard_map/ppermute | solution.py:409
  114.1 2.9 %collective-permute-done.10 = bf16[256,512]{1,0:T(8,128)(2,1)S(1)} collective-permute-done((bf16[256,512]{1,0:T(8,128)(2,1)S(1)}, bf16[256,512]{1,0:T(8,128)(2,1)S(1)}, u32[]{:S(2)}, u32[]{:S(2)}) %collective-permute-start.10) | collective-permute-done | bytes 262176 | tf_op jit(solution)/shard_map/ppermute | solution.py:409
  117.0 0.1 fusion.8
  117.1 1.8 %collective-permute-start.11 = (bf16[256,512]{1,0:T(8,128)(2,1)S(1)}, bf16[256,512]{1,0:T(8,128)(2,1)S(1)}, u32[]{:S(2)}, u32[]{:S(2)}) collective-permute-start(bf16[256,512]{1,0:T(8,128)(2,1)S(1)} %fusion.8), channel_id=1, source_target_pairs={{0,4},{1,5},{2,6},{3,7},{4,8},{5,9},{6,10},{7,11},{8,12},{9,13},{1... | collective-permute-start | bytes 786440 | tf_op jit(solution)/shard_map/ppermute | solution.py:409
  118.8 3.2 %collective-permute-done.16 = bf16[256,512]{1,0:T(8,128)(2,1)S(1)} collective-permute-done((bf16[256,512]{1,0:T(8,128)(2,1)S(1)}, bf16[256,512]{1,0:T(8,128)(2,1)S(1)}, u32[]{:S(2)}, u32[]{:S(2)}) %collective-permute-start.16) | collective-permute-done | bytes 262176 | tf_op jit(solution)/shard_map/ppermute | solution.py:409
  122.1 0.1 fusion.6
  122.2 3.6 %collective-permute-start.17 = (bf16[256,512]{1,0:T(8,128)(2,1)S(1)}, bf16[256,512]{1,0:T(8,128)(2,1)S(1)}, u32[]{:S(2)}, u32[]{:S(2)}) collective-permute-start(bf16[256,512]{1,0:T(8,128)(2,1)S(1)} %fusion.6), channel_id=1, source_target_pairs={{0,12},{1,13},{2,14},{3,15},{4,0},{5,1},{6,2},{7,3},{8,4},{9,5},{1... | collective-permute-start | bytes 786440 | tf_op jit(solution)/shard_map/ppermute | solution.py:409
  125.8 6.6 %collective-permute-done.5 = bf16[256,512]{1,0:T(8,128)(2,1)S(1)} collective-permute-done((bf16[256,512]{1,0:T(8,128)(2,1)S(1)}, bf16[256,512]{1,0:T(8,128)(2,1)S(1)}, u32[]{:S(2)}, u32[]{:S(2)}) %collective-permute-start.5) | collective-permute-done | bytes 262176 | tf_op jit(solution)/shard_map/ppermute | solution.py:409
  132.4 4.3 %collective-permute-done.17 = bf16[256,512]{1,0:T(8,128)(2,1)S(1)} collective-permute-done((bf16[256,512]{1,0:T(8,128)(2,1)S(1)}, bf16[256,512]{1,0:T(8,128)(2,1)S(1)}, u32[]{:S(2)}, u32[]{:S(2)}) %collective-permute-start.17) | collective-permute-done | bytes 262176 | tf_op jit(solution)/shard_map/ppermute | solution.py:409
  136.7 1.0 fusion.4
  (61 shorter events, 0.4 us)
Async XLA Ops:
  0.0 14.4 %copy-start.18 = (s32[4]{0:T(128)S(1)}, s32[4]{0:T(128)}, u32[]{:S(2)}) copy-start(s32[4]{0:T(128)} %constant.62.clone) | copy-start | bytes 52
  2.3 35.9 %collective-permute-start = (bf16[1,256,512]{2,1,0:T(8,128)(2,1)}, bf16[1,256,512]{2,1,0:T(8,128)(2,1)S(1)}, u32[]{:S(2)}, u32[]{:S(2)}) collective-permute-start(bf16[1,256,512]{2,1,0:T(8,128)(2,1)} %get-tuple-element.20), channel_id=1, source_target_pairs={{0,8},{1,9},{2,10},{3,11},{4,12},{5,13},{6,14},{7,15},{8,0},{9,1},... | collective-permute-start | bytes 786440 | tf_op jit(solution)/shard_map/ppermute | solution.py:409
  6.3 33.6 %collective-permute-start.6 = (bf16[1,256,512]{2,1,0:T(8,128)(2,1)}, bf16[1,256,512]{2,1,0:T(8,128)(2,1)S(1)}, u32[]{:S(2)}, u32[]{:S(2)}) collective-permute-start(bf16[1,256,512]{2,1,0:T(8,128)(2,1)} %get-tuple-element.20), channel_id=1, source_target_pairs={{0,12},{1,13},{2,14},{3,15},{4,0},{5,1},{6,2},{7,3},{8,4},{9,5},{1... | collective-permute-start | bytes 786440 | tf_op jit(solution)/shard_map/ppermute | solution.py:409
  7.7 32.7 %collective-permute-start.12 = (bf16[1,256,512]{2,1,0:T(8,128)(2,1)}, bf16[1,256,512]{2,1,0:T(8,128)(2,1)S(1)}, u32[]{:S(2)}, u32[]{:S(2)}) collective-permute-start(bf16[1,256,512]{2,1,0:T(8,128)(2,1)} %get-tuple-element.20), channel_id=1, source_target_pairs={{0,4},{1,5},{2,6},{3,7},{4,8},{5,9},{6,10},{7,11},{8,12},{9,13},{1... | collective-permute-start | bytes 786440 | tf_op jit(solution)/shard_map/ppermute | solution.py:409
  8.4 29.4 %collective-permute-start.18 = (bf16[1,256,512]{2,1,0:T(8,128)(2,1)}, bf16[1,256,512]{2,1,0:T(8,128)(2,1)S(1)}, u32[]{:S(2)}, u32[]{:S(2)}) collective-permute-start(bf16[1,256,512]{2,1,0:T(8,128)(2,1)} %get-tuple-element.20), channel_id=1, source_target_pairs={{0,2},{1,3},{2,0},{3,1},{4,6},{5,7},{6,4},{7,5},{8,10},{9,11},{10,... | collective-permute-start | bytes 786440 | tf_op jit(solution)/shard_map/ppermute | solution.py:409
  9.9 48.2 %all-to-all-start = ((bf16[16,24,512]{2,1,0:T(8,128)(2,1)}), bf16[16,24,512]{2,1,0:T(8,128)(2,1)S(1)}, u32[]{:S(2)}, u32[]{:S(2)}) async-start(bf16[16,24,512]{2,1,0:T(8,128)(2,1)} %get-tuple-element.24), calls=%async_computation | async-start | bytes 786432 | tf_op jit(solution)/shard_map/all_to_all | solution.py:412
  14.4 11.0 %copy-start.14 = (s32[4]{0:T(128)}, s32[4]{0:T(128)S(1)}, u32[]{:S(2)}) copy-start(s32[4]{0:T(128)S(1)} %get-tuple-element.36.ids) | copy-start | bytes 52
  14.5 11.0 %copy-start.15 = (s32[4]{0:T(128)}, s32[4]{0:T(128)S(1)}, u32[]{:S(2)}) copy-start(s32[4]{0:T(128)S(1)} %get-tuple-element.38.ids) | copy-start | bytes 52
  14.5 11.0 %copy-start.16 = (s32[4]{0:T(128)}, s32[4]{0:T(128)S(1)}, u32[]{:S(2)}) copy-start(s32[4]{0:T(128)S(1)} %get-tuple-element.35.ids) | copy-start | bytes 52
  14.5 11.0 %copy-start.17 = (s32[4]{0:T(128)}, s32[4]{0:T(128)S(1)}, u32[]{:S(2)}) copy-start(s32[4]{0:T(128)S(1)} %get-tuple-element.37.ids) | copy-start | bytes 52
  25.5 9.9 %copy-start.6 = (bf16[1,256,512]{2,1,0:T(8,128)(2,1)S(1)}, bf16[1,256,512]{2,1,0:T(8,128)(2,1)}, u32[]{:S(2)}) copy-start(bf16[1,256,512]{2,1,0:T(8,128)(2,1)} %get-tuple-element.20) | copy-start | bytes 786436
  25.5 9.9 %copy-start.11 = (bf16[16,16,3,3,3]{1,0,4,3,2:T(8,128)(2,1)S(1)}, bf16[16,16,3,3,3]{1,0,4,3,2:T(8,128)(2,1)}, u32[]{:S(2)}) copy-start(bf16[16,16,3,3,3]{1,0,4,3,2:T(8,128)(2,1)} %param.21) | copy-start | bytes 41476
  25.5 10.8 %copy-start.12 = (bf16[16,2,3,3,3]{0,1,4,3,2:T(2,128)(2,1)S(1)}, bf16[16,2,3,3,3]{0,1,4,3,2:T(2,128)(2,1)}, u32[]{:S(2)}) copy-start(bf16[16,2,3,3,3]{0,1,4,3,2:T(2,128)(2,1)} %param.20) | copy-start | bytes 5188
  25.6 11.5 %copy-start.13 = (bf16[2,16,3,3,3]{1,0,4,3,2:T(2,128)(2,1)S(1)}, bf16[2,16,3,3,3]{1,0,4,3,2:T(2,128)(2,1)}, u32[]{:S(2)}) copy-start(bf16[2,16,3,3,3]{1,0,4,3,2:T(2,128)(2,1)} %param.22) | copy-start | bytes 5188
  37.7 33.8 %copy-start.10 = (bf16[2,256,512]{2,1,0:T(8,128)(2,1)}, bf16[2,256,512]{2,1,0:T(8,128)(2,1)S(1)}, u32[]{:S(2)}) copy-start(bf16[2,256,512]{2,1,0:T(8,128)(2,1)S(1)} %constant_dynamic-update-slice_fusion.6.near) | copy-start | bytes 1572868
  37.7 33.8 %collective-permute-start.19 = (bf16[2,256,512]{2,1,0:T(8,128)(2,1)S(1)}, bf16[2,256,512]{2,1,0:T(8,128)(2,1)}, u32[]{:S(2)}, u32[]{:S(2)}) collective-permute-start(bf16[2,256,512]{2,1,0:T(8,128)(2,1)S(1)} %constant_dynamic-update-slice_fusion.6.near), channel_id=1, source_target_pairs={{0,1},{1,0},{2,3},{3,2},{4,5},{5,4},{6,7},{7,6},{8,9},{9,8},{10,11... | collective-permute-start | bytes 1572872 | tf_op jit(solution)/shard_map/ppermute | solution.py:409
  38.2 9.1 %collective-permute-start.1 = (bf16[1,256,512]{2,1,0:T(8,128)(2,1)S(1)}, bf16[1,256,512]{2,1,0:T(8,128)(2,1)S(1)}, u32[]{:S(2)}, u32[]{:S(2)}) collective-permute-start(bf16[1,256,512]{2,1,0:T(8,128)(2,1)S(1)} %collective-permute-done), channel_id=1, source_target_pairs={{0,2},{1,3},{2,0},{3,1},{4,6},{5,7},{6,4},{7,5},{8,10},{9,11},{10,... | collective-permute-start | bytes 786440 | tf_op jit(solution)/shard_map/ppermute | solution.py:409
  39.9 13.0 %collective-permute-start.7 = (bf16[1,256,512]{2,1,0:T(8,128)(2,1)S(1)}, bf16[1,256,512]{2,1,0:T(8,128)(2,1)S(1)}, u32[]{:S(2)}, u32[]{:S(2)}) collective-permute-start(bf16[1,256,512]{2,1,0:T(8,128)(2,1)S(1)} %collective-permute-done.6), channel_id=1, source_target_pairs={{0,2},{1,3},{2,0},{3,1},{4,6},{5,7},{6,4},{7,5},{8,10},{9,11},{10,... | collective-permute-start | bytes 786440 | tf_op jit(solution)/shard_map/ppermute | solution.py:409
  40.4 17.6 %collective-permute-start.13 = (bf16[1,256,512]{2,1,0:T(8,128)(2,1)S(1)}, bf16[1,256,512]{2,1,0:T(8,128)(2,1)S(1)}, u32[]{:S(2)}, u32[]{:S(2)}) collective-permute-start(bf16[1,256,512]{2,1,0:T(8,128)(2,1)S(1)} %collective-permute-done.12), channel_id=1, source_target_pairs={{0,2},{1,3},{2,0},{3,1},{4,6},{5,7},{6,4},{7,5},{8,10},{9,11},{10,... | collective-permute-start | bytes 786440 | tf_op jit(solution)/shard_map/ppermute | solution.py:409
  47.4 24.2 %copy-start.9 = (bf16[2,256,512]{2,1,0:T(8,128)(2,1)}, bf16[2,256,512]{2,1,0:T(8,128)(2,1)S(1)}, u32[]{:S(2)}) copy-start(bf16[2,256,512]{2,1,0:T(8,128)(2,1)S(1)} %constant_dynamic-update-slice_fusion.near) | copy-start | bytes 1572868
  47.4 30.3 %collective-permute-start.2 = (bf16[2,256,512]{2,1,0:T(8,128)(2,1)S(1)}, bf16[2,256,512]{2,1,0:T(8,128)(2,1)}, u32[]{:S(2)}, u32[]{:S(2)}) collective-permute-start(bf16[2,256,512]{2,1,0:T(8,128)(2,1)S(1)} %constant_dynamic-update-slice_fusion.near), channel_id=1, source_target_pairs={{0,1},{1,0},{2,3},{3,2},{4,5},{5,4},{6,7},{7,6},{8,9},{9,8},{10,11... | collective-permute-start | bytes 1572872 | tf_op jit(solution)/shard_map/ppermute | solution.py:409
  53.0 18.6 %copy-start.8 = (bf16[2,256,512]{2,1,0:T(8,128)(2,1)}, bf16[2,256,512]{2,1,0:T(8,128)(2,1)S(1)}, u32[]{:S(2)}) copy-start(bf16[2,256,512]{2,1,0:T(8,128)(2,1)S(1)} %constant_dynamic-update-slice_fusion.2.near) | copy-start | bytes 1572868
  53.0 30.5 %collective-permute-start.8 = (bf16[2,256,512]{2,1,0:T(8,128)(2,1)S(1)}, bf16[2,256,512]{2,1,0:T(8,128)(2,1)}, u32[]{:S(2)}, u32[]{:S(2)}) collective-permute-start(bf16[2,256,512]{2,1,0:T(8,128)(2,1)S(1)} %constant_dynamic-update-slice_fusion.2.near), channel_id=1, source_target_pairs={{0,1},{1,0},{2,3},{3,2},{4,5},{5,4},{6,7},{7,6},{8,9},{9,8},{10,11... | collective-permute-start | bytes 1572872 | tf_op jit(solution)/shard_map/ppermute | solution.py:409
  58.0 13.6 %copy-start.7 = (bf16[2,256,512]{2,1,0:T(8,128)(2,1)}, bf16[2,256,512]{2,1,0:T(8,128)(2,1)S(1)}, u32[]{:S(2)}) copy-start(bf16[2,256,512]{2,1,0:T(8,128)(2,1)S(1)} %constant_dynamic-update-slice_fusion.4.near) | copy-start | bytes 1572868
  58.0 31.6 %collective-permute-start.14 = (bf16[2,256,512]{2,1,0:T(8,128)(2,1)S(1)}, bf16[2,256,512]{2,1,0:T(8,128)(2,1)S(1)}, u32[]{:S(2)}, u32[]{:S(2)}) collective-permute-start(bf16[2,256,512]{2,1,0:T(8,128)(2,1)S(1)} %constant_dynamic-update-slice_fusion.4.near), channel_id=1, source_target_pairs={{0,1},{1,0},{2,3},{3,2},{4,5},{5,4},{6,7},{7,6},{8,9},{9,8},{10,11... | collective-permute-start | bytes 1572872 | tf_op jit(solution)/shard_map/ppermute | solution.py:409
  58.1 0.8 copy-start.5
  77.2 19.1 %collective-permute-start.20 = (bf16[2,256,512]{2,1,0:T(8,128)(2,1)}, bf16[2,256,512]{2,1,0:T(8,128)(2,1)S(1)}, u32[]{:S(2)}, u32[]{:S(2)}) collective-permute-start(bf16[2,256,512]{2,1,0:T(8,128)(2,1)} %get-tuple-element.34), channel_id=1, source_target_pairs={{0,1},{1,0},{2,3},{3,2},{4,5},{5,4},{6,7},{7,6},{8,9},{9,8},{10,11... | collective-permute-start | bytes 1572872 | tf_op jit(solution)/shard_map/ppermute | solution.py:409
  83.4 15.0 %collective-permute-start.3 = (bf16[2,256,512]{2,1,0:T(8,128)(2,1)}, bf16[2,256,512]{2,1,0:T(8,128)(2,1)S(1)}, u32[]{:S(2)}, u32[]{:S(2)}) collective-permute-start(bf16[2,256,512]{2,1,0:T(8,128)(2,1)} %get-tuple-element.26), channel_id=1, source_target_pairs={{0,1},{1,0},{2,3},{3,2},{4,5},{5,4},{6,7},{7,6},{8,9},{9,8},{10,11... | collective-permute-start | bytes 1572872 | tf_op jit(solution)/shard_map/ppermute | solution.py:409
  89.1 7.2 %copy-start.1 = (bf16[2,256,512]{2,1,0:T(8,128)(2,1)S(1)}, bf16[2,256,512]{2,1,0:T(8,128)(2,1)}, u32[]{:S(2)}) copy-start(bf16[2,256,512]{2,1,0:T(8,128)(2,1)} %get-tuple-element.33) | copy-start | bytes 1572868
  89.1 10.1 %collective-permute-start.9 = (bf16[2,256,512]{2,1,0:T(8,128)(2,1)}, bf16[2,256,512]{2,1,0:T(8,128)(2,1)S(1)}, u32[]{:S(2)}, u32[]{:S(2)}) collective-permute-start(bf16[2,256,512]{2,1,0:T(8,128)(2,1)} %get-tuple-element.28), channel_id=1, source_target_pairs={{0,1},{1,0},{2,3},{3,2},{4,5},{5,4},{6,7},{7,6},{8,9},{9,8},{10,11... | collective-permute-start | bytes 1572872 | tf_op jit(solution)/shard_map/ppermute | solution.py:409
  89.5 0.8 copy-start.19
  96.2 2.2 %copy-start.2 = (bf16[2,256,512]{2,1,0:T(8,128)(2,1)S(1)}, bf16[2,256,512]{2,1,0:T(8,128)(2,1)}, u32[]{:S(2)}) copy-start(bf16[2,256,512]{2,1,0:T(8,128)(2,1)} %get-tuple-element.25) | copy-start | bytes 1572868
  96.2 4.7 %collective-permute-start.15 = (bf16[2,256,512]{2,1,0:T(8,128)(2,1)}, bf16[2,256,512]{2,1,0:T(8,128)(2,1)S(1)}, u32[]{:S(2)}, u32[]{:S(2)}) collective-permute-start(bf16[2,256,512]{2,1,0:T(8,128)(2,1)} %get-tuple-element.32), channel_id=1, source_target_pairs={{0,1},{1,0},{2,3},{3,2},{4,5},{5,4},{6,7},{7,6},{8,9},{9,8},{10,11... | collective-permute-start | bytes 1572872 | tf_op jit(solution)/shard_map/ppermute | solution.py:409
  96.5 2.8 %copy-start.3 = (bf16[2,256,512]{2,1,0:T(8,128)(2,1)S(1)}, bf16[2,256,512]{2,1,0:T(8,128)(2,1)}, u32[]{:S(2)}) copy-start(bf16[2,256,512]{2,1,0:T(8,128)(2,1)} %get-tuple-element.27) | copy-start | bytes 1572868
  96.6 29.2 %collective-permute-start.21 = (bf16[256,512]{1,0:T(8,128)(2,1)S(1)}, bf16[256,512]{1,0:T(8,128)(2,1)S(1)}, u32[]{:S(2)}, u32[]{:S(2)}) collective-permute-start(bf16[256,512]{1,0:T(8,128)(2,1)S(1)} %fusion.14), channel_id=1, source_target_pairs={{0,2},{1,3},{2,0},{3,1},{4,6},{5,7},{6,4},{7,5},{8,10},{9,11},{10,... | collective-permute-start | bytes 786440 | tf_op jit(solution)/shard_map/ppermute | solution.py:409
  98.5 2.4 %copy-start.4 = (bf16[2,256,512]{2,1,0:T(8,128)(2,1)S(1)}, bf16[2,256,512]{2,1,0:T(8,128)(2,1)}, u32[]{:S(2)}) copy-start(bf16[2,256,512]{2,1,0:T(8,128)(2,1)} %get-tuple-element.31) | copy-start | bytes 1572868
  98.6 12.8 %collective-permute-start.4 = (bf16[256,512]{1,0:T(8,128)(2,1)S(1)}, bf16[256,512]{1,0:T(8,128)(2,1)S(1)}, u32[]{:S(2)}, u32[]{:S(2)}) collective-permute-start(bf16[256,512]{1,0:T(8,128)(2,1)S(1)} %fusion.11), channel_id=1, source_target_pairs={{0,2},{1,3},{2,0},{3,1},{4,6},{5,7},{6,4},{7,5},{8,10},{9,11},{10,... | collective-permute-start | bytes 786440 | tf_op jit(solution)/shard_map/ppermute | solution.py:409
  99.5 17.6 %collective-permute-start.10 = (bf16[256,512]{1,0:T(8,128)(2,1)S(1)}, bf16[256,512]{1,0:T(8,128)(2,1)S(1)}, u32[]{:S(2)}, u32[]{:S(2)}) collective-permute-start(bf16[256,512]{1,0:T(8,128)(2,1)S(1)} %fusion.12), channel_id=1, source_target_pairs={{0,2},{1,3},{2,0},{3,1},{4,6},{5,7},{6,4},{7,5},{8,10},{9,11},{10,... | collective-permute-start | bytes 786440 | tf_op jit(solution)/shard_map/ppermute | solution.py:409
  101.1 35.5 %copy-start = (f32[1,256,512]{2,1,0:T(8,128)S(1)}, f32[1,256,512]{2,1,0:T(8,128)}, u32[]{:S(2)}) copy-start(f32[1,256,512]{2,1,0:T(8,128)} %estimate.1) | copy-start | bytes 1572868
  101.2 20.9 %collective-permute-start.16 = (bf16[256,512]{1,0:T(8,128)(2,1)S(1)}, bf16[256,512]{1,0:T(8,128)(2,1)S(1)}, u32[]{:S(2)}, u32[]{:S(2)}) collective-permute-start(bf16[256,512]{1,0:T(8,128)(2,1)S(1)} %fusion.13), channel_id=1, source_target_pairs={{0,2},{1,3},{2,0},{3,1},{4,6},{5,7},{6,4},{7,5},{8,10},{9,11},{10,... | collective-permute-start | bytes 786440 | tf_op jit(solution)/shard_map/ppermute | solution.py:409
  111.5 20.9 %collective-permute-start.5 = (bf16[256,512]{1,0:T(8,128)(2,1)S(1)}, bf16[256,512]{1,0:T(8,128)(2,1)S(1)}, u32[]{:S(2)}, u32[]{:S(2)}) collective-permute-start(bf16[256,512]{1,0:T(8,128)(2,1)S(1)} %fusion.10), channel_id=1, source_target_pairs={{0,8},{1,9},{2,10},{3,11},{4,12},{5,13},{6,14},{7,15},{8,0},{9,1},... | collective-permute-start | bytes 786440 | tf_op jit(solution)/shard_map/ppermute | solution.py:409
  117.1 15.3 %collective-permute-start.11 = (bf16[256,512]{1,0:T(8,128)(2,1)S(1)}, bf16[256,512]{1,0:T(8,128)(2,1)S(1)}, u32[]{:S(2)}, u32[]{:S(2)}) collective-permute-start(bf16[256,512]{1,0:T(8,128)(2,1)S(1)} %fusion.8), channel_id=1, source_target_pairs={{0,4},{1,5},{2,6},{3,7},{4,8},{5,9},{6,10},{7,11},{8,12},{9,13},{1... | collective-permute-start | bytes 786440 | tf_op jit(solution)/shard_map/ppermute | solution.py:409
  122.2 14.5 %collective-permute-start.17 = (bf16[256,512]{1,0:T(8,128)(2,1)S(1)}, bf16[256,512]{1,0:T(8,128)(2,1)S(1)}, u32[]{:S(2)}, u32[]{:S(2)}) collective-permute-start(bf16[256,512]{1,0:T(8,128)(2,1)S(1)} %fusion.6), channel_id=1, source_target_pairs={{0,12},{1,13},{2,14},{3,15},{4,0},{5,1},{6,2},{7,3},{8,4},{9,5},{1... | collective-permute-start | bytes 786440 | tf_op jit(solution)/shard_map/ppermute | solution.py:409

commit v2 on v1

--- a/solution.py
+++ b/solution.py
@@ -14,7 +14,8 @@
 BF = jnp.bfloat16
 F32 = jnp.float32
 LANE_BLOCKS = 4
-VMEM_LIMIT = 56 * 1024 * 1024
+TILE = 32
+MIB = 1024 * 1024
 
 
 def trig(rows, cols, length):
@@ -60,8 +61,13 @@
     return jnp.dot(a, b, preferred_element_type=F32)
 
 
+def joined(real, imag):
+    return jnp.concatenate([real.astype(BF), imag.astype(BF)], 1)
+
+
 def data_kernel(group, ids, *refs):
     count = group * LANE_BLOCKS
+    refs = refs[: count + 5 + group] + refs[-2:]
     maps, left, right, first, second = refs[count : count + 5]
     masks = refs[count + 5 : count + 5 + group]
     out, proj = refs[count + 5 + group :]
@@ -79,25 +85,28 @@
                 real, imag = lines[: LANE_BLOCKS // 2], lines[LANE_BLOCKS // 2 :]
                 stacked = jnp.concatenate([jnp.concatenate(real, 1), jnp.concatenate(imag, 1)], 0)
                 parts.append(dot(left[e], stacked))
-            upper, lower = parts[0] + parts[1], parts[0] - parts[1]
-            real = jnp.concatenate([upper[:half], lower[:half]], 0).astype(BF)
-            imag = jnp.concatenate([upper[half:], lower[half:]], 0).astype(BF)
-            masked.append(jnp.concatenate([real, imag], 1) * keep)
+            uppers, lowers = [], []
+            for r in range(0, half, TILE):
+                at, to = slice(r, r + TILE), slice(half + r, half + r + TILE)
+                uppers.append(joined(parts[0][at] + parts[1][at], parts[0][to] + parts[1][to]) * keep)
+                lowers.append(joined(parts[0][at] - parts[1][at], parts[0][to] - parts[1][to]) * keep)
+            masked += uppers + lowers
         back = dot(jnp.concatenate(masked, 0), right[...])
         for e in range(2):
             lhs = first[e] * mask[:, wide + e * width : wide + (e + 1) * width]
             proj[g, e] = dot(lhs, second[e]).astype(BF)
-        real, imag = None, None
-        for c in range(coils):
-            br, bi = back[c * rows : (c + 1) * rows, :width], back[c * rows : (c + 1) * rows, width:]
-            sr, si = maps[c, :, :width], maps[c, :, width:]
-            tr, ti = sr * br + si * bi, sr * bi - si * br
-            real, imag = (tr, ti) if real is None else (real + tr, imag + ti)
-        out[g, :, :width] = real.astype(BF)
-        out[g, :, width:] = imag.astype(BF)
-
-
-def data_term(ids, kdata, maps, masks, tables, group=2):
+        for r in range(0, rows, TILE):
+            real, imag = None, None
+            for c in range(coils):
+                line = back[c * rows + r : c * rows + r + TILE]
+                br, bi = line[:, :width], line[:, width:]
+                sr, si = maps[c, r : r + TILE, :width], maps[c, r : r + TILE, width:]
+                tr, ti = sr * br + si * bi, sr * bi - si * br
+                real, imag = (tr, ti) if real is None else (real + tr, imag + ti)
+            out[g, r : r + TILE] = joined(real, imag)
+
+
+def data_term(ids, kdata, maps, masks, tables, after, group=2):
     phases, coils, rows, wide = kdata.shape
     count = ids.shape[0]
     lanes = wide // LANE_BLOCKS
@@ -115,7 +124,8 @@
             grid=(count // group,),
             in_specs=[lines(g, q) for g in range(group) for q in range(LANE_BLOCKS)]
             + [whole(a) for a in (maps,) + tables]
-            + [row(g) for g in range(group)],
+            + [row(g) for g in range(group)]
+            + [pl.BlockSpec(memory_space=pl.ANY)] * len(after),
             out_specs=[
                 pl.BlockSpec((group, rows, wide), lambda i, ids: (i, 0, 0)),
                 pl.BlockSpec((group, 2, wide // 2, wide // 2), lambda i, ids: (i, 0, 0, 0)),
@@ -125,13 +135,14 @@
             jax.ShapeDtypeStruct((count, rows, wide), BF),
             jax.ShapeDtypeStruct((count, 2, wide // 2, wide // 2), BF),
         ],
-        compiler_params=pltpu.CompilerParams(vmem_limit_bytes=VMEM_LIMIT),
+        compiler_params=pltpu.CompilerParams(vmem_limit_bytes=24 * MIB),
         cost_estimate=cost(1.1 * count),
         name="data_term",
-    )(ids, *[kdata] * (group * LANE_BLOCKS), maps, *tables, *[masks] * group)
-
-
-def image_kernel(ids, place, far, near, maps, data, proj, noise_a, noise_b, away, mine, held):
+    )(ids, *[pltpu.with_memory_space_constraint(kdata, pltpu.HBM)] * (group * LANE_BLOCKS), maps, *tables, *[masks] * group, *after)
+
+
+def image_kernel(ids, place, far_a, far_b, near_a, near_b, maps, data, proj, noise_a, noise_b, *rest):
+    away, mine, held = rest[-3:]
     step = pl.program_id(0)
     coils, rows, wide = maps.shape
     width, quarter = wide // 2, wide // 4
@@ -139,37 +150,41 @@
 
     @pl.when(step == 0)
     def _():
-        held[...] = far[...]
+        held[0] = far_a[0]
+        held[1] = far_b[0]
 
     @pl.when(step == 1)
     def _():
-        held[...] = near[...]
+        held[0] = near_a[0]
+        held[1] = near_b[0]
 
     at = pl.ds(pl.multiple_of(place[0], strip), strip)
     for g, noise in enumerate((noise_a, noise_b)):
-        xr = held[g, :, :width].astype(F32)
-        xi = held[g, :, width:].astype(F32)
         plus, minus = [], []
         for c in range(coils):
-            sr, si = maps[c, :, :width], maps[c, :, width:]
-            cr, ci = sr * xr - si * xi, sr * xi + si * xr
-            cr0, cr1, ci0, ci1 = cr[:, :quarter], cr[:, quarter:], ci[:, :quarter], ci[:, quarter:]
-            plus.append(jnp.concatenate([cr0 + cr1, ci0 + ci1], 1).astype(BF))
-            minus.append(jnp.concatenate([cr0 - cr1, ci0 - ci1], 1).astype(BF))
+            for r in range(0, rows, TILE):
+                to = slice(r, r + TILE)
+                xr, xi = held[g, to, :width].astype(F32), held[g, to, width:].astype(F32)
+                sr, si = maps[c, to, :width], maps[c, to, width:]
+                cr, ci = sr * xr - si * xi, sr * xi + si * xr
+                cr0, cr1, ci0, ci1 = cr[:, :quarter], cr[:, quarter:], ci[:, :quarter], ci[:, quarter:]
+                plus.append(joined(cr0 + cr1, ci0 + ci1))
+                minus.append(joined(cr0 - cr1, ci0 - ci1))
         even = dot(jnp.concatenate(plus, 0), proj[g, 0])
         odd = dot(jnp.concatenate(minus, 0), proj[g, 1])
-        real = -data[g, :, :width].astype(F32)
-        imag = -data[g, :, width:].astype(F32)
-        for c in range(coils):
-            sr, si = maps[c, :, :width], maps[c, :, width:]
-            p, q = even[c * rows : (c + 1) * rows], odd[c * rows : (c + 1) * rows]
-            low, high = p + q, p - q
-            br = jnp.concatenate([low[:, :quarter], high[:, :quarter]], 1)
-            bi = jnp.concatenate([low[:, quarter:], high[:, quarter:]], 1)
-            real = real + sr * br + si * bi
-            imag = imag + sr * bi - si * br
-        held[g, :, :width] = real.astype(BF)
-        held[g, :, width:] = imag.astype(BF)
+        for r in range(0, rows, TILE):
+            to = slice(r, r + TILE)
+            real = -data[g, to, :width].astype(F32)
+            imag = -data[g, to, width:].astype(F32)
+            for c in range(coils):
+                sr, si = maps[c, to, :width], maps[c, to, width:]
+                p, q = even[c * rows + r : c * rows + r + TILE], odd[c * rows + r : c * rows + r + TILE]
+                low, high = p + q, p - q
+                br = jnp.concatenate([low[:, :quarter], high[:, :quarter]], 1)
+                bi = jnp.concatenate([low[:, quarter:], high[:, quarter:]], 1)
+                real = real + sr * br + si * bi
+                imag = imag + sr * bi - si * br
+            held[g, to, :] = joined(real, imag)
         held[g, at, :] = (held[g, at, :].astype(F32) + WEIGHT_RED * noise[0]).astype(BF)
 
     @pl.when(step == 0)
@@ -181,7 +196,7 @@
         mine[...] = held[...]
 
 
-def image_term(ids, place, far, near, maps, data, proj, noise, chunk):
+def image_term(ids, place, images, maps, data, proj, noise, chunk, after):
     coils, rows, wide = maps.shape
     strip, width = noise.shape[1], wide // 2
     whole = lambda a: pl.BlockSpec(a.shape, lambda i, ids, place: (0,) * a.ndim)
@@ -192,22 +207,22 @@
             num_scalar_prefetch=2,
             grid=(2,),
             in_specs=[
-                whole(far),
-                whole(near),
+                *[whole(a) for a in images],
                 whole(maps),
                 pl.BlockSpec((2, rows, wide), lambda i, ids, place: (2 * chunk + i, 0, 0)),
                 pl.BlockSpec((2, 2, width, width), lambda i, ids, place: (2 * chunk + i, 0, 0, 0)),
                 extra(0),
                 extra(1),
-            ],
-            out_specs=[whole(far)] * 2,
+            ]
+            + [pl.BlockSpec(memory_space=pl.ANY)] * len(after),
+            out_specs=[pl.BlockSpec((2, rows, wide), lambda i, ids, place: (0, 0, 0))] * 2,
             scratch_shapes=[pltpu.VMEM((2, rows, wide), BF)],
         ),
         out_shape=[jax.ShapeDtypeStruct((2, rows, wide), BF)] * 2,
-        compiler_params=pltpu.CompilerParams(vmem_limit_bytes=VMEM_LIMIT),
+        compiler_params=pltpu.CompilerParams(vmem_limit_bytes=16 * MIB),
         cost_estimate=cost(5.0),
         name="image_term",
-    )(ids, place, far, near, maps, data, proj, noise, noise)
+    )(ids, place, *images, maps, data, proj, noise, noise, *after)
 
 
 def shifted(value, step):
@@ -220,7 +235,8 @@
     return jnp.where(lane == width - 1, 0.0, pltpu.roll(value, width - 1, 1))
 
 
-def conv_kernel(ch, place, strips, w1, w2, w3, pick1, pick2, spread3, out, x1, h1, noise, a1, a2, a3):
+def conv_kernel(ch, place, strips, w1, w2, w3, pick1, pick2, spread3, *rest):
+    out, x1, h1, noise, a1, a2, a3 = rest[-7:]
     phases, tall, wide = strips.shape
     width = wide // 2
     strip = tall - 8
@@ -229,22 +245,31 @@
     top = jnp.where(place[0] == 0, 0.0, 1.0)
     bottom = jnp.where(place[0] + strip == image_rows, 0.0, 1.0)
 
-    base = dot(w1[...], pick1[...])
+    base = None
+    for tap in range(27):
+        part = lax.dot_general(w1[tap], pick1[tap], (((0,), (0,)), ((), ())), preferred_element_type=F32)
+        base = part if base is None else base + part
     for j in range(n1):
         line = base if j == 0 else pltpu.roll(base, j, 1)
         a1[j * ch : (j + 1) * ch] = line[:, : a1.shape[1]].astype(BF)
-    base = dot(w2[...], pick2[...])
+    tiles = [jnp.zeros((ch, 128), F32)] * (-(-a2.shape[1] // 128))
+    for tap in range(27):
+        d, e, f = tap // 9, tap // 3 % 3, tap % 3
+        at = ((d * 3 + f) * (n2 + 2) + e) * ch
+        tiles[at // 128] = tiles[at // 128] + dot(w2[tap], pick2[at % 128 // ch])
+    base = jnp.concatenate(tiles, 1)
     for j in range(n2):
         line = base if j == 0 else pltpu.roll(base, j * ch, 1)
         a2[j * ch : (j + 1) * ch] = line[:, : a2.shape[1]].astype(BF)
-    base = dot(w3[...], spread3[...])
-    row = lax.broadcasted_iota(jnp.int32, (strip, base.shape[1]), 0)
-    lane = lax.broadcasted_iota(jnp.int32, (strip, base.shape[1]), 1)
+    lines = [dot(w3[tap], spread3[...]) for tap in range(27)]
+    row = lax.broadcasted_iota(jnp.int32, (strip, spread3.shape[1]), 0)
+    lane = lax.broadcasted_iota(jnp.int32, (strip, spread3.shape[1]), 1)
     for k in range(18):
         line = None
         for e in range(3):
             inside = (lane >= (row + e) * ch) & (lane < (row + e + 1) * ch)
-            part = jnp.where(inside, base[3 * k + e : 3 * k + e + 1], 0.0)
+            d, f, o = k // 6, k // 2 % 3, k % 2
+            part = jnp.where(inside, lines[(d * 3 + e) * 3 + f][o : o + 1], 0.0)
             line = part if line is None else line + part
         a3[k * strip : (k + 1) * strip] = line[:, : a3.shape[1]].astype(BF)
 
@@ -307,38 +332,39 @@
     lax.fori_loop(0, phases, store, 0, unroll=4)
 
 
-def pick_tables(cin, tall, n2, ch, n3):
+def pick_tables(cin, tall, ch, n3):
     pad = lambda n: -(-n // 128) * 128
-    pick1 = np.zeros((cin * 27, pad(9 * cin * tall)), np.float32)
-    pick2 = np.zeros((ch * 27, pad(9 * (n2 + 2) * ch)), np.float32)
+    pick1 = np.zeros((27, cin, pad(9 * cin * tall)), np.float32)
     for d in range(3):
         for e in range(3):
             for f in range(3):
-                tap = (d * 3 + e) * 3 + f
                 for c in range(cin):
-                    pick1[c * 27 + tap, ((d * 3 + f) * cin + c) * tall + 1 + e] = 1.0
-                for c in range(ch):
-                    pick2[c * 27 + tap, ((d * 3 + f) * (n2 + 2) + e) * ch + c] = 1.0
+                    pick1[(d * 3 + e) * 3 + f, c, ((d * 3 + f) * cin + c) * tall + 1 + e] = 1.0
+    pick2 = np.zeros((128 // ch, ch, 128), np.float32)
+    for slot in range(128 // ch):
+        pick2[slot, :, slot * ch : (slot + 1) * ch] = np.eye(ch)
     spread3 = np.zeros((ch, pad(n3 * ch)), np.float32)
     for c in range(ch):
         spread3[c, c : n3 * ch : ch] = 1.0
     return as_bf16(pick1), as_bf16(pick2), as_bf16(spread3)
 
 
-def denoise(strips, w_first, w_middle, w_last, place):
+def denoise(strips, w_first, w_middle, w_last, place, after):
     phases, tall, wide = strips.shape
     strip, width, (ch, cin) = tall - 8, wide // 2, w_first.shape[:2]
     n1, n2, n3 = strip + 4, (strip + 2) // 2, strip + 2
-    picks = pick_tables(cin, tall, n2, ch, n3)
+    picks = pick_tables(cin, tall, ch, n3)
     weights = (
-        w_first.reshape(ch, cin * 27),
-        w_middle.reshape(ch, ch * 27),
-        jnp.transpose(w_last, (2, 4, 0, 3, 1)).reshape(54, ch),
+        jnp.transpose(w_first, (2, 3, 4, 1, 0)).reshape(27, cin, ch),
+        jnp.transpose(w_middle, (2, 3, 4, 0, 1)).reshape(27, ch, ch),
+        jnp.transpose(w_last, (2, 3, 4, 0, 1)).reshape(27, 2, ch),
     )
     vmem = pl.BlockSpec(memory_space=pltpu.VMEM)
     return pl.pallas_call(
         functools.partial(conv_kernel, ch),
-        in_specs=[pl.BlockSpec(memory_space=pltpu.SMEM)] + [vmem] * 7,
+        in_specs=[pl.BlockSpec(memory_space=pltpu.SMEM)]
+        + [vmem] * 7
+        + [pl.BlockSpec(memory_space=pl.ANY)] * len(after),
         out_specs=vmem,
         out_shape=jax.ShapeDtypeStruct((phases, strip, wide), F32),
         scratch_shapes=[
@@ -349,10 +375,10 @@
             pltpu.VMEM((n2 * ch, 9 * (n2 + 2) * ch), BF),
             pltpu.VMEM((18 * strip, n3 * ch), BF),
         ],
-        compiler_params=pltpu.CompilerParams(vmem_limit_bytes=VMEM_LIMIT),
+        compiler_params=pltpu.CompilerParams(vmem_limit_bytes=20 * MIB),
         cost_estimate=cost(13.0),
         name="denoise",
-    )(place, strips, *weights, *picks)
+    )(place, strips, *weights, *picks, *after)
 
 
 def prepare_kernel(estimate, mask, pick, image, strips, masks, padded):
@@ -408,39 +434,70 @@
         pairs = [(i, ((i ^ flip) + 4 * shift) % count) for i in range(count)]
         return lax.ppermute(value, "phase", pairs)
 
-    image, strips, masks = prepare(estimate, mask)
-    strips = lax.all_to_all(strips, "phase", 0, 0, tiled=True)
-
-    order = [k for k in (2, 1, planes - 1) if 0 < k < planes]
-    order = list(dict.fromkeys(order + list(range(1, planes)) + [0]))
-    images = {}
-    for k in order:
-        xz = image if k == 0 else send(image, shift=planes - k)
-        near = jnp.concatenate([xz, send(xz, flip=2)])
-        images[k] = (send(near, flip=1), near)
-
+    def behind(value, *earlier):
+        return lax.optimization_barrier((value,) + earlier)[0]
+
+    order = list(dict.fromkeys([planes // 2, 0] + list(range(planes))))
+    lead, rest = order[:2], order[2:]
     flips = jnp.array([1, 3, 0, 2], jnp.int32)
     ids = {k: ((me ^ flips) + 4 * k) % count for k in order}
-    terms = {}
-    for pair in [order[i : i + 2] for i in range(0, planes, 2)]:
-        both = jnp.concatenate([ids[k] for k in pair])
-        data, proj = data_term(both, kdata, maps, masks, tables)
-        for n, k in enumerate(pair):
+
+    image, strips, masks = prepare(estimate, mask)
+    own, across, images, terms = {0: image}, {}, {}, {}
+    far = order[0]
+    if far:
+        own[far] = send(image, shift=planes - far)
+    across[0] = send(image, flip=2)
+    strips = lax.all_to_all(strips, "phase", 0, 0, tiled=True)
+
+    def data_of(chunks, after):
+        both = jnp.concatenate([ids[k] for k in chunks])
+        data, proj = data_term(both, kdata, maps, masks, tables, after)
+        for n, k in enumerate(chunks):
             terms[k] = (data, proj, n)
-
-    noise = denoise(strips, w_first, w_middle, w_last, place)
-
-    total = None
-    for k in order:
+        return data
+
+    def gather(k):
+        images[k] = (send(own[k], flip=1), send(across[k], flip=1), own[k], across[k])
+
+    pairs, planed = {}, {}
+
+    def start(k, after):
         data, proj, n = terms[k]
-        away, mine = image_term(ids[k], place, *images[k], maps, data, proj, noise, n)
-        got = send(away, flip=1)
-        pair = mine.astype(F32) + got.astype(F32)
-        other = send(pair[1].astype(BF), flip=2)
-        plane = pair[0] + other.astype(F32)
-        if k:
-            plane = send(plane.astype(BF), shift=k).astype(F32)
-        total = plane if total is None else total + plane
+        away, mine = image_term(ids[k], place, images[k], maps, data, proj, noise, n, after)
+        pairs[k] = mine.astype(F32) + send(away, flip=1).astype(F32)
+
+    def finish(k):
+        plane = (pairs[k][0] + send(pairs[k][1].astype(BF), flip=2).astype(F32)).astype(BF)
+        planed[k] = (plane, send(plane, shift=k) if k else plane)
+
+    first = data_of(lead, ())
+    gather(0)
+    for k in rest:
+        own[k] = send(behind(image, own[far]), shift=planes - k)
+    if far:
+        across[far] = send(own[far], flip=2)
+    noise = denoise(strips, w_first, w_middle, w_last, place, (first, own[far], across[0]))
+    if far:
+        across[far] = behind(across[far], noise)
+        gather(far)
+    for k in rest:
+        across[k] = send(own[k], flip=2)
+
+    for k in lead:
+        start(k, tuple(own[r] for r in rest))
+        finish(k)
+    after = tuple(pairs[k] for k in lead)
+    if rest:
+        data_of(rest, after + (noise,) + tuple(across[k] for k in rest))
+    after = (planed[lead[0]][0],)
+    for k in rest:
+        gather(k)
+    for k in rest:
+        start(k, after)
+        finish(k)
+        after = (pairs[k],)
+    total = sum(planed[k][1].astype(F32) for k in order)
     return estimate - STEP_SIZE * total[None]
 
 

time: 138 us -> 110 us (0.80)
  Pallas kernels: 57.4 us -> 40 us
  waiting for transfers between devices: 42.2 us -> 27.2 us
  local copies, waits for them, and re-layouts: 4.24 us -> 9.87 us
    ppermute x22 -> x26, waiting for transfers between devices: 42.2 us -> 27.2 us  [send(): return lax.ppermute(value, 'phase', pairs)]
    pallas_call x4, Pallas kernels: 22.9 us -> 12.1 us  [image_term(): pl.pallas_call(image_kernel, grid_spec=pltpu.PrefetchScalarGridSpec(num_s...]
    unnamed x46 -> x40, local copies, waits for them, and re-layouts: 1.94 us -> 9.74 us
    pallas_call x2, Pallas kernels: 19.5 us -> 15.1 us  [data_term(): pl.pallas_call(functools.partial(data_kernel, group), grid_spec=pltpu.Pre...]
    pallas_call x1, Pallas kernels: 12.7 us -> 10.4 us  [denoise(): pl.pallas_call(functools.partial(conv_kernel, ch), in_specs=[pl.BlockSpec...]
    reshape x5 -> x0, local copies, waits for them, and re-layouts: 2.08 us -> none  [the longest x2 0.77 us: denoise(): w_middle.reshape(ch, ch * 27)]
    ppermute x22 -> x26, starting transfers between devices: 25.8 us -> 26.2 us  [send(): return lax.ppermute(value, 'phase', pairs)]
  transfers between devices with their start and end apart: 23 -> 27, of which waited for: 8 -> 11; matrix products, arithmetic and copies ran while one was open for 3% -> 1% of each run, Pallas kernels for 40% -> 30%
where the time goes in v2:
time: 110 us; the launch traced here: 109 us
  Pallas kernels  40 us (36%)
  starting transfers between devices  29.8 us (27%)
  waiting for transfers between devices  27.2 us (25%)
  local copies, waits for them, and re-layouts  9.87 us (9%)
  other arithmetic  2 us (2%)
    ppermute x26, waiting for transfers between devices, send(): return lax.ppermute(value, 'phase', pairs)  27.2 us
    ppermute x26, starting transfers between devices, send(): return lax.ppermute(value, 'phase', pairs)  26.2 us
    pallas_call x2, Pallas kernels, data_term(): pl.pallas_call(functools.partial(data_kernel, group), grid_spec=pltpu.Pre...  15.1 us
    pallas_call x4, Pallas kernels, image_term(): pl.pallas_call(image_kernel, grid_spec=pltpu.PrefetchScalarGridSpec(num_s...  12.1 us
    pallas_call x1, Pallas kernels, denoise(): pl.pallas_call(functools.partial(conv_kernel, ch), in_specs=[pl.BlockSpec...  10.4 us
    unnamed x40, local copies, waits for them, and re-layouts  9.74 us
    all_to_all x1, starting transfers between devices, shards(): strips = lax.all_to_all(strips, 'phase', 0, 0, tiled=True)  3.55 us
    pallas_call x1, Pallas kernels, prepare(): pl.pallas_call(prepare_kernel, out_shape=[jax.ShapeDtypeStruct((1, rows,...  2.38 us
  transfers between devices with their start and end apart: 27, of which 11 were waited for; matrix products, arithmetic and copies ran while one was open for 1% of the time, Pallas kernels for 30%

profile of v2, /device:TPU:0, one launch (start us, length us, event | category | flops | bytes accessed | tf_op | source)
XLA Modules:
  0.0 109.2 jit_solution(13243331283844263614)
XLA Ops:
  0.0 2.4 %prepare.1 = (bf16[1,256,512]{2,1,0:T(8,128)(2,1)}, bf16[16,24,512]{2,1,0:T(8,128)(2,1)}, f32[16,1,1024]{2,1,0:T(1,128)}) custom-call(f32[1,256,512]{2,1,0:T(8,128)} %estimate.1, s32[16,256]{1,0:T(8,128)} %mask.1, bf16[256,1024]{1,0:T(8,128)(2,1)} %constant.69.pick), custom_call_target="tpu_custom_call" | custom-call | flops 2000000000 | tf_op jit(solution)/shard_map/prepare/pallas_call | solution.py:411
  2.4 4.1 %collective-permute-start = (bf16[1,256,512]{2,1,0:T(8,128)(2,1)}, bf16[1,256,512]{2,1,0:T(8,128)(2,1)S(1)}, u32[]{:S(2)}, u32[]{:S(2)}) collective-permute-start(bf16[1,256,512]{2,1,0:T(8,128)(2,1)} %get-tuple-element.28.near_a), channel_id=1, source_target_pairs={{0,8},{1,9},{2,10},{3,11},{4,12},{5,13},{6,14},{7,15},{8,0},{9,1},... | collective-permute-start | bytes 786440 | tf_op jit(solution)/shard_map/ppermute | solution.py:435
  6.4 1.5 %collective-permute-start.3 = (bf16[1,256,512]{2,1,0:T(8,128)(2,1)}, bf16[1,256,512]{2,1,0:T(8,128)(2,1)}, u32[]{:S(2)}, u32[]{:S(2)}) collective-permute-start(bf16[1,256,512]{2,1,0:T(8,128)(2,1)} %get-tuple-element.28.near_a), channel_id=1, source_target_pairs={{0,2},{1,3},{2,0},{3,1},{4,6},{5,7},{6,4},{7,5},{8,10},{9,11},{10,... | collective-permute-start | bytes 786440 | tf_op jit(solution)/shard_map/ppermute | solution.py:435
  8.0 0.0 collective-permute-start.10
  8.0 3.6 %all-to-all-start = ((bf16[16,24,512]{2,1,0:T(8,128)(2,1)}), bf16[16,24,512]{2,1,0:T(8,128)(2,1)S(1)}, u32[]{:S(2)}, u32[]{:S(2)}) async-start(bf16[16,24,512]{2,1,0:T(8,128)(2,1)} %get-tuple-element.23), calls=%async_computation | async-start | bytes 786432 | tf_op jit(solution)/shard_map/all_to_all | solution.py:451
  11.6 0.1 pad_add_fusion.ids
  11.7 0.8 copy-done.4
  12.5 7.5 %data_term.2 = (bf16[8,256,512]{2,1,0:T(8,128)(2,1)S(1)}, bf16[8,2,256,256]{3,2,1,0:T(8,128)(2,1)S(1)}) custom-call(s32[8]{0:T(128)S(1)} %pad_add_fusion.ids, f32[16,2,256,512]{3,2,1,0:T(8,128)} %refs_7_.3, f32[16,2,256,512]{3,2,1,0:T(8,128)} %refs_7_.3, f32[16,2,256,512]{3,2,1,0:T(8,128)} %refs_7_.3, f32[16,2,256,512]{3,2,1,0:T(8,128)} %refs_7_.3, ...), custom_call_target="tpu_custom_call" | custom-call | flops 8800000000 | tf_op jit(solution)/shard_map/data_term/pallas_call | solution.py:120
  20.0 1.3 %copy-done.6 = bf16[8,256,512]{2,1,0:T(8,128)(2,1)} copy-done((bf16[8,256,512]{2,1,0:T(8,128)(2,1)}, bf16[8,256,512]{2,1,0:T(8,128)(2,1)S(1)}, u32[]{:S(2)}) %copy-start.6) | copy-done | bytes 2097176
  21.3 1.4 %copy-done.9 = bf16[8,2,256,256]{3,2,1,0:T(8,128)(2,1)} copy-done((bf16[8,2,256,256]{3,2,1,0:T(8,128)(2,1)}, bf16[8,2,256,256]{3,2,1,0:T(8,128)(2,1)S(1)}, u32[]{:S(2)}) %copy-start.9) | copy-done | bytes 2097176
  22.7 1.0 collective-permute-done.rest_1_.near_a
  23.7 2.8 %collective-permute-start.5 = (bf16[1,256,512]{2,1,0:T(8,128)(2,1)S(1)}, bf16[1,256,512]{2,1,0:T(8,128)(2,1)S(1)}, u32[]{:S(2)}, u32[]{:S(2)}) collective-permute-start(bf16[1,256,512]{2,1,0:T(8,128)(2,1)S(1)} %copy-done.11), channel_id=1, source_target_pairs={{0,12},{1,13},{2,14},{3,15},{4,0},{5,1},{6,2},{7,3},{8,4},{9,5},{1... | collective-permute-start | bytes 786440 | tf_op jit(solution)/shard_map/ppermute | solution.py:435
  26.5 1.5 %collective-permute-start.2 = (bf16[1,256,512]{2,1,0:T(8,128)(2,1)S(1)}, bf16[1,256,512]{2,1,0:T(8,128)(2,1)}, u32[]{:S(2)}, u32[]{:S(2)}) collective-permute-start(bf16[1,256,512]{2,1,0:T(8,128)(2,1)S(1)} %collective-permute-done.rest_1_.near_a), channel_id=1, source_target_pairs={{0,2},{1,3},{2,0},{3,1},{4,6},{5,7},{6,4},{7,5},{8,10},{9,11},{10,... | collective-permute-start | bytes 786440 | tf_op jit(solution)/shard_map/ppermute | solution.py:435
  28.0 1.6 %copy-done.7 = bf16[8,256,512]{2,1,0:T(8,128)(2,1)S(1)} copy-done((bf16[8,256,512]{2,1,0:T(8,128)(2,1)S(1)}, bf16[8,256,512]{2,1,0:T(8,128)(2,1)}, u32[]{:S(2)}) %copy-start.7) | copy-done | bytes 2097176
  29.6 0.9 copy-done.12
  30.5 0.7 copy-done.13
  31.2 0.7 copy-done.14
  31.9 0.8 copy-done.15
  32.7 0.8 copy-done.16
  33.5 0.7 copy-done.17
  34.2 10.4 %denoise.1.noise_a.noise_b.refs_17_ = f32[16,16,512]{2,1,0:T(8,128)S(1)} custom-call(s32[1]{0:T(128)} %bitcast.place, bf16[16,24,512]{2,1,0:T(8,128)(2,1)S(1)} %all-to-all-done.strips, bf16[27,2,16]{2,1,0:T(2,128)(2,1)S(1)} %bitcast.47, bf16[27,16,16]{2,1,0:T(8,128)(2,1)S(1)} %bitcast.46, bf16[27,2,16]{2,1,0:T(2,128)(2,1)S(1)} %bitcast.48, ...), custom_call_target="tpu_custom_call" | custom-call | flops 12999999488 | tf_op jit(solution)/shard_map/denoise/pallas_call | solution.py:363
  44.6 0.6 collective-permute-start.1
  45.2 0.5 collective-permute-start.15
  45.7 3.6 %image_term.5 = (bf16[2,256,512]{2,1,0:T(8,128)(2,1)S(1)}, bf16[2,256,512]{2,1,0:T(8,128)(2,1)S(1)}) custom-call(s32[4]{0:T(128)S(1)} %get-tuple-element.39.ids, s32[1]{0:T(128)} %bitcast.place, bf16[1,256,512]{2,1,0:T(8,128)(2,1)} %collective-permute-done.10.far_a, bf16[1,256,512]{2,1,0:T(8,128)(2,1)} %collective-permute-done.11.far_b, ...), custom_call_target="tpu_custom_call" | custom-call | flops 5000000000 | tf_op jit(solution)/shard_map/image_term/pallas_call | solution.py:204
  49.4 0.6 collective-permute-start.12
  49.9 3.5 %image_term.4 = (bf16[2,256,512]{2,1,0:T(8,128)(2,1)S(1)}, bf16[2,256,512]{2,1,0:T(8,128)(2,1)S(1)}) custom-call(s32[4]{0:T(128)S(1)} %get-tuple-element.42.ids, s32[1]{0:T(128)} %bitcast.place, bf16[1,256,512]{2,1,0:T(8,128)(2,1)S(1)} %collective-permute-done.1.far_a, bf16[1,256,512]{2,1,0:T(8,128)(2,1)S(1)} %collective-permute-done.4.far_b, ...), custom_call_target="tpu_custom_call" | custom-call | flops 5000000000 | tf_op jit(solution)/shard_map/image_term/pallas_call | solution.py:204
  53.4 0.1 collective-permute-start.7
  53.5 0.1 pad_add_fusion.1.ids
  53.6 1.5 %collective-permute-start.17 = (bf16[1,256,512]{2,1,0:T(8,128)(2,1)S(1)}, bf16[1,256,512]{2,1,0:T(8,128)(2,1)S(1)}, u32[]{:S(2)}, u32[]{:S(2)}) collective-permute-start(bf16[1,256,512]{2,1,0:T(8,128)(2,1)S(1)} %collective-permute-done.6.rest_1_.near_a), channel_id=1, source_target_pairs={{0,2},{1,3},{2,0},{3,1},{4,6},{5,7},{6,4},{7,5},{8,10},{9,11},{10,... | collective-permute-start | bytes 786440 | tf_op jit(solution)/shard_map/ppermute | solution.py:435
  55.1 0.2 collective-permute-start.14
  55.3 0.3 collective-permute-start.16
  55.6 0.2 convert_add_fusion.2.refs_16_
  55.8 0.1 convert_add_fusion.3.refs_15_
  56.0 1.2 %collective-permute-start.8 = (bf16[256,512]{1,0:T(8,128)(2,1)S(1)}, bf16[256,512]{1,0:T(8,128)(2,1)S(1)}, u32[]{:S(2)}, u32[]{:S(2)}) collective-permute-start(bf16[256,512]{1,0:T(8,128)(2,1)S(1)} %fusion.8), channel_id=1, source_target_pairs={{0,2},{1,3},{2,0},{3,1},{4,6},{5,7},{6,4},{7,5},{8,10},{9,11},{10,... | collective-permute-start | bytes 786440 | tf_op jit(solution)/shard_map/ppermute | solution.py:435
  57.1 5.5 %collective-permute-done.17.refs_19_.near_b = bf16[1,256,512]{2,1,0:T(8,128)(2,1)S(1)} collective-permute-done((bf16[1,256,512]{2,1,0:T(8,128)(2,1)S(1)}, bf16[1,256,512]{2,1,0:T(8,128)(2,1)S(1)}, u32[]{:S(2)}, u32[]{:S(2)}) %collective-permute-start.17) | collective-permute-done | bytes 262176 | tf_op jit(solution)/shard_map/ppermute | solution.py:435
  62.7 7.6 %data_term.3 = (bf16[8,256,512]{2,1,0:T(8,128)(2,1)S(1)}, bf16[8,2,256,256]{3,2,1,0:T(8,128)(2,1)S(1)}) custom-call(s32[8]{0:T(128)S(1)} %pad_add_fusion.1.ids, f32[16,2,256,512]{3,2,1,0:T(8,128)} %refs_7_.3, f32[16,2,256,512]{3,2,1,0:T(8,128)} %refs_7_.3, f32[16,2,256,512]{3,2,1,0:T(8,128)} %refs_7_.3, f32[16,2,256,512]{3,2,1,0:T(8,128)} %refs_7_.3, ...), custom_call_target="tpu_custom_call" | custom-call | flops 8800000000 | tf_op jit(solution)/shard_map/data_term/pallas_call | solution.py:120
  70.4 0.1 fusion.7.rest_0_
  70.5 2.5 %image_term.6 = (bf16[2,256,512]{2,1,0:T(8,128)(2,1)S(1)}, bf16[2,256,512]{2,1,0:T(8,128)(2,1)S(1)}) custom-call(s32[4]{0:T(128)S(1)} %get-tuple-element.41.ids, s32[1]{0:T(128)} %bitcast.place, bf16[1,256,512]{2,1,0:T(8,128)(2,1)S(1)} %collective-permute-done.14.far_a, bf16[1,256,512]{2,1,0:T(8,128)(2,1)S(1)} %collective-permute-done.16.far_b, ...), custom_call_target="tpu_custom_call" | custom-call | flops 5000000000 | tf_op jit(solution)/shard_map/image_term/pallas_call | solution.py:204
  73.0 0.1 collective-permute-start.18
  73.1 0.5 collective-permute-start.21
  73.6 0.1 collective-permute-start.22
  73.6 1.3 %collective-permute-done.18 = bf16[2,256,512]{2,1,0:T(8,128)(2,1)S(1)} collective-permute-done((bf16[2,256,512]{2,1,0:T(8,128)(2,1)S(1)}, bf16[2,256,512]{2,1,0:T(8,128)(2,1)S(1)}, u32[]{:S(2)}, u32[]{:S(2)}) %collective-permute-start.18) | collective-permute-done | bytes 524320 | tf_op jit(solution)/shard_map/ppermute | solution.py:435
  75.0 0.1 convert_add_fusion.1.rest_0_
  75.1 0.2 collective-permute-done.21.far_a
  75.3 0.4 collective-permute-done.22.far_b
  75.7 2.5 %image_term.7 = (bf16[2,256,512]{2,1,0:T(8,128)(2,1)S(1)}, bf16[2,256,512]{2,1,0:T(8,128)(2,1)S(1)}) custom-call(s32[4]{0:T(128)S(1)} %get-tuple-element.40.ids, s32[1]{0:T(128)} %bitcast.place, bf16[1,256,512]{2,1,0:T(8,128)(2,1)S(1)} %collective-permute-done.21.far_a, bf16[1,256,512]{2,1,0:T(8,128)(2,1)S(1)} %collective-permute-done.22.far_b, ...), custom_call_target="tpu_custom_call" | custom-call | flops 5000000000 | tf_op jit(solution)/shard_map/image_term/pallas_call | solution.py:204
  78.2 0.2 collective-permute-start.23
  78.5 1.6 %collective-permute-start.19 = (bf16[256,512]{1,0:T(8,128)(2,1)S(1)}, bf16[256,512]{1,0:T(8,128)(2,1)S(1)}, u32[]{:S(2)}, u32[]{:S(2)}) collective-permute-start(bf16[256,512]{1,0:T(8,128)(2,1)S(1)} %fusion.10), channel_id=1, source_target_pairs={{0,2},{1,3},{2,0},{3,1},{4,6},{5,7},{6,4},{7,5},{8,10},{9,11},{10,... | collective-permute-start | bytes 786440 | tf_op jit(solution)/shard_map/ppermute | solution.py:435
  80.1 0.1 collective-permute-done.23
  80.2 0.1 convert_add_fusion
  80.4 0.0 copy-start.18
  80.4 1.6 %collective-permute-start.24 = (bf16[256,512]{1,0:T(8,128)(2,1)S(1)}, bf16[256,512]{1,0:T(8,128)(2,1)S(1)}, u32[]{:S(2)}, u32[]{:S(2)}) collective-permute-start(bf16[256,512]{1,0:T(8,128)(2,1)S(1)} %fusion.11), channel_id=1, source_target_pairs={{0,2},{1,3},{2,0},{3,1},{4,6},{5,7},{6,4},{7,5},{8,10},{9,11},{10,... | collective-permute-start | bytes 786440 | tf_op jit(solution)/shard_map/ppermute | solution.py:435
  82.0 0.6 collective-permute-start.13
  82.6 2.3 %collective-permute-start.9 = (bf16[256,512]{1,0:T(8,128)(2,1)S(1)}, bf16[256,512]{1,0:T(8,128)(2,1)S(1)}, u32[]{:S(2)}, u32[]{:S(2)}) collective-permute-start(bf16[256,512]{1,0:T(8,128)(2,1)S(1)} %fusion.7.rest_0_), channel_id=1, source_target_pairs={{0,8},{1,9},{2,10},{3,11},{4,12},{5,13},{6,14},{7,15},{8,0},{9,1},... | collective-permute-start | bytes 786440 | tf_op jit(solution)/shard_map/ppermute | solution.py:435
  84.9 2.8 %collective-permute-done.19 = bf16[256,512]{1,0:T(8,128)(2,1)S(1)} collective-permute-done((bf16[256,512]{1,0:T(8,128)(2,1)S(1)}, bf16[256,512]{1,0:T(8,128)(2,1)S(1)}, u32[]{:S(2)}, u32[]{:S(2)}) %collective-permute-start.19) | collective-permute-done | bytes 262176 | tf_op jit(solution)/shard_map/ppermute | solution.py:435
  87.7 0.1 fusion.3
  87.7 0.6 collective-permute-start.20
  88.3 4.9 %collective-permute-done.24 = bf16[256,512]{1,0:T(8,128)(2,1)S(1)} collective-permute-done((bf16[256,512]{1,0:T(8,128)(2,1)S(1)}, bf16[256,512]{1,0:T(8,128)(2,1)S(1)}, u32[]{:S(2)}, u32[]{:S(2)}) %collective-permute-start.24) | collective-permute-done | bytes 262176 | tf_op jit(solution)/shard_map/ppermute | solution.py:435
  93.3 0.1 fusion.1
  93.4 3.9 %collective-permute-start.25 = (bf16[256,512]{1,0:T(8,128)(2,1)S(1)}, bf16[256,512]{1,0:T(8,128)(2,1)S(1)}, u32[]{:S(2)}, u32[]{:S(2)}) collective-permute-start(bf16[256,512]{1,0:T(8,128)(2,1)S(1)} %fusion.1), channel_id=1, source_target_pairs={{0,12},{1,13},{2,14},{3,15},{4,0},{5,1},{6,2},{7,3},{8,4},{9,5},{1... | collective-permute-start | bytes 786440 | tf_op jit(solution)/shard_map/ppermute | solution.py:435
  97.2 1.1 %collective-permute-done.13 = bf16[256,512]{1,0:T(8,128)(2,1)S(1)} collective-permute-done((bf16[256,512]{1,0:T(8,128)(2,1)S(1)}, bf16[256,512]{1,0:T(8,128)(2,1)S(1)}, u32[]{:S(2)}, u32[]{:S(2)}) %collective-permute-start.13) | collective-permute-done | bytes 262176 | tf_op jit(solution)/shard_map/ppermute | solution.py:435
  98.3 5.6 %collective-permute-done.9 = bf16[256,512]{1,0:T(8,128)(2,1)S(1)} collective-permute-done((bf16[256,512]{1,0:T(8,128)(2,1)S(1)}, bf16[256,512]{1,0:T(8,128)(2,1)S(1)}, u32[]{:S(2)}, u32[]{:S(2)}) %collective-permute-start.9) | collective-permute-done | bytes 262176 | tf_op jit(solution)/shard_map/ppermute | solution.py:435
  103.9 4.2 %collective-permute-done.25 = bf16[256,512]{1,0:T(8,128)(2,1)S(1)} collective-permute-done((bf16[256,512]{1,0:T(8,128)(2,1)S(1)}, bf16[256,512]{1,0:T(8,128)(2,1)S(1)}, u32[]{:S(2)}, u32[]{:S(2)}) %collective-permute-start.25) | collective-permute-done | bytes 262176 | tf_op jit(solution)/shard_map/ppermute | solution.py:435
  108.1 1.0 bitcast_subtract_fusion
  (53 shorter events, 0.2 us)
Async XLA Ops:
  0.0 11.5 %copy-start.19 = (s32[4]{0:T(128)S(1)}, s32[4]{0:T(128)}, u32[]{:S(2)}) copy-start(s32[4]{0:T(128)} %constant.61.clone) | copy-start | bytes 52
  0.0 11.6 %copy-start.1 = (bf16[2,256,256]{2,1,0:T(8,128)(2,1)S(1)}, bf16[2,256,256]{2,1,0:T(8,128)(2,1)}, u32[]{:S(2)}) copy-start(bf16[2,256,256]{2,1,0:T(8,128)(2,1)} %constant.73.refs_9_.refs_11_) | copy-start | bytes 786436
  0.0 11.6 %copy-start.2 = (bf16[512,512]{1,0:T(8,128)(2,1)S(1)}, bf16[512,512]{1,0:T(8,128)(2,1)}, u32[]{:S(2)}) copy-start(bf16[512,512]{1,0:T(8,128)(2,1)} %constant.74.refs_10_) | copy-start | bytes 1572868
  0.0 11.6 %copy-start.3 = (bf16[2,256,256]{2,1,0:T(8,128)(2,1)S(1)}, bf16[2,256,256]{2,1,0:T(8,128)(2,1)}, u32[]{:S(2)}) copy-start(bf16[2,256,256]{2,1,0:T(8,128)(2,1)} %constant.75.refs_12_) | copy-start | bytes 786436
  0.0 11.6 %copy-start = (f32[2,256,512]{2,1,0:T(8,128)S(1)}, f32[2,256,512]{2,1,0:T(8,128)}, u32[]{:S(2)}) copy-start(f32[2,256,512]{2,1,0:T(8,128)} %maps.7) | copy-start | bytes 3145732
  2.4 21.3 %collective-permute-start = (bf16[1,256,512]{2,1,0:T(8,128)(2,1)}, bf16[1,256,512]{2,1,0:T(8,128)(2,1)S(1)}, u32[]{:S(2)}, u32[]{:S(2)}) collective-permute-start(bf16[1,256,512]{2,1,0:T(8,128)(2,1)} %get-tuple-element.28.near_a), channel_id=1, source_target_pairs={{0,8},{1,9},{2,10},{3,11},{4,12},{5,13},{6,14},{7,15},{8,0},{9,1},... | collective-permute-start | bytes 786440 | tf_op jit(solution)/shard_map/ppermute | solution.py:435
  6.4 21.5 %collective-permute-start.3 = (bf16[1,256,512]{2,1,0:T(8,128)(2,1)}, bf16[1,256,512]{2,1,0:T(8,128)(2,1)}, u32[]{:S(2)}, u32[]{:S(2)}) collective-permute-start(bf16[1,256,512]{2,1,0:T(8,128)(2,1)} %get-tuple-element.28.near_a), channel_id=1, source_target_pairs={{0,2},{1,3},{2,0},{3,1},{4,6},{5,7},{6,4},{7,5},{8,10},{9,11},{10,... | collective-permute-start | bytes 786440 | tf_op jit(solution)/shard_map/ppermute | solution.py:435
  8.0 37.7 %collective-permute-start.10 = (bf16[1,256,512]{2,1,0:T(8,128)(2,1)}, bf16[1,256,512]{2,1,0:T(8,128)(2,1)}, u32[]{:S(2)}, u32[]{:S(2)}) collective-permute-start(bf16[1,256,512]{2,1,0:T(8,128)(2,1)} %get-tuple-element.28.near_a), channel_id=1, source_target_pairs={{0,1},{1,0},{2,3},{3,2},{4,5},{5,4},{6,7},{7,6},{8,9},{9,8},{10,11... | collective-permute-start | bytes 786440 | tf_op jit(solution)/shard_map/ppermute | solution.py:435
  8.0 20.0 %all-to-all-start = ((bf16[16,24,512]{2,1,0:T(8,128)(2,1)}), bf16[16,24,512]{2,1,0:T(8,128)(2,1)S(1)}, u32[]{:S(2)}, u32[]{:S(2)}) async-start(bf16[16,24,512]{2,1,0:T(8,128)(2,1)} %get-tuple-element.23), calls=%async_computation | async-start | bytes 786432 | tf_op jit(solution)/shard_map/all_to_all | solution.py:451
  11.7 0.8 copy-start.4
  12.5 11.2 %copy-start.11 = (bf16[1,256,512]{2,1,0:T(8,128)(2,1)S(1)}, bf16[1,256,512]{2,1,0:T(8,128)(2,1)}, u32[]{:S(2)}) copy-start(bf16[1,256,512]{2,1,0:T(8,128)(2,1)} %get-tuple-element.28.near_a) | copy-start | bytes 786436
  20.0 1.3 %copy-start.6 = (bf16[8,256,512]{2,1,0:T(8,128)(2,1)}, bf16[8,256,512]{2,1,0:T(8,128)(2,1)S(1)}, u32[]{:S(2)}) copy-start(bf16[8,256,512]{2,1,0:T(8,128)(2,1)S(1)} %get-tuple-element.25.rest_0_.data) | copy-start | bytes 6291460
  21.3 1.4 %copy-start.9 = (bf16[8,2,256,256]{3,2,1,0:T(8,128)(2,1)}, bf16[8,2,256,256]{3,2,1,0:T(8,128)(2,1)S(1)}, u32[]{:S(2)}) copy-start(bf16[8,2,256,256]{3,2,1,0:T(8,128)(2,1)S(1)} %get-tuple-element.27.proj) | copy-start | bytes 6291460
  23.7 21.5 %collective-permute-start.5 = (bf16[1,256,512]{2,1,0:T(8,128)(2,1)S(1)}, bf16[1,256,512]{2,1,0:T(8,128)(2,1)S(1)}, u32[]{:S(2)}, u32[]{:S(2)}) collective-permute-start(bf16[1,256,512]{2,1,0:T(8,128)(2,1)S(1)} %copy-done.11), channel_id=1, source_target_pairs={{0,12},{1,13},{2,14},{3,15},{4,0},{5,1},{6,2},{7,3},{8,4},{9,5},{1... | collective-permute-start | bytes 786440 | tf_op jit(solution)/shard_map/ppermute | solution.py:435
  26.5 19.2 %collective-permute-start.6 = (bf16[1,256,512]{2,1,0:T(8,128)(2,1)S(1)}, bf16[1,256,512]{2,1,0:T(8,128)(2,1)S(1)}, u32[]{:S(2)}, u32[]{:S(2)}) collective-permute-start(bf16[1,256,512]{2,1,0:T(8,128)(2,1)S(1)} %copy-done.11), channel_id=1, source_target_pairs={{0,4},{1,5},{2,6},{3,7},{4,8},{5,9},{6,10},{7,11},{8,12},{9,13},{1... | collective-permute-start | bytes 786440 | tf_op jit(solution)/shard_map/ppermute | solution.py:435
  26.5 18.1 %collective-permute-start.2 = (bf16[1,256,512]{2,1,0:T(8,128)(2,1)S(1)}, bf16[1,256,512]{2,1,0:T(8,128)(2,1)}, u32[]{:S(2)}, u32[]{:S(2)}) collective-permute-start(bf16[1,256,512]{2,1,0:T(8,128)(2,1)S(1)} %collective-permute-done.rest_1_.near_a), channel_id=1, source_target_pairs={{0,2},{1,3},{2,0},{3,1},{4,6},{5,7},{6,4},{7,5},{8,10},{9,11},{10,... | collective-permute-start | bytes 786440 | tf_op jit(solution)/shard_map/ppermute | solution.py:435
  28.0 17.8 %collective-permute-start.11 = (bf16[1,256,512]{2,1,0:T(8,128)(2,1)}, bf16[1,256,512]{2,1,0:T(8,128)(2,1)}, u32[]{:S(2)}, u32[]{:S(2)}) collective-permute-start(bf16[1,256,512]{2,1,0:T(8,128)(2,1)} %collective-permute-done.3.rest_2_.near_b), channel_id=1, source_target_pairs={{0,1},{1,0},{2,3},{3,2},{4,5},{5,4},{6,7},{7,6},{8,9},{9,8},{10,11... | collective-permute-start | bytes 786440 | tf_op jit(solution)/shard_map/ppermute | solution.py:435
  28.0 1.6 %copy-start.7 = (bf16[8,256,512]{2,1,0:T(8,128)(2,1)S(1)}, bf16[8,256,512]{2,1,0:T(8,128)(2,1)}, u32[]{:S(2)}) copy-start(bf16[8,256,512]{2,1,0:T(8,128)(2,1)} %copy-done.6) | copy-start | bytes 6291460
  29.6 0.9 copy-start.12
  30.5 0.7 copy-start.13
  31.2 0.7 copy-start.14
  31.9 0.8 copy-start.15
  32.7 0.8 copy-start.16
  33.5 0.7 copy-start.17
  34.2 11.6 %copy-start.8 = (bf16[8,256,512]{2,1,0:T(8,128)(2,1)S(1)}, bf16[8,256,512]{2,1,0:T(8,128)(2,1)}, u32[]{:S(2)}) copy-start(bf16[8,256,512]{2,1,0:T(8,128)(2,1)} %copy-done.6) | copy-start | bytes 6291460
  34.2 11.6 %copy-start.10 = (bf16[8,2,256,256]{3,2,1,0:T(8,128)(2,1)S(1)}, bf16[8,2,256,256]{3,2,1,0:T(8,128)(2,1)}, u32[]{:S(2)}) copy-start(bf16[8,2,256,256]{3,2,1,0:T(8,128)(2,1)} %copy-done.9) | copy-start | bytes 6291460
  44.6 5.4 %collective-permute-start.1 = (bf16[1,256,512]{2,1,0:T(8,128)(2,1)S(1)}, bf16[1,256,512]{2,1,0:T(8,128)(2,1)S(1)}, u32[]{:S(2)}, u32[]{:S(2)}) collective-permute-start(bf16[1,256,512]{2,1,0:T(8,128)(2,1)S(1)} %collective-permute-done.rest_1_.near_a), channel_id=1, source_target_pairs={{0,1},{1,0},{2,3},{3,2},{4,5},{5,4},{6,7},{7,6},{8,9},{9,8},{10,11... | collective-permute-start | bytes 786440 | tf_op jit(solution)/shard_map/ppermute | solution.py:435
  45.2 10.1 %collective-permute-start.15 = (bf16[1,256,512]{2,1,0:T(8,128)(2,1)S(1)}, bf16[1,256,512]{2,1,0:T(8,128)(2,1)S(1)}, u32[]{:S(2)}, u32[]{:S(2)}) collective-permute-start(bf16[1,256,512]{2,1,0:T(8,128)(2,1)S(1)} %collective-permute-done.5.rest_0_.near_a), channel_id=1, source_target_pairs={{0,2},{1,3},{2,0},{3,1},{4,6},{5,7},{6,4},{7,5},{8,10},{9,11},{10,... | collective-permute-start | bytes 786440 | tf_op jit(solution)/shard_map/ppermute | solution.py:435
  45.7 4.2 %collective-permute-start.4 = (bf16[1,256,512]{2,1,0:T(8,128)(2,1)}, bf16[1,256,512]{2,1,0:T(8,128)(2,1)S(1)}, u32[]{:S(2)}, u32[]{:S(2)}) collective-permute-start(bf16[1,256,512]{2,1,0:T(8,128)(2,1)} %collective-permute-done.2.near_b), channel_id=1, source_target_pairs={{0,1},{1,0},{2,3},{3,2},{4,5},{5,4},{6,7},{7,6},{8,9},{9,8},{10,11... | collective-permute-start | bytes 786440 | tf_op jit(solution)/shard_map/ppermute | solution.py:435
  49.4 6.2 %collective-permute-start.12 = (bf16[2,256,512]{2,1,0:T(8,128)(2,1)S(1)}, bf16[2,256,512]{2,1,0:T(8,128)(2,1)S(1)}, u32[]{:S(2)}, u32[]{:S(2)}) collective-permute-start(bf16[2,256,512]{2,1,0:T(8,128)(2,1)S(1)} %get-tuple-element.32), channel_id=1, source_target_pairs={{0,1},{1,0},{2,3},{3,2},{4,5},{5,4},{6,7},{7,6},{8,9},{9,8},{10,11... | collective-permute-start | bytes 1572872 | tf_op jit(solution)/shard_map/ppermute | solution.py:435
  53.4 2.4 %collective-permute-start.7 = (bf16[2,256,512]{2,1,0:T(8,128)(2,1)S(1)}, bf16[2,256,512]{2,1,0:T(8,128)(2,1)S(1)}, u32[]{:S(2)}, u32[]{:S(2)}) collective-permute-start(bf16[2,256,512]{2,1,0:T(8,128)(2,1)S(1)} %get-tuple-element.30), channel_id=1, source_target_pairs={{0,1},{1,0},{2,3},{3,2},{4,5},{5,4},{6,7},{7,6},{8,9},{9,8},{10,11... | collective-permute-start | bytes 1572872 | tf_op jit(solution)/shard_map/ppermute | solution.py:435
  53.6 9.1 %collective-permute-start.17 = (bf16[1,256,512]{2,1,0:T(8,128)(2,1)S(1)}, bf16[1,256,512]{2,1,0:T(8,128)(2,1)S(1)}, u32[]{:S(2)}, u32[]{:S(2)}) collective-permute-start(bf16[1,256,512]{2,1,0:T(8,128)(2,1)S(1)} %collective-permute-done.6.rest_1_.near_a), channel_id=1, source_target_pairs={{0,2},{1,3},{2,0},{3,1},{4,6},{5,7},{6,4},{7,5},{8,10},{9,11},{10,... | collective-permute-start | bytes 786440 | tf_op jit(solution)/shard_map/ppermute | solution.py:435
  55.1 15.3 %collective-permute-start.14 = (bf16[1,256,512]{2,1,0:T(8,128)(2,1)S(1)}, bf16[1,256,512]{2,1,0:T(8,128)(2,1)S(1)}, u32[]{:S(2)}, u32[]{:S(2)}) collective-permute-start(bf16[1,256,512]{2,1,0:T(8,128)(2,1)S(1)} %collective-permute-done.5.rest_0_.near_a), channel_id=1, source_target_pairs={{0,1},{1,0},{2,3},{3,2},{4,5},{5,4},{6,7},{7,6},{8,9},{9,8},{10,11... | collective-permute-start | bytes 786440 | tf_op jit(solution)/shard_map/ppermute | solution.py:435
  55.3 15.2 %collective-permute-start.16 = (bf16[1,256,512]{2,1,0:T(8,128)(2,1)S(1)}, bf16[1,256,512]{2,1,0:T(8,128)(2,1)S(1)}, u32[]{:S(2)}, u32[]{:S(2)}) collective-permute-start(bf16[1,256,512]{2,1,0:T(8,128)(2,1)S(1)} %collective-permute-done.15.refs_18_.near_b), channel_id=1, source_target_pairs={{0,1},{1,0},{2,3},{3,2},{4,5},{5,4},{6,7},{7,6},{8,9},{9,8},{10,11... | collective-permute-start | bytes 786440 | tf_op jit(solution)/shard_map/ppermute | solution.py:435
  55.6 7.1 %copy-start.5 = (f32[16,1,1024]{2,1,0:T(1,128)S(1)}, f32[16,1,1024]{2,1,0:T(1,128)}, u32[]{:S(2)}) copy-start(f32[16,1,1024]{2,1,0:T(1,128)} %get-tuple-element.24.refs_13_.refs_14_) | copy-start | bytes 196612
  56.0 14.4 %collective-permute-start.8 = (bf16[256,512]{1,0:T(8,128)(2,1)S(1)}, bf16[256,512]{1,0:T(8,128)(2,1)S(1)}, u32[]{:S(2)}, u32[]{:S(2)}) collective-permute-start(bf16[256,512]{1,0:T(8,128)(2,1)S(1)} %fusion.8), channel_id=1, source_target_pairs={{0,2},{1,3},{2,0},{3,1},{4,6},{5,7},{6,4},{7,5},{8,10},{9,11},{10,... | collective-permute-start | bytes 786440 | tf_op jit(solution)/shard_map/ppermute | solution.py:435
  73.0 2.0 %collective-permute-start.18 = (bf16[2,256,512]{2,1,0:T(8,128)(2,1)S(1)}, bf16[2,256,512]{2,1,0:T(8,128)(2,1)S(1)}, u32[]{:S(2)}, u32[]{:S(2)}) collective-permute-start(bf16[2,256,512]{2,1,0:T(8,128)(2,1)S(1)} %get-tuple-element.36), channel_id=1, source_target_pairs={{0,1},{1,0},{2,3},{3,2},{4,5},{5,4},{6,7},{7,6},{8,9},{9,8},{10,11... | collective-permute-start | bytes 1572872 | tf_op jit(solution)/shard_map/ppermute | solution.py:435
  73.1 2.3 %collective-permute-start.21 = (bf16[1,256,512]{2,1,0:T(8,128)(2,1)S(1)}, bf16[1,256,512]{2,1,0:T(8,128)(2,1)S(1)}, u32[]{:S(2)}, u32[]{:S(2)}) collective-permute-start(bf16[1,256,512]{2,1,0:T(8,128)(2,1)S(1)} %collective-permute-done.6.rest_1_.near_a), channel_id=1, source_target_pairs={{0,1},{1,0},{2,3},{3,2},{4,5},{5,4},{6,7},{7,6},{8,9},{9,8},{10,11... | collective-permute-start | bytes 786440 | tf_op jit(solution)/shard_map/ppermute | solution.py:435
  73.6 2.1 %collective-permute-start.22 = (bf16[1,256,512]{2,1,0:T(8,128)(2,1)S(1)}, bf16[1,256,512]{2,1,0:T(8,128)(2,1)S(1)}, u32[]{:S(2)}, u32[]{:S(2)}) collective-permute-start(bf16[1,256,512]{2,1,0:T(8,128)(2,1)S(1)} %collective-permute-done.17.refs_19_.near_b), channel_id=1, source_target_pairs={{0,1},{1,0},{2,3},{3,2},{4,5},{5,4},{6,7},{7,6},{8,9},{9,8},{10,11... | collective-permute-start | bytes 786440 | tf_op jit(solution)/shard_map/ppermute | solution.py:435
  78.2 2.0 %collective-permute-start.23 = (bf16[2,256,512]{2,1,0:T(8,128)(2,1)S(1)}, bf16[2,256,512]{2,1,0:T(8,128)(2,1)S(1)}, u32[]{:S(2)}, u32[]{:S(2)}) collective-permute-start(bf16[2,256,512]{2,1,0:T(8,128)(2,1)S(1)} %get-tuple-element.38), channel_id=1, source_target_pairs={{0,1},{1,0},{2,3},{3,2},{4,5},{5,4},{6,7},{7,6},{8,9},{9,8},{10,11... | collective-permute-start | bytes 1572872 | tf_op jit(solution)/shard_map/ppermute | solution.py:435
  78.5 9.2 %collective-permute-start.19 = (bf16[256,512]{1,0:T(8,128)(2,1)S(1)}, bf16[256,512]{1,0:T(8,128)(2,1)S(1)}, u32[]{:S(2)}, u32[]{:S(2)}) collective-permute-start(bf16[256,512]{1,0:T(8,128)(2,1)S(1)} %fusion.10), channel_id=1, source_target_pairs={{0,2},{1,3},{2,0},{3,1},{4,6},{5,7},{6,4},{7,5},{8,10},{9,11},{10,... | collective-permute-start | bytes 786440 | tf_op jit(solution)/shard_map/ppermute | solution.py:435
  80.4 27.8 %copy-start.18 = (f32[1,256,512]{2,1,0:T(8,128)S(1)}, f32[1,256,512]{2,1,0:T(8,128)}, u32[]{:S(2)}) copy-start(f32[1,256,512]{2,1,0:T(8,128)} %estimate.1) | copy-start | bytes 1572868
  80.4 12.9 %collective-permute-start.24 = (bf16[256,512]{1,0:T(8,128)(2,1)S(1)}, bf16[256,512]{1,0:T(8,128)(2,1)S(1)}, u32[]{:S(2)}, u32[]{:S(2)}) collective-permute-start(bf16[256,512]{1,0:T(8,128)(2,1)S(1)} %fusion.11), channel_id=1, source_target_pairs={{0,2},{1,3},{2,0},{3,1},{4,6},{5,7},{6,4},{7,5},{8,10},{9,11},{10,... | collective-permute-start | bytes 786440 | tf_op jit(solution)/shard_map/ppermute | solution.py:435
  82.0 16.3 %collective-permute-start.13 = (bf16[256,512]{1,0:T(8,128)(2,1)S(1)}, bf16[256,512]{1,0:T(8,128)(2,1)S(1)}, u32[]{:S(2)}, u32[]{:S(2)}) collective-permute-start(bf16[256,512]{1,0:T(8,128)(2,1)S(1)} %fusion.9), channel_id=1, source_target_pairs={{0,2},{1,3},{2,0},{3,1},{4,6},{5,7},{6,4},{7,5},{8,10},{9,11},{10,... | collective-permute-start | bytes 786440 | tf_op jit(solution)/shard_map/ppermute | solution.py:435
  82.6 21.3 %collective-permute-start.9 = (bf16[256,512]{1,0:T(8,128)(2,1)S(1)}, bf16[256,512]{1,0:T(8,128)(2,1)S(1)}, u32[]{:S(2)}, u32[]{:S(2)}) collective-permute-start(bf16[256,512]{1,0:T(8,128)(2,1)S(1)} %fusion.7.rest_0_), channel_id=1, source_target_pairs={{0,8},{1,9},{2,10},{3,11},{4,12},{5,13},{6,14},{7,15},{8,0},{9,1},... | collective-permute-start | bytes 786440 | tf_op jit(solution)/shard_map/ppermute | solution.py:435
  87.7 16.2 %collective-permute-start.20 = (bf16[256,512]{1,0:T(8,128)(2,1)S(1)}, bf16[256,512]{1,0:T(8,128)(2,1)S(1)}, u32[]{:S(2)}, u32[]{:S(2)}) collective-permute-start(bf16[256,512]{1,0:T(8,128)(2,1)S(1)} %fusion.3), channel_id=1, source_target_pairs={{0,4},{1,5},{2,6},{3,7},{4,8},{5,9},{6,10},{7,11},{8,12},{9,13},{1... | collective-permute-start | bytes 786440 | tf_op jit(solution)/shard_map/ppermute | solution.py:435
  93.4 14.8 %collective-permute-start.25 = (bf16[256,512]{1,0:T(8,128)(2,1)S(1)}, bf16[256,512]{1,0:T(8,128)(2,1)S(1)}, u32[]{:S(2)}, u32[]{:S(2)}) collective-permute-start(bf16[256,512]{1,0:T(8,128)(2,1)S(1)} %fusion.1), channel_id=1, source_target_pairs={{0,12},{1,13},{2,14},{3,15},{4,0},{5,1},{6,2},{7,3},{8,4},{9,5},{1... | collective-permute-start | bytes 786440 | tf_op jit(solution)/shard_map/ppermute | solution.py:435

commit v3 on v2

--- a/solution.py
+++ b/solution.py
@@ -59,6 +59,10 @@
 
 def dot(a, b):
     return jnp.dot(a, b, preferred_element_type=F32)
+
+
+def in_hbm(value):
+    return pltpu.with_memory_space_constraint(value, pltpu.HBM)
 
 
 def joined(real, imag):
@@ -106,7 +110,7 @@
             out[g, r : r + TILE] = joined(real, imag)
 
 
-def data_term(ids, kdata, maps, masks, tables, after, group=2):
+def data_term(ids, kdata, maps, masks, tables, after, spill, group=2):
     phases, coils, rows, wide = kdata.shape
     count = ids.shape[0]
     lanes = wide // LANE_BLOCKS
@@ -132,13 +136,13 @@
             ],
         ),
         out_shape=[
-            jax.ShapeDtypeStruct((count, rows, wide), BF),
-            jax.ShapeDtypeStruct((count, 2, wide // 2, wide // 2), BF),
+            (pltpu.HBM if spill else jax.ShapeDtypeStruct)((count, rows, wide), BF),
+            (pltpu.HBM if spill else jax.ShapeDtypeStruct)((count, 2, wide // 2, wide // 2), BF),
         ],
         compiler_params=pltpu.CompilerParams(vmem_limit_bytes=24 * MIB),
         cost_estimate=cost(1.1 * count),
         name="data_term",
-    )(ids, *[pltpu.with_memory_space_constraint(kdata, pltpu.HBM)] * (group * LANE_BLOCKS), maps, *tables, *[masks] * group, *after)
+    )(ids, *[in_hbm(kdata)] * (group * LANE_BLOCKS), maps, *tables, *[masks] * group, *after)
 
 
 def image_kernel(ids, place, far_a, far_b, near_a, near_b, maps, data, proj, noise_a, noise_b, *rest):
@@ -378,7 +382,7 @@
         compiler_params=pltpu.CompilerParams(vmem_limit_bytes=20 * MIB),
         cost_estimate=cost(13.0),
         name="denoise",
-    )(place, strips, *weights, *picks, *after)
+    )(place, strips, *[in_hbm(a) for a in weights + picks], *after)
 
 
 def prepare_kernel(estimate, mask, pick, image, strips, masks, padded):
@@ -452,7 +456,7 @@
 
     def data_of(chunks, after):
         both = jnp.concatenate([ids[k] for k in chunks])
-        data, proj = data_term(both, kdata, maps, masks, tables, after)
+        data, proj = data_term(both, kdata, maps, masks, tables, after, chunks is lead)
         for n, k in enumerate(chunks):
             terms[k] = (data, proj, n)
         return data
@@ -467,8 +471,9 @@
         away, mine = image_term(ids[k], place, images[k], maps, data, proj, noise, n, after)
         pairs[k] = mine.astype(F32) + send(away, flip=1).astype(F32)
 
-    def finish(k):
-        plane = (pairs[k][0] + send(pairs[k][1].astype(BF), flip=2).astype(F32)).astype(BF)
+    def finish(k, earlier=()):
+        other = behind(pairs[k][1].astype(BF), *earlier)
+        plane = (pairs[k][0] + send(other, flip=2).astype(F32)).astype(BF)
         planed[k] = (plane, send(plane, shift=k) if k else plane)
 
     first = data_of(lead, ())
@@ -487,16 +492,16 @@
     for k in lead:
         start(k, tuple(own[r] for r in rest))
         finish(k)
-    after = tuple(pairs[k] for k in lead)
-    if rest:
-        data_of(rest, after + (noise,) + tuple(across[k] for k in rest))
-    after = (planed[lead[0]][0],)
     for k in rest:
         gather(k)
-    for k in rest:
-        start(k, after)
-        finish(k)
-        after = (pairs[k],)
+    if rest:
+        data_of(rest, tuple(pairs[k] for k in lead) + (noise, across[rest[0]]))
+    for n, k in enumerate(rest):
+        if n == 0:
+            start(k, (planed[order[0]][0],) + tuple(across[r] for r in rest[1:]))
+        else:
+            start(k, (pairs[rest[n - 1]],))
+        finish(k, (planed[order[n - 1]][1],) if n else ())
     total = sum(planed[k][1].astype(F32) for k in order)
     return estimate - STEP_SIZE * total[None]
 

time: 110 us -> 106 us (0.964)
  local copies, waits for them, and re-layouts: 9.87 us -> 2.59 us
  waiting for transfers between devices: 27.2 us -> 29.9 us
  Pallas kernels: 40 us -> 42.3 us
  starting transfers between devices: 29.8 us -> 28.4 us
    unnamed x40 -> x24, local copies, waits for them, and re-layouts: 9.74 us -> 2.46 us
    ppermute x26, waiting for transfers between devices: 27.2 us -> 29.9 us  [send(): return lax.ppermute(value, 'phase', pairs)]
    ppermute x26, starting transfers between devices: 26.2 us -> 24.8 us  [send(): return lax.ppermute(value, 'phase', pairs)]
    pallas_call x2, Pallas kernels: 15.1 us -> 16.3 us  [data_term(): pl.pallas_call(functools.partial(data_kernel, group), grid_spec=pltpu.Pre...]
  transfers between devices with their start and end apart: 27 -> 27, of which waited for: 11 -> 9; matrix products, arithmetic and copies ran while one was open for 1% -> 1% of each run, Pallas kernels for 30% -> 33%
where the time goes in v3:
time: 106 us; the launch traced here: 105 us
  Pallas kernels  42.3 us (40%)
  waiting for transfers between devices  29.9 us (28%)
  starting transfers between devices  28.4 us (27%)
  local copies, waits for them, and re-layouts  2.59 us (2%)
  other arithmetic  2 us (2%)
    ppermute x26, waiting for transfers between devices, send(): return lax.ppermute(value, 'phase', pairs)  29.9 us
    ppermute x26, starting transfers between devices, send(): return lax.ppermute(value, 'phase', pairs)  24.8 us
    pallas_call x2, Pallas kernels, data_term(): pl.pallas_call(functools.partial(data_kernel, group), grid_spec=pltpu.Pre...  16.3 us
    pallas_call x4, Pallas kernels, image_term(): pl.pallas_call(image_kernel, grid_spec=pltpu.PrefetchScalarGridSpec(num_s...  12.1 us
    pallas_call x1, Pallas kernels, denoise(): pl.pallas_call(functools.partial(conv_kernel, ch), in_specs=[pl.BlockSpec...  11.4 us
    all_to_all x1, starting transfers between devices, shards(): strips = lax.all_to_all(strips, 'phase', 0, 0, tiled=True)  3.55 us
    unnamed x24, local copies, waits for them, and re-layouts  2.46 us
    pallas_call x1, Pallas kernels, prepare(): pl.pallas_call(prepare_kernel, out_shape=[jax.ShapeDtypeStruct((1, rows,...  2.4 us
  transfers between devices with their start and end apart: 27, of which 9 were waited for; matrix products, arithmetic and copies ran while one was open for 1% of the time, Pallas kernels for 33%

profile of v3, /device:TPU:0, one launch (start us, length us, event | category | flops | bytes accessed | tf_op | source)
XLA Modules:
  0.0 105.5 jit_solution(4778554952183381420)
XLA Ops:
  0.0 2.4 %prepare.1 = (bf16[1,256,512]{2,1,0:T(8,128)(2,1)}, bf16[16,24,512]{2,1,0:T(8,128)(2,1)}, f32[16,1,1024]{2,1,0:T(1,128)}) custom-call(f32[1,256,512]{2,1,0:T(8,128)} %estimate.1, s32[16,256]{1,0:T(8,128)} %mask.1, bf16[256,1024]{1,0:T(8,128)(2,1)} %constant.69.pick), custom_call_target="tpu_custom_call" | custom-call | flops 2000000000 | tf_op jit(solution)/shard_map/prepare/pallas_call | solution.py:415
  2.4 4.1 %collective-permute-start = (bf16[1,256,512]{2,1,0:T(8,128)(2,1)}, bf16[1,256,512]{2,1,0:T(8,128)(2,1)S(1)}, u32[]{:S(2)}, u32[]{:S(2)}) collective-permute-start(bf16[1,256,512]{2,1,0:T(8,128)(2,1)} %get-tuple-element.29.near_a), channel_id=1, source_target_pairs={{0,8},{1,9},{2,10},{3,11},{4,12},{5,13},{6,14},{7,15},{8,0},{9,1},... | collective-permute-start | bytes 786440 | tf_op jit(solution)/shard_map/ppermute | solution.py:439
  6.5 1.5 %collective-permute-start.3 = (bf16[1,256,512]{2,1,0:T(8,128)(2,1)}, bf16[1,256,512]{2,1,0:T(8,128)(2,1)}, u32[]{:S(2)}, u32[]{:S(2)}) collective-permute-start(bf16[1,256,512]{2,1,0:T(8,128)(2,1)} %get-tuple-element.29.near_a), channel_id=1, source_target_pairs={{0,2},{1,3},{2,0},{3,1},{4,6},{5,7},{6,4},{7,5},{8,10},{9,11},{10,... | collective-permute-start | bytes 786440 | tf_op jit(solution)/shard_map/ppermute | solution.py:439
  8.0 0.0 collective-permute-start.10
  8.0 3.6 %all-to-all-start = ((bf16[16,24,512]{2,1,0:T(8,128)(2,1)}), bf16[16,24,512]{2,1,0:T(8,128)(2,1)S(1)}, u32[]{:S(2)}, u32[]{:S(2)}) async-start(bf16[16,24,512]{2,1,0:T(8,128)(2,1)} %get-tuple-element.24), calls=%async_computation | async-start | bytes 786432 | tf_op jit(solution)/shard_map/all_to_all | solution.py:455
  11.6 0.1 pad_add_fusion.ids
  11.7 0.8 copy-done.4
  12.5 8.7 %data_term.2 = (bf16[8,256,512]{2,1,0:T(8,128)(2,1)}, bf16[8,2,256,256]{3,2,1,0:T(8,128)(2,1)}) custom-call(s32[8]{0:T(128)S(1)} %pad_add_fusion.ids, f32[16,2,256,512]{3,2,1,0:T(8,128)} %refs_7_.3, f32[16,2,256,512]{3,2,1,0:T(8,128)} %refs_7_.3, f32[16,2,256,512]{3,2,1,0:T(8,128)} %refs_7_.3, f32[16,2,256,512]{3,2,1,0:T(8,128)} %refs_7_.3, ...), custom_call_target="tpu_custom_call" | custom-call | flops 8800000000 | tf_op jit(solution)/shard_map/data_term/pallas_call | solution.py:124
  21.2 2.5 %collective-permute-done.rest_1_.near_a = bf16[1,256,512]{2,1,0:T(8,128)(2,1)S(1)} collective-permute-done((bf16[1,256,512]{2,1,0:T(8,128)(2,1)}, bf16[1,256,512]{2,1,0:T(8,128)(2,1)S(1)}, u32[]{:S(2)}, u32[]{:S(2)}) %collective-permute-start) | collective-permute-done | bytes 262176 | tf_op jit(solution)/shard_map/ppermute | solution.py:439
  23.7 2.8 %collective-permute-start.5 = (bf16[1,256,512]{2,1,0:T(8,128)(2,1)S(1)}, bf16[1,256,512]{2,1,0:T(8,128)(2,1)S(1)}, u32[]{:S(2)}, u32[]{:S(2)}) collective-permute-start(bf16[1,256,512]{2,1,0:T(8,128)(2,1)S(1)} %copy-done.9), channel_id=1, source_target_pairs={{0,12},{1,13},{2,14},{3,15},{4,0},{5,1},{6,2},{7,3},{8,4},{9,5},{1... | collective-permute-start | bytes 786440 | tf_op jit(solution)/shard_map/ppermute | solution.py:439
  26.5 0.0 collective-permute-start.6
  26.5 1.5 %collective-permute-start.2 = (bf16[1,256,512]{2,1,0:T(8,128)(2,1)S(1)}, bf16[1,256,512]{2,1,0:T(8,128)(2,1)}, u32[]{:S(2)}, u32[]{:S(2)}) collective-permute-start(bf16[1,256,512]{2,1,0:T(8,128)(2,1)S(1)} %collective-permute-done.rest_1_.near_a), channel_id=1, source_target_pairs={{0,2},{1,3},{2,0},{3,1},{4,6},{5,7},{6,4},{7,5},{8,10},{9,11},{10,... | collective-permute-start | bytes 786440 | tf_op jit(solution)/shard_map/ppermute | solution.py:439
  28.0 0.0 collective-permute-done.3.rest_2_.near_b
  28.0 1.6 %copy-done.6 = bf16[8,256,512]{2,1,0:T(8,128)(2,1)S(1)} copy-done((bf16[8,256,512]{2,1,0:T(8,128)(2,1)S(1)}, bf16[8,256,512]{2,1,0:T(8,128)(2,1)}, u32[]{:S(2)}) %copy-start.6) | copy-done | bytes 2097176
  29.6 11.4 %denoise.1.noise_a.noise_b.refs_17_ = f32[16,16,512]{2,1,0:T(8,128)S(1)} custom-call(s32[1]{0:T(128)} %bitcast.place, bf16[16,24,512]{2,1,0:T(8,128)(2,1)S(1)} %all-to-all-done.strips, bf16[27,2,16]{2,1,0:T(2,128)(2,1)} %bitcast.47, bf16[27,16,16]{2,1,0:T(8,128)(2,1)} %bitcast.46, bf16[27,2,16]{2,1,0:T(2,128)(2,1)} %bitcast.48, ...), custom_call_target="tpu_custom_call" | custom-call | flops 12999999488 | tf_op jit(solution)/shard_map/denoise/pallas_call | solution.py:367
  41.0 0.0 collective-permute-done.2.near_b
  41.0 0.6 collective-permute-start.1
  41.6 0.0 collective-permute-done.5.rest_0_.near_a
  41.6 0.5 collective-permute-start.15
  42.2 0.0 collective-permute-done.11.far_b
  42.2 3.6 %image_term.5 = (bf16[2,256,512]{2,1,0:T(8,128)(2,1)S(1)}, bf16[2,256,512]{2,1,0:T(8,128)(2,1)S(1)}) custom-call(s32[4]{0:T(128)S(1)} %get-tuple-element.41.ids, s32[1]{0:T(128)} %bitcast.place, bf16[1,256,512]{2,1,0:T(8,128)(2,1)} %collective-permute-done.10.far_a, bf16[1,256,512]{2,1,0:T(8,128)(2,1)} %collective-permute-done.11.far_b, ...), custom_call_target="tpu_custom_call" | custom-call | flops 5000000000 | tf_op jit(solution)/shard_map/image_term/pallas_call | solution.py:208
  45.8 0.6 collective-permute-start.12
  46.4 0.0 collective-permute-done.1.far_a
  46.4 3.5 %image_term.4 = (bf16[2,256,512]{2,1,0:T(8,128)(2,1)S(1)}, bf16[2,256,512]{2,1,0:T(8,128)(2,1)S(1)}) custom-call(s32[4]{0:T(128)S(1)} %get-tuple-element.44.ids, s32[1]{0:T(128)} %bitcast.place, bf16[1,256,512]{2,1,0:T(8,128)(2,1)S(1)} %collective-permute-done.1.far_a, bf16[1,256,512]{2,1,0:T(8,128)(2,1)S(1)} %collective-permute-done.4.far_b, ...), custom_call_target="tpu_custom_call" | custom-call | flops 5000000000 | tf_op jit(solution)/shard_map/image_term/pallas_call | solution.py:208
  49.9 0.1 collective-permute-start.7
  50.0 0.1 pad_add_fusion.1.ids
  50.1 1.5 %collective-permute-start.17 = (bf16[1,256,512]{2,1,0:T(8,128)(2,1)S(1)}, bf16[1,256,512]{2,1,0:T(8,128)(2,1)S(1)}, u32[]{:S(2)}, u32[]{:S(2)}) collective-permute-start(bf16[1,256,512]{2,1,0:T(8,128)(2,1)S(1)} %collective-permute-done.6.rest_1_.near_a), channel_id=1, source_target_pairs={{0,2},{1,3},{2,0},{3,1},{4,6},{5,7},{6,4},{7,5},{8,10},{9,11},{10,... | collective-permute-start | bytes 786440 | tf_op jit(solution)/shard_map/ppermute | solution.py:439
  51.6 0.2 collective-permute-start.14
  51.8 0.3 collective-permute-start.16
  52.1 0.0 collective-permute-done.12
  52.1 0.2 convert_add_fusion.2.refs_16_
  52.2 0.1 convert_add_fusion.3.refs_15_
  52.4 1.2 %collective-permute-start.8 = (bf16[256,512]{1,0:T(8,128)(2,1)S(1)}, bf16[256,512]{1,0:T(8,128)(2,1)S(1)}, u32[]{:S(2)}, u32[]{:S(2)}) collective-permute-start(bf16[256,512]{1,0:T(8,128)(2,1)S(1)} %fusion.8), channel_id=1, source_target_pairs={{0,2},{1,3},{2,0},{3,1},{4,6},{5,7},{6,4},{7,5},{8,10},{9,11},{10,... | collective-permute-start | bytes 786440 | tf_op jit(solution)/shard_map/ppermute | solution.py:439
  53.6 7.6 %data_term.3 = (bf16[8,256,512]{2,1,0:T(8,128)(2,1)S(1)}, bf16[8,2,256,256]{3,2,1,0:T(8,128)(2,1)S(1)}) custom-call(s32[8]{0:T(128)S(1)} %pad_add_fusion.1.ids, f32[16,2,256,512]{3,2,1,0:T(8,128)} %refs_7_.3, f32[16,2,256,512]{3,2,1,0:T(8,128)} %refs_7_.3, f32[16,2,256,512]{3,2,1,0:T(8,128)} %refs_7_.3, f32[16,2,256,512]{3,2,1,0:T(8,128)} %refs_7_.3, ...), custom_call_target="tpu_custom_call" | custom-call | flops 8800000000 | tf_op jit(solution)/shard_map/data_term/pallas_call | solution.py:124
  61.3 3.1 %collective-permute-done.8 = bf16[256,512]{1,0:T(8,128)(2,1)S(1)} collective-permute-done((bf16[256,512]{1,0:T(8,128)(2,1)S(1)}, bf16[256,512]{1,0:T(8,128)(2,1)S(1)}, u32[]{:S(2)}, u32[]{:S(2)}) %collective-permute-start.8) | collective-permute-done | bytes 262176 | tf_op jit(solution)/shard_map/ppermute | solution.py:439
  64.4 0.1 fusion.7.rest_0_
  64.4 0.0 collective-permute-done.17.rest_1_.near_b
  64.5 2.5 %image_term.6 = (bf16[2,256,512]{2,1,0:T(8,128)(2,1)S(1)}, bf16[2,256,512]{2,1,0:T(8,128)(2,1)S(1)}) custom-call(s32[4]{0:T(128)S(1)} %get-tuple-element.43.ids, s32[1]{0:T(128)} %bitcast.place, bf16[1,256,512]{2,1,0:T(8,128)(2,1)S(1)} %collective-permute-done.14.far_a, bf16[1,256,512]{2,1,0:T(8,128)(2,1)S(1)} %collective-permute-done.16.far_b, ...), custom_call_target="tpu_custom_call" | custom-call | flops 5000000000 | tf_op jit(solution)/shard_map/image_term/pallas_call | solution.py:208
  67.0 0.1 collective-permute-start.18
  67.1 0.5 collective-permute-start.21
  67.6 0.1 collective-permute-start.22
  67.7 1.3 %collective-permute-done.18 = bf16[2,256,512]{2,1,0:T(8,128)(2,1)S(1)} collective-permute-done((bf16[2,256,512]{2,1,0:T(8,128)(2,1)S(1)}, bf16[2,256,512]{2,1,0:T(8,128)(2,1)S(1)}, u32[]{:S(2)}, u32[]{:S(2)}) %collective-permute-start.18) | collective-permute-done | bytes 524320 | tf_op jit(solution)/shard_map/ppermute | solution.py:439
  69.0 0.1 convert_add_fusion.1.rest_0_
  69.1 0.2 collective-permute-done.21.far_a
  69.3 0.4 collective-permute-done.22.far_b
  69.7 2.5 %image_term.7 = (bf16[2,256,512]{2,1,0:T(8,128)(2,1)S(1)}, bf16[2,256,512]{2,1,0:T(8,128)(2,1)S(1)}) custom-call(s32[4]{0:T(128)S(1)} %get-tuple-element.42.ids, s32[1]{0:T(128)} %bitcast.place, bf16[1,256,512]{2,1,0:T(8,128)(2,1)S(1)} %collective-permute-done.21.far_a, bf16[1,256,512]{2,1,0:T(8,128)(2,1)S(1)} %collective-permute-done.22.far_b, ...), custom_call_target="tpu_custom_call" | custom-call | flops 5000000000 | tf_op jit(solution)/shard_map/image_term/pallas_call | solution.py:208
  72.3 0.2 collective-permute-start.23
  72.4 2.1 %collective-permute-start.9 = (bf16[256,512]{1,0:T(8,128)(2,1)S(1)}, bf16[256,512]{1,0:T(8,128)(2,1)S(1)}, u32[]{:S(2)}, u32[]{:S(2)}) collective-permute-start(bf16[256,512]{1,0:T(8,128)(2,1)S(1)} %fusion.7.rest_0_), channel_id=1, source_target_pairs={{0,8},{1,9},{2,10},{3,11},{4,12},{5,13},{6,14},{7,15},{8,0},{9,1},... | collective-permute-start | bytes 786440 | tf_op jit(solution)/shard_map/ppermute | solution.py:439
  74.6 1.8 %collective-permute-start.19 = (bf16[256,512]{1,0:T(8,128)(2,1)S(1)}, bf16[256,512]{1,0:T(8,128)(2,1)S(1)}, u32[]{:S(2)}, u32[]{:S(2)}) collective-permute-start(bf16[256,512]{1,0:T(8,128)(2,1)S(1)} %fusion.10), channel_id=1, source_target_pairs={{0,2},{1,3},{2,0},{3,1},{4,6},{5,7},{6,4},{7,5},{8,10},{9,11},{10,... | collective-permute-start | bytes 786440 | tf_op jit(solution)/shard_map/ppermute | solution.py:439
  76.4 0.1 convert_add_fusion
  76.5 0.0 copy-start.10
  76.6 11.0 %collective-permute-done.9 = bf16[256,512]{1,0:T(8,128)(2,1)S(1)} collective-permute-done((bf16[256,512]{1,0:T(8,128)(2,1)S(1)}, bf16[256,512]{1,0:T(8,128)(2,1)S(1)}, u32[]{:S(2)}, u32[]{:S(2)}) %collective-permute-start.9) | collective-permute-done | bytes 262176 | tf_op jit(solution)/shard_map/ppermute | solution.py:439
  87.6 1.5 %collective-permute-start.24 = (bf16[256,512]{1,0:T(8,128)(2,1)S(1)}, bf16[256,512]{1,0:T(8,128)(2,1)S(1)}, u32[]{:S(2)}, u32[]{:S(2)}) collective-permute-start(bf16[256,512]{1,0:T(8,128)(2,1)S(1)} %fusion.11), channel_id=1, source_target_pairs={{0,2},{1,3},{2,0},{3,1},{4,6},{5,7},{6,4},{7,5},{8,10},{9,11},{10,... | collective-permute-start | bytes 786440 | tf_op jit(solution)/shard_map/ppermute | solution.py:439
  89.1 0.6 collective-permute-start.13
  89.7 0.0 collective-permute-done.19
  89.7 0.1 fusion.3
  89.8 0.2 collective-permute-start.20
  90.0 6.8 %collective-permute-done.24 = bf16[256,512]{1,0:T(8,128)(2,1)S(1)} collective-permute-done((bf16[256,512]{1,0:T(8,128)(2,1)S(1)}, bf16[256,512]{1,0:T(8,128)(2,1)S(1)}, u32[]{:S(2)}, u32[]{:S(2)}) %collective-permute-start.24) | collective-permute-done | bytes 262176 | tf_op jit(solution)/shard_map/ppermute | solution.py:439
  96.8 0.1 fusion.1
  96.9 2.9 %collective-permute-start.25 = (bf16[256,512]{1,0:T(8,128)(2,1)S(1)}, bf16[256,512]{1,0:T(8,128)(2,1)S(1)}, u32[]{:S(2)}, u32[]{:S(2)}) collective-permute-start(bf16[256,512]{1,0:T(8,128)(2,1)S(1)} %fusion.1), channel_id=1, source_target_pairs={{0,12},{1,13},{2,14},{3,15},{4,0},{5,1},{6,2},{7,3},{8,4},{9,5},{1... | collective-permute-start | bytes 786440 | tf_op jit(solution)/shard_map/ppermute | solution.py:439
  99.8 1.1 %collective-permute-done.13 = bf16[256,512]{1,0:T(8,128)(2,1)S(1)} collective-permute-done((bf16[256,512]{1,0:T(8,128)(2,1)S(1)}, bf16[256,512]{1,0:T(8,128)(2,1)S(1)}, u32[]{:S(2)}, u32[]{:S(2)}) %collective-permute-start.13) | collective-permute-done | bytes 262176 | tf_op jit(solution)/shard_map/ppermute | solution.py:439
  100.9 0.0 collective-permute-done.20
  101.0 3.5 %collective-permute-done.25 = bf16[256,512]{1,0:T(8,128)(2,1)S(1)} collective-permute-done((bf16[256,512]{1,0:T(8,128)(2,1)S(1)}, bf16[256,512]{1,0:T(8,128)(2,1)S(1)}, u32[]{:S(2)}, u32[]{:S(2)}) %collective-permute-start.25) | collective-permute-done | bytes 262176 | tf_op jit(solution)/shard_map/ppermute | solution.py:439
  104.4 1.0 bitcast_subtract_fusion
  (37 shorter events, 0.2 us)
Async XLA Ops:
  0.0 11.6 %copy-start.11 = (s32[4]{0:T(128)S(1)}, s32[4]{0:T(128)}, u32[]{:S(2)}) copy-start(s32[4]{0:T(128)} %constant.61.clone) | copy-start | bytes 52
  0.0 11.7 %copy-start.1 = (bf16[2,256,256]{2,1,0:T(8,128)(2,1)S(1)}, bf16[2,256,256]{2,1,0:T(8,128)(2,1)}, u32[]{:S(2)}) copy-start(bf16[2,256,256]{2,1,0:T(8,128)(2,1)} %constant.73.refs_9_.refs_11_) | copy-start | bytes 786436
  0.0 11.7 %copy-start.2 = (bf16[512,512]{1,0:T(8,128)(2,1)S(1)}, bf16[512,512]{1,0:T(8,128)(2,1)}, u32[]{:S(2)}) copy-start(bf16[512,512]{1,0:T(8,128)(2,1)} %constant.74.refs_10_) | copy-start | bytes 1572868
  0.0 11.7 %copy-start.3 = (bf16[2,256,256]{2,1,0:T(8,128)(2,1)S(1)}, bf16[2,256,256]{2,1,0:T(8,128)(2,1)}, u32[]{:S(2)}) copy-start(bf16[2,256,256]{2,1,0:T(8,128)(2,1)} %constant.75.refs_12_) | copy-start | bytes 786436
  0.0 11.7 %copy-start = (f32[2,256,512]{2,1,0:T(8,128)S(1)}, f32[2,256,512]{2,1,0:T(8,128)}, u32[]{:S(2)}) copy-start(f32[2,256,512]{2,1,0:T(8,128)} %maps.7) | copy-start | bytes 3145732
  2.4 21.3 %collective-permute-start = (bf16[1,256,512]{2,1,0:T(8,128)(2,1)}, bf16[1,256,512]{2,1,0:T(8,128)(2,1)S(1)}, u32[]{:S(2)}, u32[]{:S(2)}) collective-permute-start(bf16[1,256,512]{2,1,0:T(8,128)(2,1)} %get-tuple-element.29.near_a), channel_id=1, source_target_pairs={{0,8},{1,9},{2,10},{3,11},{4,12},{5,13},{6,14},{7,15},{8,0},{9,1},... | collective-permute-start | bytes 786440 | tf_op jit(solution)/shard_map/ppermute | solution.py:439
  6.5 21.5 %collective-permute-start.3 = (bf16[1,256,512]{2,1,0:T(8,128)(2,1)}, bf16[1,256,512]{2,1,0:T(8,128)(2,1)}, u32[]{:S(2)}, u32[]{:S(2)}) collective-permute-start(bf16[1,256,512]{2,1,0:T(8,128)(2,1)} %get-tuple-element.29.near_a), channel_id=1, source_target_pairs={{0,2},{1,3},{2,0},{3,1},{4,6},{5,7},{6,4},{7,5},{8,10},{9,11},{10,... | collective-permute-start | bytes 786440 | tf_op jit(solution)/shard_map/ppermute | solution.py:439
  8.0 34.2 %collective-permute-start.10 = (bf16[1,256,512]{2,1,0:T(8,128)(2,1)}, bf16[1,256,512]{2,1,0:T(8,128)(2,1)}, u32[]{:S(2)}, u32[]{:S(2)}) collective-permute-start(bf16[1,256,512]{2,1,0:T(8,128)(2,1)} %get-tuple-element.29.near_a), channel_id=1, source_target_pairs={{0,1},{1,0},{2,3},{3,2},{4,5},{5,4},{6,7},{7,6},{8,9},{9,8},{10,11... | collective-permute-start | bytes 786440 | tf_op jit(solution)/shard_map/ppermute | solution.py:439
  8.0 20.0 %all-to-all-start = ((bf16[16,24,512]{2,1,0:T(8,128)(2,1)}), bf16[16,24,512]{2,1,0:T(8,128)(2,1)S(1)}, u32[]{:S(2)}, u32[]{:S(2)}) async-start(bf16[16,24,512]{2,1,0:T(8,128)(2,1)} %get-tuple-element.24), calls=%async_computation | async-start | bytes 786432 | tf_op jit(solution)/shard_map/all_to_all | solution.py:455
  11.7 0.8 copy-start.4
  12.5 11.2 %copy-start.9 = (bf16[1,256,512]{2,1,0:T(8,128)(2,1)S(1)}, bf16[1,256,512]{2,1,0:T(8,128)(2,1)}, u32[]{:S(2)}) copy-start(bf16[1,256,512]{2,1,0:T(8,128)(2,1)} %get-tuple-element.29.near_a) | copy-start | bytes 786436
  23.7 17.9 %collective-permute-start.5 = (bf16[1,256,512]{2,1,0:T(8,128)(2,1)S(1)}, bf16[1,256,512]{2,1,0:T(8,128)(2,1)S(1)}, u32[]{:S(2)}, u32[]{:S(2)}) collective-permute-start(bf16[1,256,512]{2,1,0:T(8,128)(2,1)S(1)} %copy-done.9), channel_id=1, source_target_pairs={{0,12},{1,13},{2,14},{3,15},{4,0},{5,1},{6,2},{7,3},{8,4},{9,5},{1... | collective-permute-start | bytes 786440 | tf_op jit(solution)/shard_map/ppermute | solution.py:439
  26.5 15.7 %collective-permute-start.6 = (bf16[1,256,512]{2,1,0:T(8,128)(2,1)S(1)}, bf16[1,256,512]{2,1,0:T(8,128)(2,1)S(1)}, u32[]{:S(2)}, u32[]{:S(2)}) collective-permute-start(bf16[1,256,512]{2,1,0:T(8,128)(2,1)S(1)} %copy-done.9), channel_id=1, source_target_pairs={{0,4},{1,5},{2,6},{3,7},{4,8},{5,9},{6,10},{7,11},{8,12},{9,13},{1... | collective-permute-start | bytes 786440 | tf_op jit(solution)/shard_map/ppermute | solution.py:439
  26.5 14.5 %collective-permute-start.2 = (bf16[1,256,512]{2,1,0:T(8,128)(2,1)S(1)}, bf16[1,256,512]{2,1,0:T(8,128)(2,1)}, u32[]{:S(2)}, u32[]{:S(2)}) collective-permute-start(bf16[1,256,512]{2,1,0:T(8,128)(2,1)S(1)} %collective-permute-done.rest_1_.near_a), channel_id=1, source_target_pairs={{0,2},{1,3},{2,0},{3,1},{4,6},{5,7},{6,4},{7,5},{8,10},{9,11},{10,... | collective-permute-start | bytes 786440 | tf_op jit(solution)/shard_map/ppermute | solution.py:439
  28.0 14.2 %collective-permute-start.11 = (bf16[1,256,512]{2,1,0:T(8,128)(2,1)}, bf16[1,256,512]{2,1,0:T(8,128)(2,1)}, u32[]{:S(2)}, u32[]{:S(2)}) collective-permute-start(bf16[1,256,512]{2,1,0:T(8,128)(2,1)} %collective-permute-done.3.rest_2_.near_b), channel_id=1, source_target_pairs={{0,1},{1,0},{2,3},{3,2},{4,5},{5,4},{6,7},{7,6},{8,9},{9,8},{10,11... | collective-permute-start | bytes 786440 | tf_op jit(solution)/shard_map/ppermute | solution.py:439
  28.0 1.6 %copy-start.6 = (bf16[8,256,512]{2,1,0:T(8,128)(2,1)S(1)}, bf16[8,256,512]{2,1,0:T(8,128)(2,1)}, u32[]{:S(2)}) copy-start(bf16[8,256,512]{2,1,0:T(8,128)(2,1)} %get-tuple-element.26.rest_0_.data) | copy-start | bytes 6291460
  29.6 12.6 %copy-start.7 = (bf16[8,256,512]{2,1,0:T(8,128)(2,1)S(1)}, bf16[8,256,512]{2,1,0:T(8,128)(2,1)}, u32[]{:S(2)}) copy-start(bf16[8,256,512]{2,1,0:T(8,128)(2,1)} %get-tuple-element.26.rest_0_.data) | copy-start | bytes 6291460
  29.6 12.6 %copy-start.8 = (bf16[8,2,256,256]{3,2,1,0:T(8,128)(2,1)S(1)}, bf16[8,2,256,256]{3,2,1,0:T(8,128)(2,1)}, u32[]{:S(2)}) copy-start(bf16[8,2,256,256]{3,2,1,0:T(8,128)(2,1)} %get-tuple-element.28.proj) | copy-start | bytes 6291460
  41.0 5.4 %collective-permute-start.1 = (bf16[1,256,512]{2,1,0:T(8,128)(2,1)S(1)}, bf16[1,256,512]{2,1,0:T(8,128)(2,1)S(1)}, u32[]{:S(2)}, u32[]{:S(2)}) collective-permute-start(bf16[1,256,512]{2,1,0:T(8,128)(2,1)S(1)} %collective-permute-done.rest_1_.near_a), channel_id=1, source_target_pairs={{0,1},{1,0},{2,3},{3,2},{4,5},{5,4},{6,7},{7,6},{8,9},{9,8},{10,11... | collective-permute-start | bytes 786440 | tf_op jit(solution)/shard_map/ppermute | solution.py:439
  41.6 10.1 %collective-permute-start.15 = (bf16[1,256,512]{2,1,0:T(8,128)(2,1)S(1)}, bf16[1,256,512]{2,1,0:T(8,128)(2,1)S(1)}, u32[]{:S(2)}, u32[]{:S(2)}) collective-permute-start(bf16[1,256,512]{2,1,0:T(8,128)(2,1)S(1)} %collective-permute-done.5.rest_0_.near_a), channel_id=1, source_target_pairs={{0,2},{1,3},{2,0},{3,1},{4,6},{5,7},{6,4},{7,5},{8,10},{9,11},{10,... | collective-permute-start | bytes 786440 | tf_op jit(solution)/shard_map/ppermute | solution.py:439
  42.2 4.2 %collective-permute-start.4 = (bf16[1,256,512]{2,1,0:T(8,128)(2,1)}, bf16[1,256,512]{2,1,0:T(8,128)(2,1)S(1)}, u32[]{:S(2)}, u32[]{:S(2)}) collective-permute-start(bf16[1,256,512]{2,1,0:T(8,128)(2,1)} %collective-permute-done.2.near_b), channel_id=1, source_target_pairs={{0,1},{1,0},{2,3},{3,2},{4,5},{5,4},{6,7},{7,6},{8,9},{9,8},{10,11... | collective-permute-start | bytes 786440 | tf_op jit(solution)/shard_map/ppermute | solution.py:439
  45.8 6.2 %collective-permute-start.12 = (bf16[2,256,512]{2,1,0:T(8,128)(2,1)S(1)}, bf16[2,256,512]{2,1,0:T(8,128)(2,1)S(1)}, u32[]{:S(2)}, u32[]{:S(2)}) collective-permute-start(bf16[2,256,512]{2,1,0:T(8,128)(2,1)S(1)} %get-tuple-element.33), channel_id=1, source_target_pairs={{0,1},{1,0},{2,3},{3,2},{4,5},{5,4},{6,7},{7,6},{8,9},{9,8},{10,11... | collective-permute-start | bytes 1572872 | tf_op jit(solution)/shard_map/ppermute | solution.py:439
  49.9 2.4 %collective-permute-start.7 = (bf16[2,256,512]{2,1,0:T(8,128)(2,1)S(1)}, bf16[2,256,512]{2,1,0:T(8,128)(2,1)S(1)}, u32[]{:S(2)}, u32[]{:S(2)}) collective-permute-start(bf16[2,256,512]{2,1,0:T(8,128)(2,1)S(1)} %get-tuple-element.31), channel_id=1, source_target_pairs={{0,1},{1,0},{2,3},{3,2},{4,5},{5,4},{6,7},{7,6},{8,9},{9,8},{10,11... | collective-permute-start | bytes 1572872 | tf_op jit(solution)/shard_map/ppermute | solution.py:439
  50.1 14.4 %collective-permute-start.17 = (bf16[1,256,512]{2,1,0:T(8,128)(2,1)S(1)}, bf16[1,256,512]{2,1,0:T(8,128)(2,1)S(1)}, u32[]{:S(2)}, u32[]{:S(2)}) collective-permute-start(bf16[1,256,512]{2,1,0:T(8,128)(2,1)S(1)} %collective-permute-done.6.rest_1_.near_a), channel_id=1, source_target_pairs={{0,2},{1,3},{2,0},{3,1},{4,6},{5,7},{6,4},{7,5},{8,10},{9,11},{10,... | collective-permute-start | bytes 786440 | tf_op jit(solution)/shard_map/ppermute | solution.py:439
  51.6 12.9 %collective-permute-start.14 = (bf16[1,256,512]{2,1,0:T(8,128)(2,1)S(1)}, bf16[1,256,512]{2,1,0:T(8,128)(2,1)S(1)}, u32[]{:S(2)}, u32[]{:S(2)}) collective-permute-start(bf16[1,256,512]{2,1,0:T(8,128)(2,1)S(1)} %collective-permute-done.5.rest_0_.near_a), channel_id=1, source_target_pairs={{0,1},{1,0},{2,3},{3,2},{4,5},{5,4},{6,7},{7,6},{8,9},{9,8},{10,11... | collective-permute-start | bytes 786440 | tf_op jit(solution)/shard_map/ppermute | solution.py:439
  51.8 12.7 %collective-permute-start.16 = (bf16[1,256,512]{2,1,0:T(8,128)(2,1)S(1)}, bf16[1,256,512]{2,1,0:T(8,128)(2,1)S(1)}, u32[]{:S(2)}, u32[]{:S(2)}) collective-permute-start(bf16[1,256,512]{2,1,0:T(8,128)(2,1)S(1)} %collective-permute-done.15.refs_18_.near_b), channel_id=1, source_target_pairs={{0,1},{1,0},{2,3},{3,2},{4,5},{5,4},{6,7},{7,6},{8,9},{9,8},{10,11... | collective-permute-start | bytes 786440 | tf_op jit(solution)/shard_map/ppermute | solution.py:439
  52.1 1.6 %copy-start.5 = (f32[16,1,1024]{2,1,0:T(1,128)S(1)}, f32[16,1,1024]{2,1,0:T(1,128)}, u32[]{:S(2)}) copy-start(f32[16,1,1024]{2,1,0:T(1,128)} %get-tuple-element.25.refs_13_.refs_14_) | copy-start | bytes 196612
  52.4 11.9 %collective-permute-start.8 = (bf16[256,512]{1,0:T(8,128)(2,1)S(1)}, bf16[256,512]{1,0:T(8,128)(2,1)S(1)}, u32[]{:S(2)}, u32[]{:S(2)}) collective-permute-start(bf16[256,512]{1,0:T(8,128)(2,1)S(1)} %fusion.8), channel_id=1, source_target_pairs={{0,2},{1,3},{2,0},{3,1},{4,6},{5,7},{6,4},{7,5},{8,10},{9,11},{10,... | collective-permute-start | bytes 786440 | tf_op jit(solution)/shard_map/ppermute | solution.py:439
  67.0 2.0 %collective-permute-start.18 = (bf16[2,256,512]{2,1,0:T(8,128)(2,1)S(1)}, bf16[2,256,512]{2,1,0:T(8,128)(2,1)S(1)}, u32[]{:S(2)}, u32[]{:S(2)}) collective-permute-start(bf16[2,256,512]{2,1,0:T(8,128)(2,1)S(1)} %get-tuple-element.37), channel_id=1, source_target_pairs={{0,1},{1,0},{2,3},{3,2},{4,5},{5,4},{6,7},{7,6},{8,9},{9,8},{10,11... | collective-permute-start | bytes 1572872 | tf_op jit(solution)/shard_map/ppermute | solution.py:439
  67.1 2.3 %collective-permute-start.21 = (bf16[1,256,512]{2,1,0:T(8,128)(2,1)S(1)}, bf16[1,256,512]{2,1,0:T(8,128)(2,1)S(1)}, u32[]{:S(2)}, u32[]{:S(2)}) collective-permute-start(bf16[1,256,512]{2,1,0:T(8,128)(2,1)S(1)} %collective-permute-done.6.rest_1_.near_a), channel_id=1, source_target_pairs={{0,1},{1,0},{2,3},{3,2},{4,5},{5,4},{6,7},{7,6},{8,9},{9,8},{10,11... | collective-permute-start | bytes 786440 | tf_op jit(solution)/shard_map/ppermute | solution.py:439
  67.6 2.1 %collective-permute-start.22 = (bf16[1,256,512]{2,1,0:T(8,128)(2,1)S(1)}, bf16[1,256,512]{2,1,0:T(8,128)(2,1)S(1)}, u32[]{:S(2)}, u32[]{:S(2)}) collective-permute-start(bf16[1,256,512]{2,1,0:T(8,128)(2,1)S(1)} %collective-permute-done.17.rest_1_.near_b), channel_id=1, source_target_pairs={{0,1},{1,0},{2,3},{3,2},{4,5},{5,4},{6,7},{7,6},{8,9},{9,8},{10,11... | collective-permute-start | bytes 786440 | tf_op jit(solution)/shard_map/ppermute | solution.py:439
  72.3 4.1 %collective-permute-start.23 = (bf16[2,256,512]{2,1,0:T(8,128)(2,1)S(1)}, bf16[2,256,512]{2,1,0:T(8,128)(2,1)S(1)}, u32[]{:S(2)}, u32[]{:S(2)}) collective-permute-start(bf16[2,256,512]{2,1,0:T(8,128)(2,1)S(1)} %get-tuple-element.39), channel_id=1, source_target_pairs={{0,1},{1,0},{2,3},{3,2},{4,5},{5,4},{6,7},{7,6},{8,9},{9,8},{10,11... | collective-permute-start | bytes 1572872 | tf_op jit(solution)/shard_map/ppermute | solution.py:439
  72.4 15.1 %collective-permute-start.9 = (bf16[256,512]{1,0:T(8,128)(2,1)S(1)}, bf16[256,512]{1,0:T(8,128)(2,1)S(1)}, u32[]{:S(2)}, u32[]{:S(2)}) collective-permute-start(bf16[256,512]{1,0:T(8,128)(2,1)S(1)} %fusion.7.rest_0_), channel_id=1, source_target_pairs={{0,8},{1,9},{2,10},{3,11},{4,12},{5,13},{6,14},{7,15},{8,0},{9,1},... | collective-permute-start | bytes 786440 | tf_op jit(solution)/shard_map/ppermute | solution.py:439
  74.6 15.1 %collective-permute-start.19 = (bf16[256,512]{1,0:T(8,128)(2,1)S(1)}, bf16[256,512]{1,0:T(8,128)(2,1)S(1)}, u32[]{:S(2)}, u32[]{:S(2)}) collective-permute-start(bf16[256,512]{1,0:T(8,128)(2,1)S(1)} %fusion.10), channel_id=1, source_target_pairs={{0,2},{1,3},{2,0},{3,1},{4,6},{5,7},{6,4},{7,5},{8,10},{9,11},{10,... | collective-permute-start | bytes 786440 | tf_op jit(solution)/shard_map/ppermute | solution.py:439
  76.5 27.9 %copy-start.10 = (f32[1,256,512]{2,1,0:T(8,128)S(1)}, f32[1,256,512]{2,1,0:T(8,128)}, u32[]{:S(2)}) copy-start(f32[1,256,512]{2,1,0:T(8,128)} %estimate.1) | copy-start | bytes 1572868
  87.6 9.2 %collective-permute-start.24 = (bf16[256,512]{1,0:T(8,128)(2,1)S(1)}, bf16[256,512]{1,0:T(8,128)(2,1)S(1)}, u32[]{:S(2)}, u32[]{:S(2)}) collective-permute-start(bf16[256,512]{1,0:T(8,128)(2,1)S(1)} %fusion.11), channel_id=1, source_target_pairs={{0,2},{1,3},{2,0},{3,1},{4,6},{5,7},{6,4},{7,5},{8,10},{9,11},{10,... | collective-permute-start | bytes 786440 | tf_op jit(solution)/shard_map/ppermute | solution.py:439
  89.1 11.9 %collective-permute-start.13 = (bf16[256,512]{1,0:T(8,128)(2,1)S(1)}, bf16[256,512]{1,0:T(8,128)(2,1)S(1)}, u32[]{:S(2)}, u32[]{:S(2)}) collective-permute-start(bf16[256,512]{1,0:T(8,128)(2,1)S(1)} %fusion.9), channel_id=1, source_target_pairs={{0,2},{1,3},{2,0},{3,1},{4,6},{5,7},{6,4},{7,5},{8,10},{9,11},{10,... | collective-permute-start | bytes 786440 | tf_op jit(solution)/shard_map/ppermute | solution.py:439
  89.8 11.2 %collective-permute-start.20 = (bf16[256,512]{1,0:T(8,128)(2,1)S(1)}, bf16[256,512]{1,0:T(8,128)(2,1)S(1)}, u32[]{:S(2)}, u32[]{:S(2)}) collective-permute-start(bf16[256,512]{1,0:T(8,128)(2,1)S(1)} %fusion.3), channel_id=1, source_target_pairs={{0,4},{1,5},{2,6},{3,7},{4,8},{5,9},{6,10},{7,11},{8,12},{9,13},{1... | collective-permute-start | bytes 786440 | tf_op jit(solution)/shard_map/ppermute | solution.py:439
  96.9 7.6 %collective-permute-start.25 = (bf16[256,512]{1,0:T(8,128)(2,1)S(1)}, bf16[256,512]{1,0:T(8,128)(2,1)S(1)}, u32[]{:S(2)}, u32[]{:S(2)}) collective-permute-start(bf16[256,512]{1,0:T(8,128)(2,1)S(1)} %fusion.1), channel_id=1, source_target_pairs={{0,12},{1,13},{2,14},{3,15},{4,0},{5,1},{6,2},{7,3},{8,4},{9,5},{1... | collective-permute-start | bytes 786440 | tf_op jit(solution)/shard_map/ppermute | solution.py:439
